TPU v7x, 256 devices: a whole 4x4x8 slice. The times are simulated.
256 devices in a mesh: group: 32 (over x, y, core), tensor: 8 (over z).
Axes of the slice: x: 4, y: 4, z: 8, core: 2. Of those that a mesh axis runs over, the one named last changes fastest.
Arguments:
- tokens: bfloat16 [65536, 8192], P('group', 'tensor'), may hold values from -6 to 6
- kv_weight: bfloat16 [8192, 2048], P('tensor'), may hold values from -0.0625 to 0.0625
- a_pool: bfloat16 [64, 8192, 128], P('group', 'tensor'), may hold values from -0.0625 to 0.0625
- b_pool: bfloat16 [64, 64, 2048], P('group', None, 'tensor'), may hold values from -0.75 to 0.75
- request_entry: int32 [448], P('group'), may hold values from 0 to 14, as said below
- block_request: int32 [32, 16], P('group'), may hold values from 0 to 13, never falling along the last dimension, each value on 1 to 2 neighbouring positions
- fetch_source: int32 [416, 1], P('group'), may hold values from 0 to 31; in each aligned block of 13 rows (0 to 12, 13 to 25, ...) no two rows name the same one
- fetch_slot: int32 [416], P('group'), may hold values from 0 to 1
Outputs:
- keys_values: bfloat16 [2048, 65536], P('tensor', 'group')
Inputs may be any that keep to these rules, and one draw needn't show every extreme that they name: Request r of group g uses entry request_entry[g * 14 + r] of the group's working table: entries below 2 are the group's own pool slots, entry 2 + f is the adapter of the group's f-th fetch; every fetch of a group is used by some request of it. `block_request`: requests cover whole blocks in order, each 1 to 2 blocks, some request exactly that many. The f-th fetch of group g reads slot fetch_slot[g * 13 + f] of the pool of group fetch_source[g * 13 + f, 0], which may be g itself; no group has more than 1 fetches from one source group, and some group has exactly 1.
All inputs are finite; a program needn't handle non-finite values.
Results may differ from a plain program's by a relative error of at most 0.02.
Values may be sent and summed in bfloat16 or wider, within the bound.
No kernel may reach another device: no remote copies, remote signals or barrier semaphores. Data moves between devices by JAX's collectives and lax.ppermute only.
A program may use at most 128 MiB of HBM per device.

v0:
```python
import jax
import jax.numpy as jnp
from jax import lax
from jax.sharding import PartitionSpec as P

HEAD = 128
CAP = 1


def per_device(
    tokens, kv_weight, a_pool, b_pool, request_entry, block_request, fetch_source, fetch_slot
):
    groups = lax.axis_size("group")
    token_rows = tokens.shape[0]
    blocks = block_request.shape[1]
    tile_lines = token_rows // blocks
    rank_width = b_pool.shape[1]
    local_column_span = b_pool.shape[2]
    source = fetch_source[:, 0]
    same_source = source[:, None] == source[None, :]
    position = jnp.sum(jnp.tril(same_source, -1).astype(jnp.int32), axis=1)
    peer_ids = jnp.arange(groups, dtype=jnp.int32)[:, None, None]
    lane_ids = jnp.arange(CAP, dtype=jnp.int32)[None, :, None]
    matches = (source[None, None, :] == peer_ids) & (position[None, None, :] == lane_ids)
    wanted = jnp.sum(jnp.where(matches, fetch_slot[None, None, :], 0), axis=2)
    requested = lax.all_to_all(wanted, "group", split_axis=0, concat_axis=0, tiled=True)
    outgoing_a = a_pool[requested]
    outgoing_b = b_pool[requested]
    arrived_a, arrived_b = (
        lax.all_to_all(outgoing_a, "group", split_axis=0, concat_axis=0, tiled=True),
        lax.all_to_all(outgoing_b, "group", split_axis=0, concat_axis=0, tiled=True),
    )
    fetched_a = arrived_a[source, position]
    fetched_b = arrived_b[source, position]
    working_a = jnp.concatenate([a_pool, fetched_a], axis=0)
    working_b = jnp.concatenate([b_pool, fetched_b], axis=0)
    block_entry = request_entry[block_request[0]]
    a_blocks = working_a[block_entry]
    x_blocks = tokens.reshape(blocks, tile_lines, tokens.shape[1])
    partial_value = jnp.einsum(
        "btd,bdr->btr", x_blocks, a_blocks, preferred_element_type=jnp.float32
    )
    shrink = lax.psum(partial_value.astype(jnp.bfloat16), "tensor")
    pretrained_output_total = lax.psum_scatter(
        lax.dot_general(
            kv_weight, tokens, (((0,), (1,)), ((), ())), preferred_element_type=jnp.float32
        ).astype(jnp.bfloat16),
        "tensor",
        scatter_dimension=0,
        tiled=True,
    ).astype(jnp.float32)
    lifting_factor_tiles = working_b[block_entry].reshape(
        blocks, rank_width, local_column_span // (2 * HEAD), 2, HEAD
    )
    bottleneck_partial_terms = shrink.reshape(blocks, tile_lines, 2, rank_width)
    adapter_correction = jnp.einsum(
        "kdfe,kerft->rftkd",
        bottleneck_partial_terms,
        lifting_factor_tiles,
        preferred_element_type=jnp.float32,
    )
    adapter_correction = adapter_correction.reshape(local_column_span, token_rows)
    return (pretrained_output_total + adapter_correction).astype(jnp.bfloat16)


def solution(mesh):
    placed = (
        P("group", "tensor"),
        P("tensor", None),
        P("group", "tensor", None),
        P("group", None, "tensor"),
        P("group"),
        P("group", None),
        P("group", None),
        P("group"),
    )
    return jax.shard_map(
        per_device, mesh=mesh, in_specs=placed, out_specs=P("tensor", "group"), check_vma=False
    )
```

profile of v0, /device:TPU:24, one launch (start us, length us, event | category | flops | bytes accessed | tf_op | source)
XLA Modules:
  0.0 360.7 jit_solution(12396944543742319591)
XLA Ops:
  6.5 0.9 convert_reduce_fusion
  7.5 0.8 fusion.5
  8.3 12.6 %all_to_all.19 = s32[32,1,1]{2,1,0:T(1,128)S(1)} all-to-all(s32[32,1,1]{2,1,0:T(1,128)S(1)} %copy.27), channel_id=1, replica_groups=mesh['group'=32,'tensor'=8] {'group'}, dimensions={0} | all-to-all | bytes 256 | tf_op jit(solution)/shard_map/all_to_all | solution.py:26
  21.0 0.7 fusion.3
  21.7 5.8 %gather_fusion.4 = bf16[32,1024,128]{2,1,0:T(8,128)(2,1)} fusion(bf16[2,1024,128]{2,1,0:T(8,128)(2,1)} %param.10, s32[1024]{0:T(1024)S(1)} %pad_clamp_fusion.2), kind=kCustom, calls=%fused_computation.4 | custom fusion | bytes 16777344 | tf_op jit(solution)/shard_map/gather | solution.py:27
  27.5 6.8 %all-to-all-start.2 = ((bf16[32,1,1024,128]{3,2,1,0:T(8,128)(2,1)}), bf16[32,1,1024,128]{3,2,1,0:T(8,128)(2,1)}, u32[]{:S(2)}, u32[]{:S(2)}) async-start(bf16[32,1,1024,128]{3,2,1,0:T(8,128)(2,1)} %bitcast.44), calls=%async_computation.3 | async-start | bytes 16777216 | tf_op jit(solution)/shard_map/all_to_all | solution.py:30
  34.4 0.7 gather_fusion.2
  35.1 100.2 %all-to-all-done.2 = bf16[32,1,1024,128]{3,2,1,0:T(8,128)(2,1)} async-done(((bf16[32,1,1024,128]{3,2,1,0:T(8,128)(2,1)}), bf16[32,1,1024,128]{3,2,1,0:T(8,128)(2,1)}, u32[]{:S(2)}, u32[]{:S(2)}) %all-to-all-start.2) | async-done | bytes 8388640 | tf_op jit(solution)/shard_map/all_to_all | solution.py:30
  135.2 6.3 %gather_fusion.5 = bf16[13,1024,128]{2,1,0:T(8,128)(2,1)} fusion(bf16[32,1,1024,128]{3,2,1,0:T(8,128)(2,1)} %all-to-all-done.2, s32[13]{0:T(128)S(1)} %fusion.13), kind=kCustom, calls=%fused_computation.5 | custom fusion | bytes 6815848 | tf_op jit(solution)/shard_map/gather | solution.py:33
  141.5 4.2 %pad_maximum_fusion = bf16[15,1024,128]{2,1,0:T(8,128)(2,1)} fusion(bf16[13,1024,128]{2,1,0:T(8,128)(2,1)} %gather_fusion.5, bf16[2,1024,128]{2,1,0:T(8,128)(2,1)S(1)} %copy-done.1), kind=kLoop, calls=%fused_computation.8 | loop fusion | flops 1966080 | bytes 7864320 | tf_op jit(solution)/shard_map/concatenate | solution.py:35
  145.7 5.1 %gather_fusion.6 = bf16[16,1024,128]{2,1,0:T(8,128)(2,1)} fusion(bf16[15,1024,128]{2,1,0:T(8,128)(2,1)} %pad_maximum_fusion, s32[1024]{0:T(1024)S(1)} %pad_clamp_fusion), kind=kCustom, calls=%fused_computation.6 | custom fusion | bytes 8388672 | tf_op jit(solution)/shard_map/gather | solution.py:38
  150.8 4.9 %convolution_convert_fusion.1 = bf16[16,128,128]{2,1,0:T(8,128)(2,1)S(1)} fusion(bf16[16,1024,128]{2,1,0:T(8,128)(2,1)} %gather_fusion.6, bf16[16,128,1024]{2,1,0:T(8,128)(2,1)} %bitcast.47), kind=kOutput, calls=%fused_computation.12 | convolution fusion | flops 537133056 | bytes 8912896 | tf_op jit(solution)/shard_map/btd,bdr->btr/dot_general | solution.py:40
  155.8 0.8 copy.29
  156.7 14.1 %convolution_convert_fusion = bf16[2048,2048]{1,0:T(8,128)(2,1)} fusion(bf16[1024,2048]{1,0:T(8,128)(2,1)} %param.9, bf16[2048,1024]{1,0:T(8,128)(2,1)} %param.8), kind=kOutput, calls=%fused_computation.7 | convolution fusion | flops 8594128896 | bytes 16777216 | tf_op jit(solution)/shard_map/dot_general | solution.py:45
  170.8 0.8 copy-done.2
  171.6 0.6 gather_fusion
  172.2 44.4 %all_to_all.20 = bf16[32,1,64,256]{3,2,1,0:T(8,128)(2,1)S(1)} all-to-all(bf16[32,1,64,256]{3,2,1,0:T(8,128)(2,1)S(1)} %bitcast.46), channel_id=1, replica_groups=mesh['group'=32,'tensor'=8] {'group'}, dimensions={0} | all-to-all | bytes 2097152 | tf_op jit(solution)/shard_map/all_to_all | solution.py:31
  216.6 0.6 gather_fusion.1
  217.2 0.6 gather_fusion.3
  217.8 36.9 %all-reduce.2.cloned.1.call-done = bf16[16,128,2,64]{1,3,0,2:T(8,128)(2,1)} async-done(((bf16[16,128,2,64]{1,3,0,2:T(8,128)(2,1)}), bf16[16,128,2,64]{1,3,0,2:T(8,128)(2,1)}) %all-reduce.2.cloned.1.call-update) | async-done | bytes 524304 | tf_op jit(solution)/shard_map/psum | solution.py:43
  254.8 1.5 convolution_bitcast_fusion
  256.3 1.2 copy.31
  257.5 93.3 %reduce-scatter.2.cloned.1.call-done = bf16[256,2048]{1,0:T(8,128)(2,1)} async-done(((bf16[2048,2048]{1,0:T(8,128)(2,1)}), bf16[256,2048]{1,0:T(8,128)(2,1)}) %reduce-scatter.2.cloned.1.call-update) | async-done | bytes 1048592 | tf_op jit(solution)/shard_map/reduce_scatter | solution.py:44
  350.8 3.0 fusion
  (23 shorter events, 0.3 us)
Async XLA Ops:
  6.5 27.8 %copy-start = (s32[14]{0:T(128)S(1)}, s32[14]{0:T(128)}, u32[]{:S(2)}) copy-start(s32[14]{0:T(128)} %param.12) | copy-start | bytes 172
  27.5 6.9 %copy-start.4 = (s32[1,16]{1,0:T(1,128)S(1)}, s32[1,16]{1,0:T(1,128)}, u32[]{:S(2)}) copy-start(s32[1,16]{1,0:T(1,128)} %param.13) | copy-start | bytes 196
  27.5 7.6 %copy-start.3 = (s32[13,1]{0,1:T(1,128)S(1)}, s32[13,1]{0,1:T(1,128)}, u32[]{:S(2)}) copy-start(s32[13,1]{0,1:T(1,128)} %param.14) | copy-start | bytes 160
  27.5 107.8 %all-to-all-start.2 = ((bf16[32,1,1024,128]{3,2,1,0:T(8,128)(2,1)}), bf16[32,1,1024,128]{3,2,1,0:T(8,128)(2,1)}, u32[]{:S(2)}, u32[]{:S(2)}) async-start(bf16[32,1,1024,128]{3,2,1,0:T(8,128)(2,1)} %bitcast.44), calls=%async_computation.3 | async-start | bytes 16777216 | tf_op jit(solution)/shard_map/all_to_all | solution.py:30
  34.2 107.3 %copy-start.1 = (bf16[2,1024,128]{2,1,0:T(8,128)(2,1)S(1)}, bf16[2,1024,128]{2,1,0:T(8,128)(2,1)}, u32[]{:S(2)}) copy-start(bf16[2,1024,128]{2,1,0:T(8,128)(2,1)} %param.10) | copy-start | bytes 1572868
  34.3 220.5 %all-reduce.2.cloned.1.call-start = ((), (), s32[]{:S(2)}) async-start(), calls=%async_computation.5 | async-start | bytes 1048576 | tf_op jit(solution)/shard_map/psum | solution.py:43
  156.6 194.2 %reduce-scatter.2.cloned.1.call-start = ((), (), s32[]{:S(2)}) async-start(), calls=%async_computation.4 | async-start | bytes 9437184 | tf_op jit(solution)/shard_map/reduce_scatter | solution.py:44
  170.8 0.8 copy-start.2
Sparse Core Ops, SparseCore 0:
  156.7 97.9 all-reduce.1
  257.5 93.3 reduce-scatter.1
where the time goes:
time: 362 us; the launch traced here: 361 us
  waiting for transfers between devices  230 us (64%)
  blocking collectives  57 us (16%)
  local copies, waits for them, and re-layouts  22.6 us (6%)
  matrix products  20.6 us (6%)
  between operations  13.5 us (4%)
  other arithmetic  9.65 us (3%)
  starting transfers between devices  6.86 us (2%)
    all_to_all x1, waiting for transfers between devices, per_device(): lax.all_to_all(outgoing_a, 'group', split_axis=0, concat_axis=0, tiled=True)  100 us
    reduce_scatter x1, waiting for transfers between devices, per_device(): lax.psum_scatter(lax.dot_general(kv_weight, tokens, (((0,), (1,)), ((), (...  93.3 us
    all_to_all x1, blocking collectives, per_device(): lax.all_to_all(outgoing_b, 'group', split_axis=0, concat_axis=0, tiled=True)  44.4 us
    psum x1, waiting for transfers between devices, per_device(): shrink = lax.psum(partial_value.astype(jnp.bfloat16), 'tensor')  36.9 us
    dot_general x1, matrix products, per_device(): lax.dot_general(kv_weight, tokens, (((0,), (1,)), ((), ())), preferred_el...  14.1 us
    all_to_all x1, blocking collectives, per_device(): lax.all_to_all(wanted, 'group', split_axis=0, concat_axis=0, tiled=True)  12.6 us
  transfers between devices with their start and end apart: 3, of which 3 were waited for; matrix products, arithmetic and copies ran while one was open for 5% of the time, Pallas kernels for 0%

commit v1 on v0

v1 whole, which is shorter than its diff:
```python
import functools

import jax
import jax.numpy as jnp
from jax import lax
from jax.experimental import pallas as pl
from jax.experimental.pallas import tpu as pltpu
from jax.sharding import PartitionSpec as P

HEAD = 128
SIDE = 4
CORES = 2
LANES = 128
NT = (((1,), (1,)), ((), ()))


def base_kernel(tokens_ref, weight_ref, out_ref):
    rows = tokens_ref.shape[0]
    tile = 512

    @pl.loop(0, rows // tile)
    def _(i):
        at = pl.ds(pl.multiple_of(i * tile, tile), tile)
        out_ref[0, at, :] = jnp.dot(
            tokens_ref[at, :], weight_ref[...], preferred_element_type=jnp.float32
        ).astype(out_ref.dtype)


def base_partial(tokens, kv_weight, parts):
    rows, depth = tokens.shape
    columns = kv_weight.shape[1] // parts
    return pl.pallas_call(
        base_kernel,
        grid=(parts,),
        in_specs=[
            pl.BlockSpec((rows, depth), lambda d: (0, 0)),
            pl.BlockSpec((depth, columns), lambda d: (0, d)),
        ],
        out_specs=pl.BlockSpec((1, rows, columns), lambda d: (d, 0, 0)),
        out_shape=jax.ShapeDtypeStruct((parts, rows, columns), jnp.bfloat16),
        cost_estimate=pl.CostEstimate(
            flops=2 * rows * depth * columns * parts,
            bytes_accessed=2 * (rows * depth + depth * columns * parts + rows * columns * parts),
            transcendentals=0,
        ),
        compiler_params=pltpu.CompilerParams(vmem_limit_bytes=40 * 2**20),
        name="base_partial",
    )(tokens, kv_weight)


def shrink_kernel(
    requests, blocks, fetches, pool, table_ref, place_ref, own_tokens, sib_tokens, *refs
):
    first, second = refs[0:5], refs[5:10]
    own_out, sib_out, token_buf, factor_buf, token_sem, factor_sem = refs[10:]
    tile = token_buf.shape[1]
    depth = token_buf.shape[2]
    half = depth // 2
    x, y, core = place_ref[0], place_ref[1], place_ref[2]

    def lookup(who, b):
        request = table_ref[who, requests + b]
        entry = table_ref[who, request]
        fetch = jnp.clip(entry - pool, 0, fetches - 1)
        source = table_ref[who, requests + blocks + fetch]
        slot = table_ref[who, requests + blocks + fetches + fetch]
        mine = entry < pool
        own_group = (x * SIDE + y) * CORES + jnp.where(who == 0, core, 1 - core)
        source = jnp.where(mine, own_group, source)
        slot = jnp.where(mine, entry, slot)
        relative_x = lax.rem(source // (SIDE * CORES) - x + SIDE, SIDE)
        relative_y = lax.rem(lax.rem(source // CORES, SIDE) - y + SIDE, SIDE)
        return lax.rem(source, CORES) == core, relative_x, relative_y, slot

    def offset(relative, slot):
        return jnp.where(
            relative == 0, 0, jnp.where(relative == 3, 2, jnp.where(relative == 1, 4, 6))
        ) + slot

    def start_half(pieces, which, at, relative, index):
        def copy(piece, entry):
            pltpu.make_async_copy(
                pieces[piece].at[entry], factor_buf.at[at, which], factor_sem.at[at, which]
            ).start()

        pl.when(relative == 0)(lambda: copy(0, index))
        pl.when(relative == 3)(lambda: copy(1, index))
        pl.when(relative == 1)(lambda: copy(2, index))
        pl.when((relative == 2) & (index < 4))(lambda: copy(3, index))
        pl.when((relative == 2) & (index >= 4))(lambda: copy(4, index - 4))

    for who, tokens_ref in ((0, own_tokens), (1, sib_tokens)):

        @pl.loop(0, blocks)
        def _(b):
            active, relative_x, relative_y, slot = lookup(who, b)
            at = who * blocks + b

            @pl.when(active)
            def _():
                pltpu.make_async_copy(
                    tokens_ref.at[pl.ds(pl.multiple_of(b * tile, tile), tile)],
                    token_buf.at[at],
                    token_sem.at[at],
                ).start()
                start_half(first, 0, at, relative_x, offset(relative_y, slot))
                start_half(second, 1, at, relative_y, offset(relative_x, slot))

    for who, out_ref in ((0, own_out), (1, sib_out)):

        @pl.loop(0, blocks)
        def _(b):
            active = lookup(who, b)[0]
            at = who * blocks + b

            @pl.when(active)
            def _():
                pltpu.make_async_copy(
                    own_tokens.at[pl.ds(0, tile)], token_buf.at[at], token_sem.at[at]
                ).wait()
                for which in range(2):
                    pltpu.make_async_copy(
                        first[0].at[0], factor_buf.at[at, which], factor_sem.at[at, which]
                    ).wait()
                total = jnp.dot(
                    token_buf[at, :, :half],
                    factor_buf[at, 0, :half],
                    preferred_element_type=jnp.float32,
                ) + jnp.dot(
                    token_buf[at, :, half:],
                    factor_buf[at, 1, :half],
                    preferred_element_type=jnp.float32,
                )
                out_ref[b, :tile] = total.astype(out_ref.dtype)
                out_ref[b, tile : tile + 64] = factor_buf[at, 0, half:]
                out_ref[b, tile + 64 :] = factor_buf[at, 1, half:]

            @pl.when(jnp.logical_not(active))
            def _():
                out_ref[b] = jnp.zeros(out_ref.shape[1:], out_ref.dtype)


def partial_shrink(table, place, own_tokens, sib_tokens, first, second, sizes):
    requests, blocks, fetches, pool = sizes
    rows, depth = own_tokens.shape
    tile = rows // blocks
    height = first[0].shape[1]
    smem = pl.BlockSpec(memory_space=pltpu.SMEM)
    hbm = pl.BlockSpec(memory_space=pl.ANY)
    shape = jax.ShapeDtypeStruct((blocks, tile + 2 * (height - depth // 2), LANES), jnp.bfloat16)
    return pl.pallas_call(
        functools.partial(shrink_kernel, requests, blocks, fetches, pool),
        in_specs=[smem, smem] + [hbm] * 12,
        out_specs=[pl.BlockSpec(memory_space=pltpu.VMEM)] * 2,
        out_shape=[shape, shape],
        scratch_shapes=[
            pltpu.VMEM((2 * blocks, tile, depth), jnp.bfloat16),
            pltpu.VMEM((2 * blocks, 2, height, LANES), jnp.bfloat16),
            pltpu.SemaphoreType.DMA((2 * blocks,)),
            pltpu.SemaphoreType.DMA((2 * blocks, 2)),
        ],
        cost_estimate=pl.CostEstimate(
            flops=2 * rows * depth * LANES, bytes_accessed=12 * 2**20, transcendentals=0
        ),
        compiler_params=pltpu.CompilerParams(vmem_limit_bytes=40 * 2**20),
        name="partial_shrink",
    )(table, place, own_tokens, sib_tokens, *first, *second)


def finish_kernel(base_ref, shrink_ref, lift_ref, out_ref):
    tile = lift_ref.shape[1]
    blocks = lift_ref.shape[0]
    columns = base_ref.shape[1]
    rank = tile // 2
    line = lax.broadcasted_iota(jnp.int32, (columns, columns), 0)
    lane = lax.broadcasted_iota(jnp.int32, (columns, columns), 1)
    eye = jnp.where(line == lane, 1.0, 0.0).astype(jnp.bfloat16)
    for b in range(blocks):
        at = pl.ds(b * tile, tile)
        turned = lax.dot_general(eye, base_ref[at, :], NT, preferred_element_type=jnp.float32)
        for kind in range(2):
            delta = lax.dot_general(
                lift_ref[b, kind * rank : (kind + 1) * rank],
                shrink_ref[at, kind * rank : (kind + 1) * rank],
                (((0,), (1,)), ((), ())),
                preferred_element_type=jnp.float32,
            )
            rows = slice(kind * HEAD, (kind + 1) * HEAD)
            out_ref[rows, at] = (turned[rows] + delta).astype(out_ref.dtype)


def finish(base, shrink, lift):
    rows, columns = base.shape
    parts = 2
    step, lifts = rows // parts, lift.shape[0] // parts
    return pl.pallas_call(
        finish_kernel,
        grid=(parts,),
        in_specs=[
            pl.BlockSpec((step, columns), lambda i: (i, 0)),
            pl.BlockSpec((step, shrink.shape[1]), lambda i: (i, 0)),
            pl.BlockSpec((lifts,) + lift.shape[1:], lambda i: (i, 0, 0)),
        ],
        out_specs=pl.BlockSpec((columns, step), lambda i: (0, i)),
        out_shape=jax.ShapeDtypeStruct((columns, rows), jnp.bfloat16),
        cost_estimate=pl.CostEstimate(
            flops=2 * rows * columns * (columns + LANES),
            bytes_accessed=6 * rows * columns,
            transcendentals=0,
        ),
        compiler_params=pltpu.CompilerParams(vmem_limit_bytes=40 * 2**20),
        name="finish",
    )(base, shrink, lift)


def moves():
    def index(x, y, core):
        return ((x % SIDE) * SIDE + y % SIDE) * CORES + core

    places = [
        (x, y, core) for x in range(SIDE) for y in range(SIDE) for core in range(CORES)
    ]

    def shift(dx, dy):
        return [(index(x, y, c), index(x + dx, y + dy, c)) for x, y, c in places]

    swap = [(index(x, y, c), index(x, y, 1 - c)) for x, y, c in places]
    return (shift(1, 0), shift(-1, 0)), (shift(0, 1), shift(0, -1)), swap


def per_device(
    tokens, kv_weight, a_pool, b_pool, request_entry, block_request, fetch_source, fetch_slot
):
    tensor = lax.axis_size("tensor")
    rows, depth = tokens.shape
    blocks = block_request.shape[1]
    pool = a_pool.shape[0]
    half = depth // 2
    along_x, along_y, swap = moves()

    partial = base_partial(tokens, kv_weight, tensor)
    base = lax.psum_scatter(
        partial.reshape(tensor * rows, -1), "tensor", scatter_dimension=0, tiled=True
    )

    position = lax.axis_index("group")
    place = jnp.stack(
        [position // (SIDE * CORES), position // CORES % SIDE, position % CORES]
    ).astype(jnp.int32)
    table = jnp.concatenate(
        [request_entry, block_request[0], fetch_source[:, 0], fetch_slot]
    )
    table = jnp.stack([table, lax.ppermute(table, "group", swap)])
    sib_tokens = lax.ppermute(tokens, "group", swap)

    halves = (
        jnp.concatenate([a_pool[:, :half], b_pool[:, :, :HEAD]], axis=1),
        jnp.concatenate([a_pool[:, half:], b_pool[:, :, HEAD:]], axis=1),
    )
    orders = ((along_y, along_x), (along_x, along_y))

    def send(value, way):
        return lax.ppermute(value, "group", way)

    lines = []
    for held, (line, _) in zip(halves, orders):
        up, down = send(held, line[0]), send(held, line[1])
        lines.append((held, up, down))
    gathered = []
    for (held, up, down), (line, _) in zip(lines, orders):
        far_up, far_down = send(up[:1], line[0]), send(down[1:], line[1])
        gathered.append(jnp.concatenate([held, up, down, far_up, far_down], axis=0))
    near = [
        (line, send(line, other[0]), send(line, other[1]))
        for line, (_, other) in zip(gathered, orders)
    ]
    first, second = [
        (line, up, down, send(up[: 2 * pool], other[0]), send(down[2 * pool :], other[1]))
        for (line, up, down), (_, other) in zip(near, orders)
    ]

    sizes = (request_entry.shape[0], blocks, fetch_slot.shape[0], pool)
    own, sib = partial_shrink(table, place, tokens, sib_tokens, first, second, sizes)
    both = own + lax.ppermute(sib, "group", swap)
    tile = rows // blocks
    shrink = both[:, :tile].reshape(rows, LANES)
    lift = both[:, tile:]

    shrink = lax.all_to_all(shrink, "tensor", split_axis=0, concat_axis=0, tiled=True)
    shrink = jnp.sum(
        shrink.reshape(tensor, rows // tensor, LANES).astype(jnp.float32), axis=0
    ).astype(jnp.bfloat16)
    shrink = jnp.broadcast_to(shrink[None], (tensor,) + shrink.shape).reshape(rows, LANES)
    shrink = lax.all_to_all(shrink, "tensor", split_axis=0, concat_axis=0, tiled=True)
    return finish(base, shrink, lift)


def solution(mesh):
    placed = (
        P("group", "tensor"),
        P("tensor", None),
        P("group", "tensor", None),
        P("group", None, "tensor"),
        P("group"),
        P("group", None),
        P("group", None),
        P("group"),
    )
    return jax.shard_map(
        per_device, mesh=mesh, in_specs=placed, out_specs=P("tensor", "group"), check_vma=False
    )
```

time: 362 us -> 177 us (0.49)
  waiting for transfers between devices: 230 us -> 47 us
  Pallas kernels: 0 us -> 30.8 us
  matrix products: 20.6 us -> 0 us
  starting transfers between devices: 6.86 us -> 21.9 us
  blocking collectives: 57 us -> 45.1 us
  other arithmetic: 9.65 us -> 0.67 us
  local copies, waits for them, and re-layouts: 22.6 us -> 15.4 us
    all_to_all x1 -> x0, waiting for transfers between devices: 100 us -> none  [per_device(): lax.all_to_all(outgoing_a, 'group', split_axis=0, concat_axis=0, tiled=True)]
    reduce_scatter x1, waiting for transfers between devices: 93.3 us -> 0.01 us  [per_device(): lax.psum_scatter(partial.reshape(tensor * rows, -1), 'tensor', scatter_di...]
    ppermute x0 -> x19, waiting for transfers between devices: none -> 47 us  [the longest x16 44.3 us: send(): return lax.ppermute(value, 'group', way)]
    psum x1 -> x0, waiting for transfers between devices: 36.9 us -> none  [per_device(): shrink = lax.psum(partial_value.astype(jnp.bfloat16), 'tensor')]
    pallas_call x0 -> x3, Pallas kernels: none -> 30.8 us  [the longest x1 15.8 us: base_partial(): pl.pallas_call(base_kernel, grid=(parts,), in_specs=[pl.BlockSpec((rows,...]
    ppermute x0 -> x19, starting transfers between devices: none -> 21.9 us  [the longest x16 21.7 us: send(): return lax.ppermute(value, 'group', way)]
    dot_general x3 -> x0, matrix products: 20.6 us -> none  [the longest x1 14.1 us: per_device(): lax.dot_general(kv_weight, tokens, (((0,), (1,)), ((), ())), preferred_el...]
    gather x7 -> x0, local copies, waits for them, and re-layouts: 19.6 us -> none  [the longest x1 6.28 us: per_device(): fetched_a = arrived_a[source, position]]
  transfers between devices with their start and end apart: 3 -> 20, of which waited for: 3 -> 10; matrix products, arithmetic and copies ran while one was open for 5% -> 3% of each run, Pallas kernels for 0% -> 7%
where the time goes in v1:
time: 177 us; the launch traced here: 174 us
  waiting for transfers between devices  47 us (27%)
  blocking collectives  45.1 us (25%)
  Pallas kernels  30.8 us (17%)
  starting transfers between devices  21.9 us (12%)
  local copies, waits for them, and re-layouts  15.4 us (9%)
  between operations  13.6 us (8%)
    all_to_all x2, blocking collectives, per_device(): lax.all_to_all(shrink, 'tensor', split_axis=0, concat_axis=0, tiled=True)  45.1 us
    ppermute x16, waiting for transfers between devices, send(): return lax.ppermute(value, 'group', way)  44.3 us
    ppermute x16, starting transfers between devices, send(): return lax.ppermute(value, 'group', way)  21.7 us
    pallas_call x1, Pallas kernels, base_partial(): pl.pallas_call(base_kernel, grid=(parts,), in_specs=[pl.BlockSpec((rows,...  15.8 us
    pallas_call x1, Pallas kernels, partial_shrink(): pl.pallas_call(functools.partial(shrink_kernel, requests, blocks, fetches...  12.6 us
    unnamed x36, local copies, waits for them, and re-layouts  11.7 us
  transfers between devices with their start and end apart: 20, of which 10 were waited for; matrix products, arithmetic and copies ran while one was open for 3% of the time, Pallas kernels for 7%

profile of v1, /device:TPU:24, one launch (start us, length us, event | category | flops | bytes accessed | tf_op | source)
XLA Modules:
  0.0 174.5 jit_solution(2704729439535499448)
XLA Ops:
  6.5 2.2 %copy-done = bf16[2048,1024]{1,0:T(8,128)(2,1)S(1)} copy-done((bf16[2048,1024]{1,0:T(8,128)(2,1)S(1)}, bf16[2048,1024]{1,0:T(8,128)(2,1)}, u32[]{:S(2)}) %copy-start) | copy-done | bytes 4194328
  8.7 2.2 %copy-done.8 = bf16[1024,2048]{1,0:T(8,128)(2,1)S(1)} copy-done((bf16[1024,2048]{1,0:T(8,128)(2,1)S(1)}, bf16[1024,2048]{1,0:T(8,128)(2,1)}, u32[]{:S(2)}) %copy-start.8) | copy-done | bytes 4194328
  10.9 15.8 %base_partial.1 = bf16[8,2048,256]{2,1,0:T(8,128)(2,1)} custom-call(bf16[2048,1024]{1,0:T(8,128)(2,1)S(1)} %copy-done, bf16[1024,2048]{1,0:T(8,128)(2,1)S(1)} %copy-done.8), custom_call_target="tpu_custom_call" | custom-call | flops 8589934592 | bytes 16777216 | tf_op jit(solution)/shard_map/base_partial/pallas_call | solution.py:32
  27.9 1.6 collective-permute-start.10
  29.5 1.7 collective-permute-start.11
  31.3 2.0 %collective-permute-start.2 = (bf16[2,576,128]{2,1,0:T(8,128)(2,1)S(1)}, bf16[2,576,128]{2,1,0:T(8,128)(2,1)S(1)}, u32[]{:S(2)}, u32[]{:S(2)}) collective-permute-start(bf16[2,576,128]{2,1,0:T(8,128)(2,1)S(1)} %get-tuple-element.15), channel_id=1, source_target_pairs={{0,16},{8,24},{16,32},{24,40},{32,48},{40,56},{48,0},{56,8},{64,80... | collective-permute-start | bytes 884744 | tf_op jit(solution)/shard_map/ppermute | solution.py:263
  33.4 4.5 %collective-permute-done.10 = bf16[2,576,128]{2,1,0:T(8,128)(2,1)S(1)} collective-permute-done((bf16[2,576,128]{2,1,0:T(8,128)(2,1)S(1)}, bf16[2,576,128]{2,1,0:T(8,128)(2,1)S(1)}, u32[]{:S(2)}, u32[]{:S(2)}) %collective-permute-start.10) | collective-permute-done | bytes 294944 | tf_op jit(solution)/shard_map/ppermute | solution.py:263
  38.3 3.0 %collective-permute-start.13 = (bf16[1,576,128]{2,1,0:T(8,128)(2,1)S(1)}, bf16[1,576,128]{2,1,0:T(8,128)(2,1)S(1)}, u32[]{:S(2)}, u32[]{:S(2)}) collective-permute-start(bf16[1,576,128]{2,1,0:T(8,128)(2,1)S(1)} %slice.61), channel_id=1, source_target_pairs={{0,192},{8,200},{16,208},{24,216},{32,224},{40,232},{48,240},{56,2... | collective-permute-start | bytes 442376 | tf_op jit(solution)/shard_map/ppermute | solution.py:263
  41.4 1.8 %collective-permute-start.4 = (bf16[1,576,128]{2,1,0:T(8,128)(2,1)S(1)}, bf16[1,576,128]{2,1,0:T(8,128)(2,1)S(1)}, u32[]{:S(2)}, u32[]{:S(2)}) collective-permute-start(bf16[1,576,128]{2,1,0:T(8,128)(2,1)S(1)} %slice.56), channel_id=1, source_target_pairs={{0,16},{8,24},{16,32},{24,40},{32,48},{40,56},{48,0},{56,8},{64,80... | collective-permute-start | bytes 442376 | tf_op jit(solution)/shard_map/ppermute | solution.py:263
  45.3 2.5 %collective-permute-start.14 = (bf16[8,576,128]{2,1,0:T(8,128)(2,1)S(1)}, bf16[8,576,128]{2,1,0:T(8,128)(2,1)S(1)}, u32[]{:S(2)}, u32[]{:S(2)}) collective-permute-start(bf16[8,576,128]{2,1,0:T(8,128)(2,1)S(1)} %constant_dynamic-update-slice_fusion.5.refs_5_), channel_id=1, source_target_pairs={{0,16},{8,24},{16,32},{24,40},{32,48},{40,56},{48,0},{56,8},{64,80... | collective-permute-start | bytes 3538952 | tf_op jit(solution)/shard_map/ppermute | solution.py:263
  47.9 3.4 %collective-permute-done.5 = bf16[1,576,128]{2,1,0:T(8,128)(2,1)S(1)} collective-permute-done((bf16[1,576,128]{2,1,0:T(8,128)(2,1)S(1)}, bf16[1,576,128]{2,1,0:T(8,128)(2,1)S(1)}, u32[]{:S(2)}, u32[]{:S(2)}) %collective-permute-start.5) | collective-permute-done | bytes 147488 | tf_op jit(solution)/shard_map/ppermute | solution.py:263
  51.4 2.0 %collective-permute-start.6 = (bf16[8,576,128]{2,1,0:T(8,128)(2,1)S(1)}, bf16[8,576,128]{2,1,0:T(8,128)(2,1)S(1)}, u32[]{:S(2)}, u32[]{:S(2)}) collective-permute-start(bf16[8,576,128]{2,1,0:T(8,128)(2,1)S(1)} %constant_dynamic-update-slice_fusion.refs_0_), channel_id=1, source_target_pairs={{0,64},{8,72},{16,80},{24,88},{32,96},{40,104},{48,112},{56,120},{... | collective-permute-start | bytes 3538952 | tf_op jit(solution)/shard_map/ppermute | solution.py:263
  53.5 19.8 %collective-permute-done.15.refs_7_ = bf16[8,576,128]{2,1,0:T(8,128)(2,1)S(1)} collective-permute-done((bf16[8,576,128]{2,1,0:T(8,128)(2,1)S(1)}, bf16[8,576,128]{2,1,0:T(8,128)(2,1)S(1)}, u32[]{:S(2)}, u32[]{:S(2)}) %collective-permute-start.15) | collective-permute-done | bytes 1179680 | tf_op jit(solution)/shard_map/ppermute | solution.py:263
  75.0 3.3 %collective-permute-start.16 = (bf16[4,576,128]{2,1,0:T(8,128)(2,1)}, bf16[4,576,128]{2,1,0:T(8,128)(2,1)}, u32[]{:S(2)}, u32[]{:S(2)}) collective-permute-start(bf16[4,576,128]{2,1,0:T(8,128)(2,1)} %slice.62), channel_id=1, source_target_pairs={{0,16},{8,24},{16,32},{24,40},{32,48},{40,56},{48,0},{56,8},{64,80... | collective-permute-start | bytes 1769480 | tf_op jit(solution)/shard_map/ppermute | solution.py:263
  79.2 1.6 collective-permute-start.9
  83.2 8.2 %collective-permute-done.17.refs_9_ = bf16[4,576,128]{2,1,0:T(8,128)(2,1)} collective-permute-done((bf16[4,576,128]{2,1,0:T(8,128)(2,1)}, bf16[4,576,128]{2,1,0:T(8,128)(2,1)}, u32[]{:S(2)}, u32[]{:S(2)}) %collective-permute-start.17) | collective-permute-done | bytes 589856 | tf_op jit(solution)/shard_map/ppermute | solution.py:263
  91.6 3.1 %collective-permute-done.9.refs_4_ = bf16[4,576,128]{2,1,0:T(8,128)(2,1)} collective-permute-done((bf16[4,576,128]{2,1,0:T(8,128)(2,1)}, bf16[4,576,128]{2,1,0:T(8,128)(2,1)}, u32[]{:S(2)}, u32[]{:S(2)}) %collective-permute-start.9) | collective-permute-done | bytes 589856 | tf_op jit(solution)/shard_map/ppermute | solution.py:263
  94.7 4.4 %collective-permute-done.8.refs_3_ = bf16[4,576,128]{2,1,0:T(8,128)(2,1)} collective-permute-done((bf16[4,576,128]{2,1,0:T(8,128)(2,1)}, bf16[4,576,128]{2,1,0:T(8,128)(2,1)}, u32[]{:S(2)}, u32[]{:S(2)}) %collective-permute-start.8) | collective-permute-done | bytes 589856 | tf_op jit(solution)/shard_map/ppermute | solution.py:263
  101.7 1.3 copy-done.6
  103.0 12.6 %partial_shrink.1 = (bf16[16,256,128]{2,1,0:T(8,128)(2,1)S(1)}, bf16[16,256,128]{2,1,0:T(8,128)(2,1)S(1)}) custom-call(s32[2,56]{1,0:T(2,128)S(1)} %pad_add_fusion.table_ref, s32[3]{0:T(128)S(1)} %pad_add_fusion.2.place_ref, bf16[2048,1024]{1,0:T(8,128)(2,1)} %own_tokens.1, bf16[2048,1024]{1,0:T(8,128)(2,1)} %collective-permute-done.1.sib_tokens, ...), custom_call_target="tpu_custom_call" | custom-call | flops 536870912 | bytes 12582912 | tf_op jit(solution)/shard_map/partial_shrink/pallas_call | solution.py:151
  115.7 2.6 %collective-permute-done.18 = bf16[16,256,128]{2,1,0:T(8,128)(2,1)S(1)} collective-permute-done((bf16[16,256,128]{2,1,0:T(8,128)(2,1)S(1)}, bf16[16,256,128]{2,1,0:T(8,128)(2,1)S(1)}, u32[]{:S(2)}, u32[]{:S(2)}) %collective-permute-start.18) | collective-permute-done | bytes 1048608 | tf_op jit(solution)/shard_map/ppermute | solution.py:284
  118.8 26.0 %all_to_all.17 = bf16[8,256,128]{2,1,0:T(8,128)(2,1)S(1)} all-to-all(bf16[8,256,128]{2,1,0:T(8,128)(2,1)S(1)} %bitcast.12), channel_id=1, replica_groups=mesh['group'=32,'tensor'=8] {'tensor'}, dimensions={0} | all-to-all | bytes 1048576 | tf_op jit(solution)/shard_map/all_to_all | solution.py:289
  144.9 19.1 %all_to_all.18 = bf16[8,256,128]{2,1,0:T(8,128)(2,1)S(1)} all-to-all(bf16[8,256,128]{2,1,0:T(8,128)(2,1)S(1)} %broadcast_in_dim.2), channel_id=1, replica_groups=mesh['group'=32,'tensor'=8] {'tensor'}, dimensions={0} | all-to-all | bytes 1048576 | tf_op jit(solution)/shard_map/all_to_all | solution.py:294
  165.2 2.4 %finish.1 = bf16[256,2048]{1,0:T(8,128)(2,1)} custom-call(bf16[2048,256]{1,0:T(8,128)(2,1)S(1)} %copy-done.7, bf16[2048,128]{1,0:T(8,128)(2,1)S(1)} %bitcast.10, bf16[16,128,128]{2,1,0:T(8,128)(2,1)S(1)} %get-tuple-element.9.lift_ref), custom_call_target="tpu_custom_call" | custom-call | flops 402653184 | bytes 3145728 | tf_op jit(solution)/shard_map/finish/pallas_call | solution.py:196
  (79 shorter events, 13.7 us)
Async XLA Ops:
  6.5 157.5 %reduce-scatter.2.cloned.1.call-start = ((), (), s32[]{:S(2)}) async-start(), calls=%async_computation.3 | async-start | bytes 9437184 | tf_op jit(solution)/shard_map/reduce_scatter | solution.py:242
  26.7 72.4 %collective-permute-start.1 = (bf16[2048,1024]{1,0:T(8,128)(2,1)}, bf16[2048,1024]{1,0:T(8,128)(2,1)}, u32[]{:S(2)}, u32[]{:S(2)}) collective-permute-start(bf16[2048,1024]{1,0:T(8,128)(2,1)} %own_tokens.1), channel_id=1, source_target_pairs={{0,8},{8,0},{16,24},{24,16},{32,40},{40,32},{48,56},{56,48},{64,72... | collective-permute-start | bytes 12582920 | tf_op jit(solution)/shard_map/ppermute | solution.py:254
  27.9 10.0 %collective-permute-start.10 = (bf16[2,576,128]{2,1,0:T(8,128)(2,1)S(1)}, bf16[2,576,128]{2,1,0:T(8,128)(2,1)S(1)}, u32[]{:S(2)}, u32[]{:S(2)}) collective-permute-start(bf16[2,576,128]{2,1,0:T(8,128)(2,1)S(1)} %get-tuple-element.13), channel_id=1, source_target_pairs={{0,64},{8,72},{16,80},{24,88},{32,96},{40,104},{48,112},{56,120},{... | collective-permute-start | bytes 884744 | tf_op jit(solution)/shard_map/ppermute | solution.py:263
  29.5 8.8 %collective-permute-start.11 = (bf16[2,576,128]{2,1,0:T(8,128)(2,1)S(1)}, bf16[2,576,128]{2,1,0:T(8,128)(2,1)S(1)}, u32[]{:S(2)}, u32[]{:S(2)}) collective-permute-start(bf16[2,576,128]{2,1,0:T(8,128)(2,1)S(1)} %get-tuple-element.13), channel_id=1, source_target_pairs={{0,192},{8,200},{16,208},{24,216},{32,224},{40,232},{48,240},{56,2... | collective-permute-start | bytes 884744 | tf_op jit(solution)/shard_map/ppermute | solution.py:263
  31.3 10.1 %collective-permute-start.2 = (bf16[2,576,128]{2,1,0:T(8,128)(2,1)S(1)}, bf16[2,576,128]{2,1,0:T(8,128)(2,1)S(1)}, u32[]{:S(2)}, u32[]{:S(2)}) collective-permute-start(bf16[2,576,128]{2,1,0:T(8,128)(2,1)S(1)} %get-tuple-element.15), channel_id=1, source_target_pairs={{0,16},{8,24},{16,32},{24,40},{32,48},{40,56},{48,0},{56,8},{64,80... | collective-permute-start | bytes 884744 | tf_op jit(solution)/shard_map/ppermute | solution.py:263
  33.3 9.8 %collective-permute-start.3 = (bf16[2,576,128]{2,1,0:T(8,128)(2,1)S(1)}, bf16[2,576,128]{2,1,0:T(8,128)(2,1)S(1)}, u32[]{:S(2)}, u32[]{:S(2)}) collective-permute-start(bf16[2,576,128]{2,1,0:T(8,128)(2,1)S(1)} %get-tuple-element.15), channel_id=1, source_target_pairs={{0,48},{8,56},{16,0},{24,8},{32,16},{40,24},{48,32},{56,40},{64,11... | collective-permute-start | bytes 884744 | tf_op jit(solution)/shard_map/ppermute | solution.py:263
  37.9 6.4 %collective-permute-start.12 = (bf16[1,576,128]{2,1,0:T(8,128)(2,1)S(1)}, bf16[1,576,128]{2,1,0:T(8,128)(2,1)S(1)}, u32[]{:S(2)}, u32[]{:S(2)}) collective-permute-start(bf16[1,576,128]{2,1,0:T(8,128)(2,1)S(1)} %slice.60), channel_id=1, source_target_pairs={{0,64},{8,72},{16,80},{24,88},{32,96},{40,104},{48,112},{56,120},{... | collective-permute-start | bytes 442376 | tf_op jit(solution)/shard_map/ppermute | solution.py:263
  38.3 6.1 %collective-permute-start.13 = (bf16[1,576,128]{2,1,0:T(8,128)(2,1)S(1)}, bf16[1,576,128]{2,1,0:T(8,128)(2,1)S(1)}, u32[]{:S(2)}, u32[]{:S(2)}) collective-permute-start(bf16[1,576,128]{2,1,0:T(8,128)(2,1)S(1)} %slice.61), channel_id=1, source_target_pairs={{0,192},{8,200},{16,208},{24,216},{32,224},{40,232},{48,240},{56,2... | collective-permute-start | bytes 442376 | tf_op jit(solution)/shard_map/ppermute | solution.py:263
  41.4 6.5 %collective-permute-start.4 = (bf16[1,576,128]{2,1,0:T(8,128)(2,1)S(1)}, bf16[1,576,128]{2,1,0:T(8,128)(2,1)S(1)}, u32[]{:S(2)}, u32[]{:S(2)}) collective-permute-start(bf16[1,576,128]{2,1,0:T(8,128)(2,1)S(1)} %slice.56), channel_id=1, source_target_pairs={{0,16},{8,24},{16,32},{24,40},{32,48},{40,56},{48,0},{56,8},{64,80... | collective-permute-start | bytes 442376 | tf_op jit(solution)/shard_map/ppermute | solution.py:263
  43.2 8.1 %collective-permute-start.5 = (bf16[1,576,128]{2,1,0:T(8,128)(2,1)S(1)}, bf16[1,576,128]{2,1,0:T(8,128)(2,1)S(1)}, u32[]{:S(2)}, u32[]{:S(2)}) collective-permute-start(bf16[1,576,128]{2,1,0:T(8,128)(2,1)S(1)} %slice.57), channel_id=1, source_target_pairs={{0,48},{8,56},{16,0},{24,8},{32,16},{40,24},{48,32},{56,40},{64,11... | collective-permute-start | bytes 442376 | tf_op jit(solution)/shard_map/ppermute | solution.py:263
  43.7 9.7 %copy-start.11 = (s32[13]{0:T(128)S(1)}, s32[13]{0:T(128)}, u32[]{:S(2)}) copy-start(s32[13]{0:T(128)} %param.15) | copy-start | bytes 160
  43.7 9.7 %copy-start.12 = (s32[13,1]{0,1:T(1,128)S(1)}, s32[13,1]{0,1:T(1,128)}, u32[]{:S(2)}) copy-start(s32[13,1]{0,1:T(1,128)} %param.14) | copy-start | bytes 160
  44.4 30.6 %copy-start.3 = (bf16[8,576,128]{2,1,0:T(8,128)(2,1)}, bf16[8,576,128]{2,1,0:T(8,128)(2,1)S(1)}, u32[]{:S(2)}) copy-start(bf16[8,576,128]{2,1,0:T(8,128)(2,1)S(1)} %constant_dynamic-update-slice_fusion.5.refs_5_) | copy-start | bytes 3538948
  44.5 28.9 %collective-permute-start.15 = (bf16[8,576,128]{2,1,0:T(8,128)(2,1)S(1)}, bf16[8,576,128]{2,1,0:T(8,128)(2,1)S(1)}, u32[]{:S(2)}, u32[]{:S(2)}) collective-permute-start(bf16[8,576,128]{2,1,0:T(8,128)(2,1)S(1)} %constant_dynamic-update-slice_fusion.5.refs_5_), channel_id=1, source_target_pairs={{0,48},{8,56},{16,0},{24,8},{32,16},{40,24},{48,32},{56,40},{64,11... | collective-permute-start | bytes 3538952 | tf_op jit(solution)/shard_map/ppermute | solution.py:263
  45.3 28.9 %collective-permute-start.14 = (bf16[8,576,128]{2,1,0:T(8,128)(2,1)S(1)}, bf16[8,576,128]{2,1,0:T(8,128)(2,1)S(1)}, u32[]{:S(2)}, u32[]{:S(2)}) collective-permute-start(bf16[8,576,128]{2,1,0:T(8,128)(2,1)S(1)} %constant_dynamic-update-slice_fusion.5.refs_5_), channel_id=1, source_target_pairs={{0,16},{8,24},{16,32},{24,40},{32,48},{40,56},{48,0},{56,8},{64,80... | collective-permute-start | bytes 3538952 | tf_op jit(solution)/shard_map/ppermute | solution.py:263
  51.3 23.8 %copy-start.5 = (bf16[8,576,128]{2,1,0:T(8,128)(2,1)}, bf16[8,576,128]{2,1,0:T(8,128)(2,1)S(1)}, u32[]{:S(2)}) copy-start(bf16[8,576,128]{2,1,0:T(8,128)(2,1)S(1)} %constant_dynamic-update-slice_fusion.refs_0_) | copy-start | bytes 3538948
  51.3 23.8 %collective-permute-start.7 = (bf16[8,576,128]{2,1,0:T(8,128)(2,1)S(1)}, bf16[8,576,128]{2,1,0:T(8,128)(2,1)S(1)}, u32[]{:S(2)}, u32[]{:S(2)}) collective-permute-start(bf16[8,576,128]{2,1,0:T(8,128)(2,1)S(1)} %constant_dynamic-update-slice_fusion.refs_0_), channel_id=1, source_target_pairs={{0,192},{8,200},{16,208},{24,216},{32,224},{40,232},{48,240},{56,2... | collective-permute-start | bytes 3538952 | tf_op jit(solution)/shard_map/ppermute | solution.py:263
  51.4 27.8 %collective-permute-start.6 = (bf16[8,576,128]{2,1,0:T(8,128)(2,1)S(1)}, bf16[8,576,128]{2,1,0:T(8,128)(2,1)S(1)}, u32[]{:S(2)}, u32[]{:S(2)}) collective-permute-start(bf16[8,576,128]{2,1,0:T(8,128)(2,1)S(1)} %constant_dynamic-update-slice_fusion.refs_0_), channel_id=1, source_target_pairs={{0,64},{8,72},{16,80},{24,88},{32,96},{40,104},{48,112},{56,120},{... | collective-permute-start | bytes 3538952 | tf_op jit(solution)/shard_map/ppermute | solution.py:263
  73.3 9.4 %collective-permute-start = (s32[56]{0:T(128)S(1)}, s32[56]{0:T(128)S(1)}, u32[]{:S(2)}, u32[]{:S(2)}) collective-permute-start(s32[56]{0:T(128)S(1)} %pad_add_fusion.1), channel_id=1, source_target_pairs={{0,8},{8,0},{16,24},{24,16},{32,40},{40,32},{48,56},{56,48},{64,72... | collective-permute-start | bytes 680 | tf_op jit(solution)/shard_map/ppermute | solution.py:253
  74.2 17.3 %collective-permute-start.17 = (bf16[4,576,128]{2,1,0:T(8,128)(2,1)}, bf16[4,576,128]{2,1,0:T(8,128)(2,1)}, u32[]{:S(2)}, u32[]{:S(2)}) collective-permute-start(bf16[4,576,128]{2,1,0:T(8,128)(2,1)} %slice.63), channel_id=1, source_target_pairs={{0,48},{8,56},{16,0},{24,8},{32,16},{40,24},{48,32},{56,40},{64,11... | collective-permute-start | bytes 1769480 | tf_op jit(solution)/shard_map/ppermute | solution.py:263
  75.0 16.6 %collective-permute-start.16 = (bf16[4,576,128]{2,1,0:T(8,128)(2,1)}, bf16[4,576,128]{2,1,0:T(8,128)(2,1)}, u32[]{:S(2)}, u32[]{:S(2)}) collective-permute-start(bf16[4,576,128]{2,1,0:T(8,128)(2,1)} %slice.62), channel_id=1, source_target_pairs={{0,16},{8,24},{16,32},{24,40},{32,48},{40,56},{48,0},{56,8},{64,80... | collective-permute-start | bytes 1769480 | tf_op jit(solution)/shard_map/ppermute | solution.py:263
  79.2 15.5 %collective-permute-start.9 = (bf16[4,576,128]{2,1,0:T(8,128)(2,1)}, bf16[4,576,128]{2,1,0:T(8,128)(2,1)}, u32[]{:S(2)}, u32[]{:S(2)}) collective-permute-start(bf16[4,576,128]{2,1,0:T(8,128)(2,1)} %slice.59), channel_id=1, source_target_pairs={{0,192},{8,200},{16,208},{24,216},{32,224},{40,232},{48,240},{56,2... | collective-permute-start | bytes 1769480 | tf_op jit(solution)/shard_map/ppermute | solution.py:263
  82.7 16.4 %collective-permute-start.8 = (bf16[4,576,128]{2,1,0:T(8,128)(2,1)}, bf16[4,576,128]{2,1,0:T(8,128)(2,1)}, u32[]{:S(2)}, u32[]{:S(2)}) collective-permute-start(bf16[4,576,128]{2,1,0:T(8,128)(2,1)} %slice.58), channel_id=1, source_target_pairs={{0,64},{8,72},{16,80},{24,88},{32,96},{40,104},{48,112},{56,120},{... | collective-permute-start | bytes 1769480 | tf_op jit(solution)/shard_map/ppermute | solution.py:263
  115.6 2.7 %collective-permute-start.18 = (bf16[16,256,128]{2,1,0:T(8,128)(2,1)S(1)}, bf16[16,256,128]{2,1,0:T(8,128)(2,1)S(1)}, u32[]{:S(2)}, u32[]{:S(2)}) collective-permute-start(bf16[16,256,128]{2,1,0:T(8,128)(2,1)S(1)} %get-tuple-element.8), channel_id=1, source_target_pairs={{0,8},{8,0},{16,24},{24,16},{32,40},{40,32},{48,56},{56,48},{64,72... | collective-permute-start | bytes 3145736 | tf_op jit(solution)/shard_map/ppermute | solution.py:284
  (11 other events, 31.9 us)
Sparse Core Ops, SparseCore 0:
  26.8 97.5 reduce-scatter.1

commit v2 on v0

v2 whole, which is shorter than its diff:
```python
import functools

import jax
import jax.numpy as jnp
from jax import lax
from jax.experimental import pallas as pl
from jax.experimental.pallas import tpu as pltpu
from jax.sharding import PartitionSpec as P

HEAD = 128
TILE = 512
VMEM = 60 * 2**20
NT = (((1,), (1,)), ((), ()))


def product_kernel(arrived, owner_ref, tokens_ref, weight_ref, *refs):
    outs = refs[-10:-8]
    token_buf, weight_buf, arrived_buf, out_buf = refs[-8:-4]
    token_sems, weight_sems, arrived_sems, out_sems = refs[-4:]
    columns = outs[0].shape[1]
    tiles = token_buf.shape[0]
    each = tiles // 2

    def token_copy(i):
        return pltpu.make_async_copy(
            tokens_ref.at[pl.ds(i * TILE, TILE)], token_buf.at[i], token_sems.at[i]
        )

    def weight_copy(which):
        at = pl.ds(pl.multiple_of(owner_ref[which] * columns, columns), columns)
        return pltpu.make_async_copy(
            weight_ref.at[:, at], weight_buf.at[which], weight_sems.at[which]
        )

    def arrived_copy(which):
        return pltpu.make_async_copy(refs[which], arrived_buf.at[which], arrived_sems.at[which])

    def out_copy(which):
        return pltpu.make_async_copy(out_buf.at[which], outs[which], out_sems.at[which])

    def fetch(i):
        which = i // each
        token_copy(i).start()
        if i % each == 0:
            weight_copy(which).start()
            if arrived:
                arrived_copy(which).start()

    ahead = 2
    for i in range(ahead):
        fetch(i)
    for i in range(tiles):
        which = i // each
        token_copy(i).wait()
        if i % each == 0:
            weight_copy(which).wait()
            if arrived:
                arrived_copy(which).wait()
        if i + ahead < tiles:
            fetch(i + ahead)
        rows = slice(i % each * TILE, (i % each + 1) * TILE)
        total = jnp.dot(token_buf[i], weight_buf[which], preferred_element_type=jnp.float32)
        if arrived:
            total += arrived_buf[which, rows, :].astype(jnp.float32)
        out_buf[which, rows, :] = total.astype(out_buf.dtype)
        if i % each == each - 1:
            out_copy(which).start()
    for which in range(2):
        out_copy(which).wait()


def product(tokens, kv_weight, owners, columns, arrived=(), after=()):
    rows, depth = tokens.shape
    hbm = pl.BlockSpec(memory_space=pl.ANY)
    return pl.pallas_call(
        functools.partial(product_kernel, len(arrived)),
        in_specs=[pl.BlockSpec(memory_space=pltpu.SMEM)] + [hbm] * (2 + len(arrived) + len(after)),
        out_specs=[hbm] * 2,
        out_shape=[jax.ShapeDtypeStruct((rows // 2, columns), jnp.bfloat16)] * 2,
        scratch_shapes=[
            pltpu.VMEM((rows // TILE, TILE, depth), jnp.bfloat16),
            pltpu.VMEM((2, depth, columns), jnp.bfloat16),
            pltpu.VMEM((2, rows // 2, columns), jnp.bfloat16),
            pltpu.VMEM((2, rows // 2, columns), jnp.bfloat16),
            pltpu.SemaphoreType.DMA((rows // TILE,)),
            pltpu.SemaphoreType.DMA((2,)),
            pltpu.SemaphoreType.DMA((2,)),
            pltpu.SemaphoreType.DMA((2,)),
        ],
        cost_estimate=pl.CostEstimate(
            flops=2 * rows * depth * columns,
            bytes_accessed=2 * (rows * depth + (2 * depth + rows) * columns),
            transcendentals=0,
        ),
        compiler_params=pltpu.CompilerParams(vmem_limit_bytes=VMEM),
        name="product",
    )(owners, tokens, kv_weight, *arrived, *after)


def shrink_kernel(
    adapter_ref, tokens_ref, pool_ref, first_ref, second_ref, out_ref, token_buf, factor_buf, sems
):
    del first_ref, second_ref
    blocks, tile, _ = token_buf.shape

    def copies(b):
        at = pl.ds(pl.multiple_of(b * tile, tile), tile)
        return (
            pltpu.make_async_copy(tokens_ref.at[at], token_buf.at[b], sems.at[b, 0]),
            pltpu.make_async_copy(
                pool_ref.at[adapter_ref[b], pl.ds(0, token_buf.shape[2])],
                factor_buf.at[b],
                sems.at[b, 1],
            ),
        )

    for b in range(blocks):
        for copy in copies(b):
            copy.start()
    for b in range(blocks):
        for copy in copies(b):
            copy.wait()
        out_ref[b * tile : (b + 1) * tile, :] = jnp.dot(
            token_buf[b], factor_buf[b], preferred_element_type=jnp.float32
        ).astype(out_ref.dtype)


def partial_shrink(adapters, tokens, pools, after):
    blocks = adapters.shape[0]
    rows, depth = tokens.shape
    width = pools.shape[2]
    return pl.pallas_call(
        shrink_kernel,
        in_specs=[pl.BlockSpec(memory_space=pltpu.SMEM)]
        + [pl.BlockSpec(memory_space=pl.ANY)] * 4,
        out_specs=pl.BlockSpec(memory_space=pltpu.VMEM),
        out_shape=jax.ShapeDtypeStruct((rows, width), jnp.bfloat16),
        scratch_shapes=[
            pltpu.VMEM((blocks, rows // blocks, depth), jnp.bfloat16),
            pltpu.VMEM((blocks, depth, width), jnp.bfloat16),
            pltpu.SemaphoreType.DMA((blocks, 2)),
        ],
        cost_estimate=pl.CostEstimate(
            flops=2 * rows * depth * width,
            bytes_accessed=2 * (rows + blocks * width) * depth,
            transcendentals=0,
        ),
        compiler_params=pltpu.CompilerParams(vmem_limit_bytes=VMEM),
        name="partial_shrink",
    )(adapters, tokens, pools, *after)


def turn_kernel(adapter_ref, *refs):
    sums, pool_ref, out_ref, lift_ref, sems = refs[:4], *refs[4:]
    height = lift_ref.shape[1]
    first = pool_ref.shape[1] - height
    columns = out_ref.shape[0]
    half = out_ref.shape[1] // 2

    def copy(b):
        return pltpu.make_async_copy(
            pool_ref.at[adapter_ref[b], pl.ds(first, height)], lift_ref.at[b], sems.at[b]
        )

    for b in range(lift_ref.shape[0]):
        copy(b).start()
    line = lax.broadcasted_iota(jnp.int32, (columns, columns), 0)
    lane = lax.broadcasted_iota(jnp.int32, (columns, columns), 1)
    eye = jnp.where(line == lane, 1.0, 0.0).astype(jnp.bfloat16)
    for which in range(2):
        for start in range(0, half, TILE):
            at = slice(start, start + TILE)
            total = add(sums[2 * which][at, :], sums[2 * which + 1][at, :])
            out_ref[:, which * half + start : which * half + start + TILE] = lax.dot_general(
                eye, total, NT, preferred_element_type=jnp.float32
            ).astype(out_ref.dtype)
    for b in range(lift_ref.shape[0]):
        copy(b).wait()


def turn(adapters, sums, pools, height):
    rows, columns = 2 * sums[0].shape[0], sums[0].shape[1]
    blocks = adapters.shape[0]
    vmem = pl.BlockSpec(memory_space=pltpu.VMEM)
    return pl.pallas_call(
        turn_kernel,
        in_specs=[pl.BlockSpec(memory_space=pltpu.SMEM)]
        + [vmem] * 4
        + [pl.BlockSpec(memory_space=pl.ANY)],
        out_specs=[vmem] * 2,
        out_shape=[
            jax.ShapeDtypeStruct((columns, rows), jnp.bfloat16),
            jax.ShapeDtypeStruct((blocks, height, pools.shape[2]), jnp.bfloat16),
        ],
        scratch_shapes=[pltpu.SemaphoreType.DMA((blocks,))],
        cost_estimate=pl.CostEstimate(
            flops=2 * rows * columns * columns, bytes_accessed=6 * rows * columns, transcendentals=0
        ),
        compiler_params=pltpu.CompilerParams(vmem_limit_bytes=VMEM),
        name="turn",
    )(adapters, *sums, pools)


def finish_kernel(base_ref, shrink_ref, lift_ref, out_ref):
    blocks, height, _ = lift_ref.shape
    rank = height // 2
    tile = base_ref.shape[1] // blocks
    for b in range(blocks):
        at = slice(b * tile, (b + 1) * tile)
        for kind in range(2):
            rows = slice(kind * HEAD, (kind + 1) * HEAD)
            ranks = slice(kind * rank, (kind + 1) * rank)
            delta = lax.dot_general(
                lift_ref[b, ranks, :],
                shrink_ref[at, ranks],
                (((0,), (1,)), ((), ())),
                preferred_element_type=jnp.float32,
            )
            out_ref[rows, at] = (base_ref[rows, at].astype(jnp.float32) + delta).astype(
                out_ref.dtype
            )


def finish(base, shrink, lift):
    columns, rows = base.shape
    steps = 2
    step, lifts = rows // steps, lift.shape[0] // steps
    return pl.pallas_call(
        finish_kernel,
        grid=(steps,),
        in_specs=[
            pl.BlockSpec((columns, step), lambda i: (0, i)),
            pl.BlockSpec((step, shrink.shape[1]), lambda i: (i, 0)),
            pl.BlockSpec((lifts,) + lift.shape[1:], lambda i: (i, 0, 0)),
        ],
        out_specs=pl.BlockSpec((columns, step), lambda i: (0, i)),
        out_shape=jax.ShapeDtypeStruct((columns, rows), jnp.bfloat16),
        cost_estimate=pl.CostEstimate(
            flops=2 * rows * columns * HEAD, bytes_accessed=6 * rows * columns, transcendentals=0
        ),
        compiler_params=pltpu.CompilerParams(vmem_limit_bytes=VMEM),
        name="finish",
    )(base, shrink, lift)


def add(*terms):
    return sum(term.astype(jnp.float32) for term in terms).astype(jnp.bfloat16)


def ring_sum(tokens, kv_weight, between):
    count = lax.axis_size("tensor")
    me = lax.axis_index("tensor")
    far = count // 2

    def hop(value, way):
        return lax.ppermute(value, "tensor", [(i, (i + way) % count) for i in range(count)])

    ways = (1, -1)
    columns = kv_weight.shape[1] // count

    def at(shift, arrived=(), after=()):
        owners = (me + jnp.array([way * shift for way in ways], jnp.int32) + count) % count
        return product(tokens, kv_weight, owners, columns, arrived, after)

    long = at(far)
    short = at(1 - far, after=long[:1])
    for step in range(1, far):
        long = at(far - step, [hop(value, way) for value, way in zip(long, ways)], short[:1])
        arrived = [hop(value, -way) for value, way in zip(short, ways)]
        after = long[0]
        if step == far - 1:
            last = [hop(value, way) for value, way in zip(long, ways)]
            made = after = between(arrived, last)
        short = at(1 - far + step, arrived, [after])
    return made, [value for pair in zip(last, short) for value in pair]


def block_adapters(pool, entries, requests, sources, slots):
    def pick(values, at):
        hit = at[:, None] == jnp.arange(values.shape[0], dtype=jnp.int32)[None]
        return jnp.sum(jnp.where(hit, values[None], 0), axis=1)

    entry = pick(entries, requests)
    fetch = jnp.clip(entry - pool, 0, slots.shape[0] - 1)
    adapter = pick(sources * pool + slots, fetch)
    return jnp.where(entry < pool, lax.axis_index("group") * pool + entry, adapter)


def per_device(
    tokens, kv_weight, a_pool, b_pool, request_entry, block_request, fetch_source, fetch_slot
):
    tensor = lax.axis_size("tensor")
    rows = tokens.shape[0]
    depth = tokens.shape[1]
    held = jnp.concatenate([a_pool, b_pool[:, :, :HEAD], b_pool[:, :, HEAD:]], axis=1)
    pools = lax.all_gather(held, "group", tiled=True)
    adapters = block_adapters(
        a_pool.shape[0], request_entry, block_request[0], fetch_source[:, 0], fetch_slot
    )

    def adapted(arrived, last):
        shrink = partial_shrink(adapters, tokens, pools, arrived)
        shrink, _ = lax.optimization_barrier((shrink, last))
        shrink = lax.all_to_all(shrink, "tensor", split_axis=0, concat_axis=0, tiled=True)
        shrink = shrink.reshape(tensor, rows // tensor, shrink.shape[1]).astype(jnp.float32)
        return jnp.sum(shrink, axis=0).astype(jnp.bfloat16)

    shrink, sums = ring_sum(tokens, kv_weight, adapted)
    shrink = jnp.broadcast_to(shrink[None], (tensor,) + shrink.shape).reshape(rows, -1)
    shrink = lax.all_to_all(shrink, "tensor", split_axis=0, concat_axis=0, tiled=True)
    base, lift = turn(adapters, sums, pools, pools.shape[1] - depth)
    return finish(base, shrink, lift)


def solution(mesh):
    placed = (
        P("group", "tensor"),
        P("tensor", None),
        P("group", "tensor", None),
        P("group", None, "tensor"),
        P("group"),
        P("group", None),
        P("group", None),
        P("group"),
    )
    return jax.shard_map(
        per_device, mesh=mesh, in_specs=placed, out_specs=P("tensor", "group"), check_vma=False
    )
```

time: 362 us -> 160 us (0.44)
  waiting for transfers between devices: 230 us -> 14.8 us
  Pallas kernels: 0 us -> 62.9 us
  blocking collectives: 57 us -> 22.6 us
  matrix products: 20.6 us -> 0 us
  starting transfers between devices: 6.86 us -> 27.3 us
  local copies, waits for them, and re-layouts: 22.6 us -> 10.6 us
    all_to_all x1, waiting for transfers between devices: 100 us -> 5.79 us  [per_device(): lax.all_to_all(shrink, 'tensor', split_axis=0, concat_axis=0, tiled=True)]
    reduce_scatter x1 -> x0, waiting for transfers between devices: 93.3 us -> none  [per_device(): lax.psum_scatter(lax.dot_general(kv_weight, tokens, (((0,), (1,)), ((), (...]
    pallas_call x0 -> x11, Pallas kernels: none -> 62.9 us  [the longest x8 49.3 us: product(): pl.pallas_call(functools.partial(product_kernel, len(arrived)), in_specs=...]
    psum x1 -> x0, waiting for transfers between devices: 36.9 us -> none  [per_device(): shrink = lax.psum(partial_value.astype(jnp.bfloat16), 'tensor')]
    all_to_all x2 -> x1, blocking collectives: 57 us -> 22.6 us  [adapted(): lax.all_to_all(shrink, 'tensor', split_axis=0, concat_axis=0, tiled=True)]
    ppermute x0 -> x14, starting transfers between devices: none -> 23.6 us  [hop(): lax.ppermute(value, 'tensor', [(i, (i + way) % count) for i in range(coun...]
    dot_general x3 -> x0, matrix products: 20.6 us -> none  [the longest x1 14.1 us: per_device(): lax.dot_general(kv_weight, tokens, (((0,), (1,)), ((), ())), preferred_el...]
    gather x7 -> x0, local copies, waits for them, and re-layouts: 19.6 us -> none  [the longest x1 6.28 us: per_device(): fetched_a = arrived_a[source, position]]
  transfers between devices with their start and end apart: 3 -> 16, of which waited for: 3 -> 8; matrix products, arithmetic and copies ran while one was open for 5% -> 3% of each run, Pallas kernels for 0% -> 38%
where the time goes in v2:
time: 160 us; the launch traced here: 158 us
  Pallas kernels  62.9 us (39%)
  starting transfers between devices  27.3 us (17%)
  blocking collectives  22.6 us (14%)
  waiting for transfers between devices  14.8 us (9%)
  between operations  13.6 us (8%)
  local copies, waits for them, and re-layouts  10.6 us (7%)
  other arithmetic  6.25 us (4%)
    pallas_call x8, Pallas kernels, product(): pl.pallas_call(functools.partial(product_kernel, len(arrived)), in_specs=...  49.3 us
    ppermute x14, starting transfers between devices, hop(): lax.ppermute(value, 'tensor', [(i, (i + way) % count) for i in range(coun...  23.6 us
    all_to_all x1, blocking collectives, adapted(): lax.all_to_all(shrink, 'tensor', split_axis=0, concat_axis=0, tiled=True)  22.6 us
    ppermute x14, waiting for transfers between devices, hop(): lax.ppermute(value, 'tensor', [(i, (i + way) % count) for i in range(coun...  8.97 us
    unnamed x54, local copies, waits for them, and re-layouts  8.42 us
    pallas_call x1, Pallas kernels, partial_shrink(): pl.pallas_call(shrink_kernel, in_specs=[pl.BlockSpec(memory_space=pltpu.S...  6.65 us
    all_to_all x1, waiting for transfers between devices, per_device(): lax.all_to_all(shrink, 'tensor', split_axis=0, concat_axis=0, tiled=True)  5.79 us
    pallas_call x1, Pallas kernels, turn(): pl.pallas_call(turn_kernel, in_specs=[pl.BlockSpec(memory_space=pltpu.SME...  3.84 us
  transfers between devices with their start and end apart: 16, of which 8 were waited for; matrix products, arithmetic and copies ran while one was open for 3% of the time, Pallas kernels for 38%

profile of v2, /device:TPU:24, one launch (start us, length us, event | category | flops | bytes accessed | tf_op | source)
XLA Modules:
  0.0 158.0 jit_solution(7424142459678345281)
XLA Ops:
  7.3 1.9 %pad_maximum_fusion = bf16[2,1152,128]{2,1,0:T(8,128)(2,1)} fusion(bf16[2,64,128]{2,1,0:T(8,128)(2,1)S(1)} %get-tuple-element.44, bf16[2,64,128]{2,1,0:T(8,128)(2,1)S(1)} %get-tuple-element.43, bf16[2,1024,128]{2,1,0:T(8,128)(2,1)} %param.18), kind=kLoop, calls=%fused_computation | loop fusion | flops 1769472 | bytes 1179648 | tf_op jit(solution)/shard_map/concatenate | solution.py:295
  9.9 5.7 %product.8 = (bf16[1024,256]{1,0:T(8,128)(2,1)}, bf16[1024,256]{1,0:T(8,128)(2,1)}) custom-call(s32[2]{0:T(128)} %get-tuple-element.46.owner_ref, bf16[2048,1024]{1,0:T(8,128)(2,1)} %tokens_ref.17, bf16[1024,2048]{1,0:T(8,128)(2,1)} %weight_ref.15), custom_call_target="tpu_custom_call" | custom-call | flops 1073741824 | bytes 6291456 | tf_op jit(solution)/shard_map/product/pallas_call | solution.py:75
  15.6 5.9 %collective-permute-start.1 = (bf16[1024,256]{1,0:T(8,128)(2,1)}, bf16[1024,256]{1,0:T(8,128)(2,1)S(1)}, u32[]{:S(2)}, u32[]{:S(2)}) collective-permute-start(bf16[1024,256]{1,0:T(8,128)(2,1)} %get-tuple-element.25), channel_id=1, source_target_pairs={{0,7},{1,0},{2,1},{3,2},{4,3},{5,4},{6,5},{7,6},{8,15},{9,8},{10,9... | collective-permute-start | bytes 1572872 | tf_op jit(solution)/shard_map/ppermute | solution.py:256
  21.6 6.0 %product.9 = (bf16[1024,256]{1,0:T(8,128)(2,1)}, bf16[1024,256]{1,0:T(8,128)(2,1)}) custom-call(s32[2]{0:T(128)} %get-tuple-element.45.owner_ref, bf16[2048,1024]{1,0:T(8,128)(2,1)} %tokens_ref.17, bf16[1024,2048]{1,0:T(8,128)(2,1)} %weight_ref.15, bf16[1024,256]{1,0:T(8,128)(2,1)} %get-tuple-element.24.refs_0_), custom_call_target="tpu_custom_call" | custom-call | flops 1073741824 | bytes 6291456 | tf_op jit(solution)/shard_map/product/pallas_call | solution.py:75
  27.6 3.3 %collective-permute-start.4 = (bf16[1024,256]{1,0:T(8,128)(2,1)}, bf16[1024,256]{1,0:T(8,128)(2,1)S(1)}, u32[]{:S(2)}, u32[]{:S(2)}) collective-permute-start(bf16[1024,256]{1,0:T(8,128)(2,1)} %get-tuple-element.26.refs_2_), channel_id=1, source_target_pairs={{0,7},{1,0},{2,1},{3,2},{4,3},{5,4},{6,5},{7,6},{8,15},{9,8},{10,9... | collective-permute-start | bytes 1572872 | tf_op jit(solution)/shard_map/ppermute | solution.py:256
  32.3 1.9 %collective-permute-done.1.refs_1_ = bf16[1024,256]{1,0:T(8,128)(2,1)S(1)} collective-permute-done((bf16[1024,256]{1,0:T(8,128)(2,1)}, bf16[1024,256]{1,0:T(8,128)(2,1)S(1)}, u32[]{:S(2)}, u32[]{:S(2)}) %collective-permute-start.1) | collective-permute-done | bytes 524320 | tf_op jit(solution)/shard_map/ppermute | solution.py:256
  34.2 3.6 %collective-permute-done.refs_0_ = bf16[1024,256]{1,0:T(8,128)(2,1)S(1)} collective-permute-done((bf16[1024,256]{1,0:T(8,128)(2,1)}, bf16[1024,256]{1,0:T(8,128)(2,1)S(1)}, u32[]{:S(2)}, u32[]{:S(2)}) %collective-permute-start) | collective-permute-done | bytes 524320 | tf_op jit(solution)/shard_map/ppermute | solution.py:256
  38.6 6.1 %product.10 = (bf16[1024,256]{1,0:T(8,128)(2,1)}, bf16[1024,256]{1,0:T(8,128)(2,1)}) custom-call(s32[2]{0:T(128)} %and_select_fusion.4.owner_ref, bf16[2048,1024]{1,0:T(8,128)(2,1)} %tokens_ref.17, bf16[1024,2048]{1,0:T(8,128)(2,1)} %weight_ref.15, bf16[1024,256]{1,0:T(8,128)(2,1)} %copy-done.11, bf16[1024,256]{1,0:T(8,128)(2,1)} %copy-done.8, ...), custom_call_target="tpu_custom_call" | custom-call | flops 1073741824 | bytes 6291456 | tf_op jit(solution)/shard_map/product/pallas_call | solution.py:75
  49.5 6.8 %product.11 = (bf16[1024,256]{1,0:T(8,128)(2,1)}, bf16[1024,256]{1,0:T(8,128)(2,1)}) custom-call(s32[2]{0:T(128)} %and_select_fusion.1.owner_ref, bf16[2048,1024]{1,0:T(8,128)(2,1)} %tokens_ref.17, bf16[1024,2048]{1,0:T(8,128)(2,1)} %weight_ref.15, bf16[1024,256]{1,0:T(8,128)(2,1)} %copy-done.7, bf16[1024,256]{1,0:T(8,128)(2,1)} %copy-done.6, ...), custom_call_target="tpu_custom_call" | custom-call | flops 1073741824 | bytes 6291456 | tf_op jit(solution)/shard_map/product/pallas_call | solution.py:75
  56.4 3.2 %collective-permute-start.8 = (bf16[1024,256]{1,0:T(8,128)(2,1)}, bf16[1024,256]{1,0:T(8,128)(2,1)S(1)}, u32[]{:S(2)}, u32[]{:S(2)}) collective-permute-start(bf16[1024,256]{1,0:T(8,128)(2,1)} %get-tuple-element.30.refs_2_), channel_id=1, source_target_pairs={{0,7},{1,0},{2,1},{3,2},{4,3},{5,4},{6,5},{7,6},{8,15},{9,8},{10,9... | collective-permute-start | bytes 1572872 | tf_op jit(solution)/shard_map/ppermute | solution.py:256
  61.2 6.2 %product.12 = (bf16[1024,256]{1,0:T(8,128)(2,1)}, bf16[1024,256]{1,0:T(8,128)(2,1)}) custom-call(s32[2]{0:T(128)} %and_select_fusion.5.owner_ref, bf16[2048,1024]{1,0:T(8,128)(2,1)} %tokens_ref.17, bf16[1024,2048]{1,0:T(8,128)(2,1)} %weight_ref.15, bf16[1024,256]{1,0:T(8,128)(2,1)} %copy-done.13, bf16[1024,256]{1,0:T(8,128)(2,1)} %copy-done.9, ...), custom_call_target="tpu_custom_call" | custom-call | flops 1073741824 | bytes 6291456 | tf_op jit(solution)/shard_map/product/pallas_call | solution.py:75
  67.6 1.9 %collective-permute-start.6 = (bf16[1024,256]{1,0:T(8,128)(2,1)}, bf16[1024,256]{1,0:T(8,128)(2,1)S(1)}, u32[]{:S(2)}, u32[]{:S(2)}) collective-permute-start(bf16[1024,256]{1,0:T(8,128)(2,1)} %get-tuple-element.31.refs_2_), channel_id=1, source_target_pairs={{0,1},{1,2},{2,3},{3,4},{4,5},{5,6},{6,7},{7,0},{8,9},{9,10},{10,1... | collective-permute-start | bytes 1572872 | tf_op jit(solution)/shard_map/ppermute | solution.py:256
  72.9 6.3 %product.13 = (bf16[1024,256]{1,0:T(8,128)(2,1)}, bf16[1024,256]{1,0:T(8,128)(2,1)}) custom-call(s32[2]{0:T(128)} %and_select_fusion.owner_ref, bf16[2048,1024]{1,0:T(8,128)(2,1)} %tokens_ref.17, bf16[1024,2048]{1,0:T(8,128)(2,1)} %weight_ref.15, bf16[1024,256]{1,0:T(8,128)(2,1)} %copy-done.14, bf16[1024,256]{1,0:T(8,128)(2,1)} %copy-done.10, ...), custom_call_target="tpu_custom_call" | custom-call | flops 1073741824 | bytes 6291456 | tf_op jit(solution)/shard_map/product/pallas_call | solution.py:75
  79.3 3.4 %collective-permute-start.11 = (bf16[1024,256]{1,0:T(8,128)(2,1)}, bf16[1024,256]{1,0:T(8,128)(2,1)S(1)}, u32[]{:S(2)}, u32[]{:S(2)}) collective-permute-start(bf16[1024,256]{1,0:T(8,128)(2,1)} %get-tuple-element.34.refs_2_), channel_id=1, source_target_pairs={{0,7},{1,0},{2,1},{3,2},{4,3},{5,4},{6,5},{7,6},{8,15},{9,8},{10,9... | collective-permute-start | bytes 1572872 | tf_op jit(solution)/shard_map/ppermute | solution.py:256
  84.3 6.3 %product.14 = (bf16[1024,256]{1,0:T(8,128)(2,1)}, bf16[1024,256]{1,0:T(8,128)(2,1)}) custom-call(s32[2]{0:T(128)} %and_select_fusion.6.owner_ref, bf16[2048,1024]{1,0:T(8,128)(2,1)} %tokens_ref.17, bf16[1024,2048]{1,0:T(8,128)(2,1)} %weight_ref.15, bf16[1024,256]{1,0:T(8,128)(2,1)} %copy-done.15, bf16[1024,256]{1,0:T(8,128)(2,1)} %copy-done.12, ...), custom_call_target="tpu_custom_call" | custom-call | flops 1073741824 | bytes 6291456 | tf_op jit(solution)/shard_map/product/pallas_call | solution.py:75
  90.6 3.2 %collective-permute-start.13 = (bf16[1024,256]{1,0:T(8,128)(2,1)}, bf16[1024,256]{1,0:T(8,128)(2,1)S(1)}, u32[]{:S(2)}, u32[]{:S(2)}) collective-permute-start(bf16[1024,256]{1,0:T(8,128)(2,1)} %get-tuple-element.37), channel_id=1, source_target_pairs={{0,7},{1,0},{2,1},{3,2},{4,3},{5,4},{6,5},{7,6},{8,15},{9,8},{10,9... | collective-permute-start | bytes 1572872 | tf_op jit(solution)/shard_map/ppermute | solution.py:256
  95.8 6.7 %partial_shrink.1 = bf16[2048,128]{1,0:T(8,128)(2,1)} custom-call(s32[16]{0:T(128)} %compare_select_fusion.14.adapter_ref, bf16[2048,1024]{1,0:T(8,128)(2,1)} %tokens_ref.17, bf16[64,1152,128]{2,1,0:T(8,128)(2,1)} %all-gather.2.cloned.1.call-done.pool_ref.refs_4_, bf16[1024,256]{1,0:T(8,128)(2,1)} %copy-done.1, bf16[1024,256]{1,0:T(8,128)(2,1)} %copy-done), custom_call_target="tpu_custom_call" | custom-call | flops 536870912 | bytes 8388608 | tf_op jit(solution)/shard_map/partial_shrink/pallas_call | solution.py:132
  102.5 1.3 collective-permute-done.10.refs_0_
  103.8 22.6 %all_to_all.17 = bf16[8,256,128]{2,1,0:T(8,128)(2,1)S(1)} all-to-all(bf16[8,256,128]{2,1,0:T(8,128)(2,1)} %bitcast.5), channel_id=1, replica_groups=mesh['group'=32,'tensor'=8] {'tensor'}, dimensions={0} | all-to-all | bytes 1048576 | tf_op jit(solution)/shard_map/all_to_all | solution.py:304
  127.3 3.7 %all-to-all-start.1 = ((bf16[8,256,128]{2,1,0:T(8,128)(2,1)}), bf16[8,256,128]{2,1,0:T(8,128)(2,1)S(1)}, u32[]{:S(2)}, u32[]{:S(2)}) async-start(bf16[8,256,128]{2,1,0:T(8,128)(2,1)} %broadcast_in_dim.39), calls=%async_computation.1 | async-start | bytes 1048576 | tf_op jit(solution)/shard_map/all_to_all | solution.py:310
  131.6 6.1 %product.15 = (bf16[1024,256]{1,0:T(8,128)(2,1)}, bf16[1024,256]{1,0:T(8,128)(2,1)}) custom-call(s32[2]{0:T(128)} %broadcast.99.owner_ref, bf16[2048,1024]{1,0:T(8,128)(2,1)} %tokens_ref.17, bf16[1024,2048]{1,0:T(8,128)(2,1)} %weight_ref.15, bf16[1024,256]{1,0:T(8,128)(2,1)} %copy-done.1, bf16[1024,256]{1,0:T(8,128)(2,1)} %copy-done, bf16[256,128]{1,0:T(8,128)(2,1)} %copy-done.3), custom_call_target="tpu_custom_call" | custom-call | flops 1073741824 | bytes 6291456 | tf_op jit(solution)/shard_map/product/pallas_call | solution.py:75
  137.7 3.8 %turn.1 = (bf16[256,2048]{1,0:T(8,128)(2,1)}, bf16[16,128,128]{2,1,0:T(8,128)(2,1)}) custom-call(s32[16]{0:T(128)} %compare_select_fusion.14.adapter_ref, bf16[1024,256]{1,0:T(8,128)(2,1)} %copy-done.4, bf16[1024,256]{1,0:T(8,128)(2,1)} %get-tuple-element.39.refs_1_, bf16[1024,256]{1,0:T(8,128)(2,1)} %copy-done.5, ...), custom_call_target="tpu_custom_call" | custom-call | flops 268435456 | bytes 3145728 | tf_op jit(solution)/shard_map/turn/pallas_call | solution.py:185
  141.5 5.8 %all-to-all-done.1 = bf16[8,256,128]{2,1,0:T(8,128)(2,1)S(1)} async-done(((bf16[8,256,128]{2,1,0:T(8,128)(2,1)}), bf16[8,256,128]{2,1,0:T(8,128)(2,1)S(1)}, u32[]{:S(2)}, u32[]{:S(2)}) %all-to-all-start.1) | async-done | bytes 524320 | tf_op jit(solution)/shard_map/all_to_all | solution.py:310
  148.1 3.1 %finish.1 = bf16[256,2048]{1,0:T(8,128)(2,1)} custom-call(bf16[256,2048]{1,0:T(8,128)(2,1)} %get-tuple-element.41.base_ref, bf16[2048,128]{1,0:T(8,128)(2,1)} %bitcast.6, bf16[16,128,128]{2,1,0:T(8,128)(2,1)} %get-tuple-element.42.lift_ref), custom_call_target="tpu_custom_call" | custom-call | flops 134217728 | bytes 3145728 | tf_op jit(solution)/shard_map/finish/pallas_call | solution.py:228
  (91 shorter events, 19.8 us)
Async XLA Ops:
  6.5 88.3 %all-gather.2.cloned.1.call-start = ((), (), s32[]{:S(2)}) async-start(), calls=%async_computation.2 | async-start | bytes 19464192 | tf_op jit(solution)/shard_map/all_gather | solution.py:296
  15.6 18.6 %collective-permute-start.1 = (bf16[1024,256]{1,0:T(8,128)(2,1)}, bf16[1024,256]{1,0:T(8,128)(2,1)S(1)}, u32[]{:S(2)}, u32[]{:S(2)}) collective-permute-start(bf16[1024,256]{1,0:T(8,128)(2,1)} %get-tuple-element.25), channel_id=1, source_target_pairs={{0,7},{1,0},{2,1},{3,2},{4,3},{5,4},{6,5},{7,6},{8,15},{9,8},{10,9... | collective-permute-start | bytes 1572872 | tf_op jit(solution)/shard_map/ppermute | solution.py:256
  21.5 16.3 %collective-permute-start = (bf16[1024,256]{1,0:T(8,128)(2,1)}, bf16[1024,256]{1,0:T(8,128)(2,1)S(1)}, u32[]{:S(2)}, u32[]{:S(2)}) collective-permute-start(bf16[1024,256]{1,0:T(8,128)(2,1)} %get-tuple-element.24.refs_0_), channel_id=1, source_target_pairs={{0,1},{1,2},{2,3},{3,4},{4,5},{5,6},{6,7},{7,0},{8,9},{9,10},{10,1... | collective-permute-start | bytes 1572872 | tf_op jit(solution)/shard_map/ppermute | solution.py:256
  21.6 10.1 %copy-start.25 = (s32[2]{0:T(128)S(1)}, s32[2]{0:T(128)}, u32[]{:S(2)}) copy-start(s32[2]{0:T(128)} %constant.91.clone) | copy-start | bytes 28
  27.6 20.3 %collective-permute-start.5 = (bf16[1024,256]{1,0:T(8,128)(2,1)}, bf16[1024,256]{1,0:T(8,128)(2,1)S(1)}, u32[]{:S(2)}, u32[]{:S(2)}) collective-permute-start(bf16[1024,256]{1,0:T(8,128)(2,1)} %get-tuple-element.29), channel_id=1, source_target_pairs={{0,1},{1,2},{2,3},{3,4},{4,5},{5,6},{6,7},{7,0},{8,9},{9,10},{10,1... | collective-permute-start | bytes 1572872 | tf_op jit(solution)/shard_map/ppermute | solution.py:256
  27.6 20.2 %collective-permute-start.4 = (bf16[1024,256]{1,0:T(8,128)(2,1)}, bf16[1024,256]{1,0:T(8,128)(2,1)S(1)}, u32[]{:S(2)}, u32[]{:S(2)}) collective-permute-start(bf16[1024,256]{1,0:T(8,128)(2,1)} %get-tuple-element.26.refs_2_), channel_id=1, source_target_pairs={{0,7},{1,0},{2,1},{3,2},{4,3},{5,4},{6,5},{7,6},{8,15},{9,8},{10,9... | collective-permute-start | bytes 1572872 | tf_op jit(solution)/shard_map/ppermute | solution.py:256
  32.3 14.5 %copy-start.24 = (s32[2]{0:T(128)S(1)}, s32[2]{0:T(128)}, u32[]{:S(2)}) copy-start(s32[2]{0:T(128)} %constant.92.clone) | copy-start | bytes 28
  32.3 15.0 %copy-start.23 = (s32[2]{0:T(128)S(1)}, s32[2]{0:T(128)}, u32[]{:S(2)}) copy-start(s32[2]{0:T(128)} %constant.93.clone) | copy-start | bytes 28
  44.7 14.9 %collective-permute-start.3 = (bf16[1024,256]{1,0:T(8,128)(2,1)}, bf16[1024,256]{1,0:T(8,128)(2,1)S(1)}, u32[]{:S(2)}, u32[]{:S(2)}) collective-permute-start(bf16[1024,256]{1,0:T(8,128)(2,1)} %get-tuple-element.28), channel_id=1, source_target_pairs={{0,7},{1,0},{2,1},{3,2},{4,3},{5,4},{6,5},{7,6},{8,15},{9,8},{10,9... | collective-permute-start | bytes 1572872 | tf_op jit(solution)/shard_map/ppermute | solution.py:256
  45.5 14.0 %collective-permute-start.2 = (bf16[1024,256]{1,0:T(8,128)(2,1)}, bf16[1024,256]{1,0:T(8,128)(2,1)S(1)}, u32[]{:S(2)}, u32[]{:S(2)}) collective-permute-start(bf16[1024,256]{1,0:T(8,128)(2,1)} %get-tuple-element.27.refs_2_), channel_id=1, source_target_pairs={{0,1},{1,2},{2,3},{3,4},{4,5},{5,6},{6,7},{7,0},{8,9},{9,10},{10,1... | collective-permute-start | bytes 1572872 | tf_op jit(solution)/shard_map/ppermute | solution.py:256
  56.3 15.0 %collective-permute-start.9 = (bf16[1024,256]{1,0:T(8,128)(2,1)}, bf16[1024,256]{1,0:T(8,128)(2,1)S(1)}, u32[]{:S(2)}, u32[]{:S(2)}) collective-permute-start(bf16[1024,256]{1,0:T(8,128)(2,1)} %get-tuple-element.33), channel_id=1, source_target_pairs={{0,1},{1,2},{2,3},{3,4},{4,5},{5,6},{6,7},{7,0},{8,9},{9,10},{10,1... | collective-permute-start | bytes 1572872 | tf_op jit(solution)/shard_map/ppermute | solution.py:256
  56.3 13.2 %copy-start.22 = (s32[2]{0:T(128)S(1)}, s32[2]{0:T(128)}, u32[]{:S(2)}) copy-start(s32[2]{0:T(128)} %constant.94.clone) | copy-start | bytes 28
  56.4 13.7 %copy-start.20 = (s32[13]{0:T(128)S(1)}, s32[13]{0:T(128)}, u32[]{:S(2)}) copy-start(s32[13]{0:T(128)} %param.23) | copy-start | bytes 160
  56.4 13.7 %copy-start.21 = (s32[13,1]{0,1:T(1,128)S(1)}, s32[13,1]{0,1:T(1,128)}, u32[]{:S(2)}) copy-start(s32[13,1]{0,1:T(1,128)} %param.22) | copy-start | bytes 160
  56.4 15.4 %collective-permute-start.8 = (bf16[1024,256]{1,0:T(8,128)(2,1)}, bf16[1024,256]{1,0:T(8,128)(2,1)S(1)}, u32[]{:S(2)}, u32[]{:S(2)}) collective-permute-start(bf16[1024,256]{1,0:T(8,128)(2,1)} %get-tuple-element.30.refs_2_), channel_id=1, source_target_pairs={{0,7},{1,0},{2,1},{3,2},{4,3},{5,4},{6,5},{7,6},{8,15},{9,8},{10,9... | collective-permute-start | bytes 1572872 | tf_op jit(solution)/shard_map/ppermute | solution.py:256
  67.4 15.3 %collective-permute-start.7 = (bf16[1024,256]{1,0:T(8,128)(2,1)}, bf16[1024,256]{1,0:T(8,128)(2,1)S(1)}, u32[]{:S(2)}, u32[]{:S(2)}) collective-permute-start(bf16[1024,256]{1,0:T(8,128)(2,1)} %get-tuple-element.32), channel_id=1, source_target_pairs={{0,7},{1,0},{2,1},{3,2},{4,3},{5,4},{6,5},{7,6},{8,15},{9,8},{10,9... | collective-permute-start | bytes 1572872 | tf_op jit(solution)/shard_map/ppermute | solution.py:256
  67.6 15.2 %collective-permute-start.6 = (bf16[1024,256]{1,0:T(8,128)(2,1)}, bf16[1024,256]{1,0:T(8,128)(2,1)S(1)}, u32[]{:S(2)}, u32[]{:S(2)}) collective-permute-start(bf16[1024,256]{1,0:T(8,128)(2,1)} %get-tuple-element.31.refs_2_), channel_id=1, source_target_pairs={{0,1},{1,2},{2,3},{3,4},{4,5},{5,6},{6,7},{7,0},{8,9},{9,10},{10,1... | collective-permute-start | bytes 1572872 | tf_op jit(solution)/shard_map/ppermute | solution.py:256
  79.2 15.7 %collective-permute-start.12 = (bf16[1024,256]{1,0:T(8,128)(2,1)}, bf16[1024,256]{1,0:T(8,128)(2,1)S(1)}, u32[]{:S(2)}, u32[]{:S(2)}) collective-permute-start(bf16[1024,256]{1,0:T(8,128)(2,1)} %get-tuple-element.36), channel_id=1, source_target_pairs={{0,1},{1,2},{2,3},{3,4},{4,5},{5,6},{6,7},{7,0},{8,9},{9,10},{10,1... | collective-permute-start | bytes 1572872 | tf_op jit(solution)/shard_map/ppermute | solution.py:256
  79.3 15.6 %collective-permute-start.11 = (bf16[1024,256]{1,0:T(8,128)(2,1)}, bf16[1024,256]{1,0:T(8,128)(2,1)S(1)}, u32[]{:S(2)}, u32[]{:S(2)}) collective-permute-start(bf16[1024,256]{1,0:T(8,128)(2,1)} %get-tuple-element.34.refs_2_), channel_id=1, source_target_pairs={{0,7},{1,0},{2,1},{3,2},{4,3},{5,4},{6,5},{7,6},{8,15},{9,8},{10,9... | collective-permute-start | bytes 1572872 | tf_op jit(solution)/shard_map/ppermute | solution.py:256
  90.5 13.2 %collective-permute-start.10 = (bf16[1024,256]{1,0:T(8,128)(2,1)}, bf16[1024,256]{1,0:T(8,128)(2,1)S(1)}, u32[]{:S(2)}, u32[]{:S(2)}) collective-permute-start(bf16[1024,256]{1,0:T(8,128)(2,1)} %get-tuple-element.35), channel_id=1, source_target_pairs={{0,1},{1,2},{2,3},{3,4},{4,5},{5,6},{6,7},{7,0},{8,9},{9,10},{10,1... | collective-permute-start | bytes 1572872 | tf_op jit(solution)/shard_map/ppermute | solution.py:256
  90.6 13.1 %collective-permute-start.13 = (bf16[1024,256]{1,0:T(8,128)(2,1)}, bf16[1024,256]{1,0:T(8,128)(2,1)S(1)}, u32[]{:S(2)}, u32[]{:S(2)}) collective-permute-start(bf16[1024,256]{1,0:T(8,128)(2,1)} %get-tuple-element.37), channel_id=1, source_target_pairs={{0,7},{1,0},{2,1},{3,2},{4,3},{5,4},{6,5},{7,6},{8,15},{9,8},{10,9... | collective-permute-start | bytes 1572872 | tf_op jit(solution)/shard_map/ppermute | solution.py:256
  103.8 23.5 %copy-start.4 = (bf16[1024,256]{1,0:T(8,128)(2,1)}, bf16[1024,256]{1,0:T(8,128)(2,1)S(1)}, u32[]{:S(2)}) copy-start(bf16[1024,256]{1,0:T(8,128)(2,1)S(1)} %collective-permute-done.10.refs_0_) | copy-start | bytes 1572868
  103.8 23.5 %copy-start.5 = (bf16[1024,256]{1,0:T(8,128)(2,1)}, bf16[1024,256]{1,0:T(8,128)(2,1)S(1)}, u32[]{:S(2)}) copy-start(bf16[1024,256]{1,0:T(8,128)(2,1)S(1)} %collective-permute-done.13.refs_2_) | copy-start | bytes 1572868
  127.3 20.0 %all-to-all-start.1 = ((bf16[8,256,128]{2,1,0:T(8,128)(2,1)}), bf16[8,256,128]{2,1,0:T(8,128)(2,1)S(1)}, u32[]{:S(2)}, u32[]{:S(2)}) async-start(bf16[8,256,128]{2,1,0:T(8,128)(2,1)} %broadcast_in_dim.39), calls=%async_computation.1 | async-start | bytes 1048576 | tf_op jit(solution)/shard_map/all_to_all | solution.py:310
  (19 other events, 52.5 us)
Sparse Core Ops, SparseCore 0:
  9.9 84.6 all-gather.1

commit v3 on v2

--- a/solution.py
+++ b/solution.py
@@ -9,14 +9,13 @@
 
 HEAD = 128
 TILE = 512
-VMEM = 60 * 2**20
+VMEM = 50 * 2**20
 NT = (((1,), (1,)), ((), ()))
 
 
 def product_kernel(arrived, owner_ref, tokens_ref, weight_ref, *refs):
-    outs = refs[-10:-8]
-    token_buf, weight_buf, arrived_buf, out_buf = refs[-8:-4]
-    token_sems, weight_sems, arrived_sems, out_sems = refs[-4:]
+    outs = refs[-6:-4]
+    token_buf, weight_buf, token_sems, weight_sems = refs[-4:]
     columns = outs[0].shape[1]
     tiles = token_buf.shape[0]
     each = tiles // 2
@@ -32,19 +31,11 @@
             weight_ref.at[:, at], weight_buf.at[which], weight_sems.at[which]
         )
 
-    def arrived_copy(which):
-        return pltpu.make_async_copy(refs[which], arrived_buf.at[which], arrived_sems.at[which])
-
-    def out_copy(which):
-        return pltpu.make_async_copy(out_buf.at[which], outs[which], out_sems.at[which])
-
     def fetch(i):
         which = i // each
         token_copy(i).start()
         if i % each == 0:
             weight_copy(which).start()
-            if arrived:
-                arrived_copy(which).start()
 
     ahead = 2
     for i in range(ahead):
@@ -54,37 +45,30 @@
         token_copy(i).wait()
         if i % each == 0:
             weight_copy(which).wait()
-            if arrived:
-                arrived_copy(which).wait()
         if i + ahead < tiles:
             fetch(i + ahead)
         rows = slice(i % each * TILE, (i % each + 1) * TILE)
         total = jnp.dot(token_buf[i], weight_buf[which], preferred_element_type=jnp.float32)
         if arrived:
-            total += arrived_buf[which, rows, :].astype(jnp.float32)
-        out_buf[which, rows, :] = total.astype(out_buf.dtype)
-        if i % each == each - 1:
-            out_copy(which).start()
-    for which in range(2):
-        out_copy(which).wait()
+            total += refs[which][rows, :].astype(jnp.float32)
+        outs[which][rows, :] = total.astype(outs[which].dtype)
 
 
 def product(tokens, kv_weight, owners, columns, arrived=(), after=()):
     rows, depth = tokens.shape
     hbm = pl.BlockSpec(memory_space=pl.ANY)
+    vmem = pl.BlockSpec(memory_space=pltpu.VMEM)
     return pl.pallas_call(
         functools.partial(product_kernel, len(arrived)),
-        in_specs=[pl.BlockSpec(memory_space=pltpu.SMEM)] + [hbm] * (2 + len(arrived) + len(after)),
-        out_specs=[hbm] * 2,
+        in_specs=[pl.BlockSpec(memory_space=pltpu.SMEM), hbm, hbm]
+        + [vmem] * len(arrived)
+        + [hbm] * len(after),
+        out_specs=[vmem] * 2,
         out_shape=[jax.ShapeDtypeStruct((rows // 2, columns), jnp.bfloat16)] * 2,
         scratch_shapes=[
             pltpu.VMEM((rows // TILE, TILE, depth), jnp.bfloat16),
             pltpu.VMEM((2, depth, columns), jnp.bfloat16),
-            pltpu.VMEM((2, rows // 2, columns), jnp.bfloat16),
-            pltpu.VMEM((2, rows // 2, columns), jnp.bfloat16),
             pltpu.SemaphoreType.DMA((rows // TILE,)),
-            pltpu.SemaphoreType.DMA((2,)),
-            pltpu.SemaphoreType.DMA((2,)),
             pltpu.SemaphoreType.DMA((2,)),
         ],
         cost_estimate=pl.CostEstimate(
@@ -108,18 +92,20 @@
         return (
             pltpu.make_async_copy(tokens_ref.at[at], token_buf.at[b], sems.at[b, 0]),
             pltpu.make_async_copy(
-                pool_ref.at[adapter_ref[b], pl.ds(0, token_buf.shape[2])],
-                factor_buf.at[b],
-                sems.at[b, 1],
+                pool_ref.at[adapter_ref[b]], factor_buf.at[b], sems.at[b, 1]
             ),
         )
 
-    for b in range(blocks):
+    ahead = 6
+    for b in range(ahead):
         for copy in copies(b):
             copy.start()
     for b in range(blocks):
         for copy in copies(b):
             copy.wait()
+        if b + ahead < blocks:
+            for copy in copies(b + ahead):
+                copy.start()
         out_ref[b * tile : (b + 1) * tile, :] = jnp.dot(
             token_buf[b], factor_buf[b], preferred_element_type=jnp.float32
         ).astype(out_ref.dtype)
@@ -150,20 +136,36 @@
     )(adapters, tokens, pools, *after)
 
 
-def turn_kernel(adapter_ref, *refs):
-    sums, pool_ref, out_ref, lift_ref, sems = refs[:4], *refs[4:]
-    height = lift_ref.shape[1]
-    first = pool_ref.shape[1] - height
+def take_kernel(adapter_ref, pool_ref, after_ref, out_ref, sems):
+    del after_ref
+
+    def copy(b):
+        return pltpu.make_async_copy(pool_ref.at[adapter_ref[b]], out_ref.at[b], sems.at[b])
+
+    for b in range(out_ref.shape[0]):
+        copy(b).start()
+    for b in range(out_ref.shape[0]):
+        copy(b).wait()
+
+
+def take(adapters, pools, after):
+    blocks = adapters.shape[0]
+    return pl.pallas_call(
+        take_kernel,
+        in_specs=[pl.BlockSpec(memory_space=pltpu.SMEM)]
+        + [pl.BlockSpec(memory_space=pl.ANY)] * 2,
+        out_specs=pl.BlockSpec(memory_space=pltpu.VMEM),
+        out_shape=jax.ShapeDtypeStruct((blocks,) + pools.shape[1:], pools.dtype),
+        scratch_shapes=[pltpu.SemaphoreType.DMA((blocks,))],
+        compiler_params=pltpu.CompilerParams(vmem_limit_bytes=60 * 2**20),
+        name="take",
+    )(adapters, pools, after)
+
+
+def turn_kernel(*refs):
+    sums, out_ref = refs[:4], refs[4]
     columns = out_ref.shape[0]
     half = out_ref.shape[1] // 2
-
-    def copy(b):
-        return pltpu.make_async_copy(
-            pool_ref.at[adapter_ref[b], pl.ds(first, height)], lift_ref.at[b], sems.at[b]
-        )
-
-    for b in range(lift_ref.shape[0]):
-        copy(b).start()
     line = lax.broadcasted_iota(jnp.int32, (columns, columns), 0)
     lane = lax.broadcasted_iota(jnp.int32, (columns, columns), 1)
     eye = jnp.where(line == lane, 1.0, 0.0).astype(jnp.bfloat16)
@@ -174,36 +176,26 @@
             out_ref[:, which * half + start : which * half + start + TILE] = lax.dot_general(
                 eye, total, NT, preferred_element_type=jnp.float32
             ).astype(out_ref.dtype)
-    for b in range(lift_ref.shape[0]):
-        copy(b).wait()
-
-
-def turn(adapters, sums, pools, height):
+
+
+def turn(sums):
     rows, columns = 2 * sums[0].shape[0], sums[0].shape[1]
-    blocks = adapters.shape[0]
     vmem = pl.BlockSpec(memory_space=pltpu.VMEM)
     return pl.pallas_call(
         turn_kernel,
-        in_specs=[pl.BlockSpec(memory_space=pltpu.SMEM)]
-        + [vmem] * 4
-        + [pl.BlockSpec(memory_space=pl.ANY)],
-        out_specs=[vmem] * 2,
-        out_shape=[
-            jax.ShapeDtypeStruct((columns, rows), jnp.bfloat16),
-            jax.ShapeDtypeStruct((blocks, height, pools.shape[2]), jnp.bfloat16),
-        ],
-        scratch_shapes=[pltpu.SemaphoreType.DMA((blocks,))],
+        in_specs=[vmem] * 4,
+        out_specs=vmem,
+        out_shape=jax.ShapeDtypeStruct((columns, rows), jnp.bfloat16),
         cost_estimate=pl.CostEstimate(
             flops=2 * rows * columns * columns, bytes_accessed=6 * rows * columns, transcendentals=0
         ),
         compiler_params=pltpu.CompilerParams(vmem_limit_bytes=VMEM),
         name="turn",
-    )(adapters, *sums, pools)
+    )(*sums)
 
 
 def finish_kernel(base_ref, shrink_ref, lift_ref, out_ref):
-    blocks, height, _ = lift_ref.shape
-    rank = height // 2
+    blocks, rank, _ = lift_ref.shape
     tile = base_ref.shape[1] // blocks
     for b in range(blocks):
         at = slice(b * tile, (b + 1) * tile)
@@ -211,7 +203,7 @@
             rows = slice(kind * HEAD, (kind + 1) * HEAD)
             ranks = slice(kind * rank, (kind + 1) * rank)
             delta = lax.dot_general(
-                lift_ref[b, ranks, :],
+                lift_ref[b, :, rows],
                 shrink_ref[at, ranks],
                 (((0,), (1,)), ((), ())),
                 preferred_element_type=jnp.float32,
@@ -291,15 +283,14 @@
 ):
     tensor = lax.axis_size("tensor")
     rows = tokens.shape[0]
-    depth = tokens.shape[1]
-    held = jnp.concatenate([a_pool, b_pool[:, :, :HEAD], b_pool[:, :, HEAD:]], axis=1)
-    pools = lax.all_gather(held, "group", tiled=True)
+    pools_a = lax.all_gather(a_pool, "group", tiled=True)
+    pools_b = lax.all_gather(b_pool, "group", tiled=True)
     adapters = block_adapters(
         a_pool.shape[0], request_entry, block_request[0], fetch_source[:, 0], fetch_slot
     )
 
     def adapted(arrived, last):
-        shrink = partial_shrink(adapters, tokens, pools, arrived)
+        shrink = partial_shrink(adapters, tokens, pools_a, arrived)
         shrink, _ = lax.optimization_barrier((shrink, last))
         shrink = lax.all_to_all(shrink, "tensor", split_axis=0, concat_axis=0, tiled=True)
         shrink = shrink.reshape(tensor, rows // tensor, shrink.shape[1]).astype(jnp.float32)
@@ -308,8 +299,8 @@
     shrink, sums = ring_sum(tokens, kv_weight, adapted)
     shrink = jnp.broadcast_to(shrink[None], (tensor,) + shrink.shape).reshape(rows, -1)
     shrink = lax.all_to_all(shrink, "tensor", split_axis=0, concat_axis=0, tiled=True)
-    base, lift = turn(adapters, sums, pools, pools.shape[1] - depth)
-    return finish(base, shrink, lift)
+    base = turn(sums)
+    return finish(base, shrink, take(adapters, pools_b, base))
 
 
 def solution(mesh):

time: 160 us -> 156 us (0.975)
  waiting for transfers between devices: 14.8 us -> 33.1 us
  Pallas kernels: 62.9 us -> 51 us
  local copies, waits for them, and re-layouts: 10.6 us -> 2.9 us
  other arithmetic: 6.25 us -> 1.2 us
  starting transfers between devices: 27.3 us -> 29.2 us
    ppermute x14, waiting for transfers between devices: 8.97 us -> 23.8 us  [hop(): lax.ppermute(value, 'tensor', [(i, (i + way) % count) for i in range(coun...]
    pallas_call x8, Pallas kernels: 49.3 us -> 40.3 us  [product(): pl.pallas_call(functools.partial(product_kernel, len(arrived)), in_specs=...]
    all_gather x1 -> x2, waiting for transfers between devices: 0.02 us -> 8.64 us  [the longest x1 8.64 us: per_device(): pools_b = lax.all_gather(b_pool, 'group', tiled=True)]
    unnamed x54 -> x26, local copies, waits for them, and re-layouts: 8.42 us -> 2.05 us
    all_to_all x1, waiting for transfers between devices: 5.79 us -> 0.01 us  [per_device(): lax.all_to_all(shrink, 'tensor', split_axis=0, concat_axis=0, tiled=True)]
    select_n x6, other arithmetic: 3.37 us -> 0.75 us  [at(): (me + jnp.array([way * shift for way in ways], jnp.int32) + count) % count]
    ppermute x14, starting transfers between devices: 23.6 us -> 25.5 us  [hop(): lax.ppermute(value, 'tensor', [(i, (i + way) % count) for i in range(coun...]
    concatenate x1 -> x0, other arithmetic: 1.89 us -> none  [per_device(): jnp.concatenate([a_pool, b_pool[:, :, :HEAD], b_pool[:, :, HEAD:]], axis=1)]
  transfers between devices with their start and end apart: 16 -> 17, of which waited for: 8 -> 13; matrix products, arithmetic and copies ran while one was open for 3% -> 1% of each run, Pallas kernels for 38% -> 32%
where the time goes in v3:
time: 156 us; the launch traced here: 153 us
  Pallas kernels  51 us (33%)
  waiting for transfers between devices  33.1 us (21%)
  starting transfers between devices  29.2 us (19%)
  blocking collectives  22.1 us (14%)
  between operations  13.7 us (9%)
  local copies, waits for them, and re-layouts  2.9 us (2%)
    pallas_call x8, Pallas kernels, product(): pl.pallas_call(functools.partial(product_kernel, len(arrived)), in_specs=...  40.3 us
    ppermute x14, starting transfers between devices, hop(): lax.ppermute(value, 'tensor', [(i, (i + way) % count) for i in range(coun...  25.5 us
    ppermute x14, waiting for transfers between devices, hop(): lax.ppermute(value, 'tensor', [(i, (i + way) % count) for i in range(coun...  23.8 us
    all_to_all x1, blocking collectives, adapted(): lax.all_to_all(shrink, 'tensor', split_axis=0, concat_axis=0, tiled=True)  22.1 us
    all_gather x1, waiting for transfers between devices, per_device(): pools_b = lax.all_gather(b_pool, 'group', tiled=True)  8.64 us
    pallas_call x1, Pallas kernels, partial_shrink(): pl.pallas_call(shrink_kernel, in_specs=[pl.BlockSpec(memory_space=pltpu.S...  5.49 us
    all_to_all x1, starting transfers between devices, per_device(): lax.all_to_all(shrink, 'tensor', split_axis=0, concat_axis=0, tiled=True)  3.71 us
  transfers between devices with their start and end apart: 17, of which 13 were waited for; matrix products, arithmetic and copies ran while one was open for 1% of the time, Pallas kernels for 32%

profile of v3, /device:TPU:24, one launch (start us, length us, event | category | flops | bytes accessed | tf_op | source)
XLA Modules:
  0.0 153.3 jit_solution(11391970129085964681)
XLA Ops:
  8.0 5.6 %product.8 = (bf16[1024,256]{1,0:T(8,128)(2,1)S(1)}, bf16[1024,256]{1,0:T(8,128)(2,1)}) custom-call(s32[2]{0:T(128)S(1)} %get-tuple-element.40.owner_ref, bf16[2048,1024]{1,0:T(8,128)(2,1)} %tokens_ref.17, bf16[1024,2048]{1,0:T(8,128)(2,1)} %weight_ref.15), custom_call_target="tpu_custom_call" | custom-call | flops 1073741824 | bytes 6291456 | tf_op jit(solution)/shard_map/product/pallas_call | solution.py:61
  15.6 4.0 %collective-permute-start.1 = (bf16[1024,256]{1,0:T(8,128)(2,1)}, bf16[1024,256]{1,0:T(8,128)(2,1)S(1)}, u32[]{:S(2)}, u32[]{:S(2)}) collective-permute-start(bf16[1024,256]{1,0:T(8,128)(2,1)} %get-tuple-element.23), channel_id=1, source_target_pairs={{0,7},{1,0},{2,1},{3,2},{4,3},{5,4},{6,5},{7,6},{8,15},{9,8},{10,9... | collective-permute-start | bytes 1572872 | tf_op jit(solution)/shard_map/ppermute | solution.py:248
  19.6 5.6 %product.9 = (bf16[1024,256]{1,0:T(8,128)(2,1)S(1)}, bf16[1024,256]{1,0:T(8,128)(2,1)}) custom-call(s32[2]{0:T(128)S(1)} %get-tuple-element.39.owner_ref, bf16[2048,1024]{1,0:T(8,128)(2,1)} %tokens_ref.17, bf16[1024,2048]{1,0:T(8,128)(2,1)} %weight_ref.15, bf16[1024,256]{1,0:T(8,128)(2,1)S(1)} %get-tuple-element.22.refs_0_), custom_call_target="tpu_custom_call" | custom-call | flops 1073741824 | bytes 6291456 | tf_op jit(solution)/shard_map/product/pallas_call | solution.py:61
  27.6 4.6 %collective-permute-done.refs_0_ = bf16[1024,256]{1,0:T(8,128)(2,1)S(1)} collective-permute-done((bf16[1024,256]{1,0:T(8,128)(2,1)S(1)}, bf16[1024,256]{1,0:T(8,128)(2,1)S(1)}, u32[]{:S(2)}, u32[]{:S(2)}) %collective-permute-start) | collective-permute-done | bytes 524320 | tf_op jit(solution)/shard_map/ppermute | solution.py:248
  32.2 4.8 %product.10 = (bf16[1024,256]{1,0:T(8,128)(2,1)S(1)}, bf16[1024,256]{1,0:T(8,128)(2,1)S(1)}) custom-call(s32[2]{0:T(128)S(1)} %and_select_fusion.4.owner_ref, bf16[2048,1024]{1,0:T(8,128)(2,1)} %tokens_ref.17, bf16[1024,2048]{1,0:T(8,128)(2,1)} %weight_ref.15, bf16[1024,256]{1,0:T(8,128)(2,1)S(1)} %collective-permute-done.refs_0_, ...), custom_call_target="tpu_custom_call" | custom-call | flops 1073741824 | bytes 6291456 | tf_op jit(solution)/shard_map/product/pallas_call | solution.py:61
  37.4 3.4 %collective-permute-start.3 = (bf16[1024,256]{1,0:T(8,128)(2,1)S(1)}, bf16[1024,256]{1,0:T(8,128)(2,1)S(1)}, u32[]{:S(2)}, u32[]{:S(2)}) collective-permute-start(bf16[1024,256]{1,0:T(8,128)(2,1)S(1)} %get-tuple-element.26), channel_id=1, source_target_pairs={{0,7},{1,0},{2,1},{3,2},{4,3},{5,4},{6,5},{7,6},{8,15},{9,8},{10,9... | collective-permute-start | bytes 1572872 | tf_op jit(solution)/shard_map/ppermute | solution.py:248
  40.8 2.5 %collective-permute-done.4.refs_0_ = bf16[1024,256]{1,0:T(8,128)(2,1)S(1)} collective-permute-done((bf16[1024,256]{1,0:T(8,128)(2,1)S(1)}, bf16[1024,256]{1,0:T(8,128)(2,1)S(1)}, u32[]{:S(2)}, u32[]{:S(2)}) %collective-permute-start.4) | collective-permute-done | bytes 524320 | tf_op jit(solution)/shard_map/ppermute | solution.py:248
  43.5 4.8 %product.11 = (bf16[1024,256]{1,0:T(8,128)(2,1)S(1)}, bf16[1024,256]{1,0:T(8,128)(2,1)S(1)}) custom-call(s32[2]{0:T(128)S(1)} %and_select_fusion.1.owner_ref, bf16[2048,1024]{1,0:T(8,128)(2,1)} %tokens_ref.17, bf16[1024,2048]{1,0:T(8,128)(2,1)} %weight_ref.15, bf16[1024,256]{1,0:T(8,128)(2,1)S(1)} %collective-permute-done.4.refs_0_, ...), custom_call_target="tpu_custom_call" | custom-call | flops 1073741824 | bytes 6291456 | tf_op jit(solution)/shard_map/product/pallas_call | solution.py:61
  48.3 3.6 %collective-permute-start.8 = (bf16[1024,256]{1,0:T(8,128)(2,1)S(1)}, bf16[1024,256]{1,0:T(8,128)(2,1)S(1)}, u32[]{:S(2)}, u32[]{:S(2)}) collective-permute-start(bf16[1024,256]{1,0:T(8,128)(2,1)S(1)} %get-tuple-element.28.refs_2_), channel_id=1, source_target_pairs={{0,7},{1,0},{2,1},{3,2},{4,3},{5,4},{6,5},{7,6},{8,15},{9,8},{10,9... | collective-permute-start | bytes 1572872 | tf_op jit(solution)/shard_map/ppermute | solution.py:248
  51.9 2.5 %collective-permute-done.2.refs_0_ = bf16[1024,256]{1,0:T(8,128)(2,1)S(1)} collective-permute-done((bf16[1024,256]{1,0:T(8,128)(2,1)S(1)}, bf16[1024,256]{1,0:T(8,128)(2,1)S(1)}, u32[]{:S(2)}, u32[]{:S(2)}) %collective-permute-start.2) | collective-permute-done | bytes 524320 | tf_op jit(solution)/shard_map/ppermute | solution.py:248
  54.6 4.8 %product.12 = (bf16[1024,256]{1,0:T(8,128)(2,1)S(1)}, bf16[1024,256]{1,0:T(8,128)(2,1)S(1)}) custom-call(s32[2]{0:T(128)S(1)} %and_select_fusion.5.owner_ref, bf16[2048,1024]{1,0:T(8,128)(2,1)} %tokens_ref.17, bf16[1024,2048]{1,0:T(8,128)(2,1)} %weight_ref.15, bf16[1024,256]{1,0:T(8,128)(2,1)S(1)} %collective-permute-done.2.refs_0_, ...), custom_call_target="tpu_custom_call" | custom-call | flops 1073741824 | bytes 6291456 | tf_op jit(solution)/shard_map/product/pallas_call | solution.py:61
  63.4 2.4 %collective-permute-done.8.refs_0_ = bf16[1024,256]{1,0:T(8,128)(2,1)S(1)} collective-permute-done((bf16[1024,256]{1,0:T(8,128)(2,1)S(1)}, bf16[1024,256]{1,0:T(8,128)(2,1)S(1)}, u32[]{:S(2)}, u32[]{:S(2)}) %collective-permute-start.8) | collective-permute-done | bytes 524320 | tf_op jit(solution)/shard_map/ppermute | solution.py:248
  65.8 2.2 %collective-permute-done.9.refs_1_ = bf16[1024,256]{1,0:T(8,128)(2,1)S(1)} collective-permute-done((bf16[1024,256]{1,0:T(8,128)(2,1)S(1)}, bf16[1024,256]{1,0:T(8,128)(2,1)S(1)}, u32[]{:S(2)}, u32[]{:S(2)}) %collective-permute-start.9) | collective-permute-done | bytes 524320 | tf_op jit(solution)/shard_map/ppermute | solution.py:248
  68.0 4.9 %product.13 = (bf16[1024,256]{1,0:T(8,128)(2,1)S(1)}, bf16[1024,256]{1,0:T(8,128)(2,1)S(1)}) custom-call(s32[2]{0:T(128)S(1)} %and_select_fusion.owner_ref, bf16[2048,1024]{1,0:T(8,128)(2,1)} %tokens_ref.17, bf16[1024,2048]{1,0:T(8,128)(2,1)} %weight_ref.15, bf16[1024,256]{1,0:T(8,128)(2,1)S(1)} %collective-permute-done.8.refs_0_, ...), custom_call_target="tpu_custom_call" | custom-call | flops 1073741824 | bytes 6291456 | tf_op jit(solution)/shard_map/product/pallas_call | solution.py:61
  77.1 4.9 %product.14 = (bf16[1024,256]{1,0:T(8,128)(2,1)}, bf16[1024,256]{1,0:T(8,128)(2,1)S(1)}) custom-call(s32[2]{0:T(128)S(1)} %and_select_fusion.6.owner_ref, bf16[2048,1024]{1,0:T(8,128)(2,1)} %tokens_ref.17, bf16[1024,2048]{1,0:T(8,128)(2,1)} %weight_ref.15, bf16[1024,256]{1,0:T(8,128)(2,1)S(1)} %collective-permute-done.6.refs_0_, ...), custom_call_target="tpu_custom_call" | custom-call | flops 1073741824 | bytes 6291456 | tf_op jit(solution)/shard_map/product/pallas_call | solution.py:61
  82.0 2.2 %collective-permute-start.10 = (bf16[1024,256]{1,0:T(8,128)(2,1)}, bf16[1024,256]{1,0:T(8,128)(2,1)S(1)}, u32[]{:S(2)}, u32[]{:S(2)}) collective-permute-start(bf16[1024,256]{1,0:T(8,128)(2,1)} %get-tuple-element.33), channel_id=1, source_target_pairs={{0,1},{1,2},{2,3},{3,4},{4,5},{5,6},{6,7},{7,0},{8,9},{9,10},{10,1... | collective-permute-start | bytes 1572872 | tf_op jit(solution)/shard_map/ppermute | solution.py:248
  86.1 2.2 %collective-permute-done.11.first_ref.refs_0_ = bf16[1024,256]{1,0:T(8,128)(2,1)S(1)} collective-permute-done((bf16[1024,256]{1,0:T(8,128)(2,1)S(1)}, bf16[1024,256]{1,0:T(8,128)(2,1)S(1)}, u32[]{:S(2)}, u32[]{:S(2)}) %collective-permute-start.11) | collective-permute-done | bytes 524320 | tf_op jit(solution)/shard_map/ppermute | solution.py:248
  90.4 5.5 %partial_shrink.1 = bf16[2048,128]{1,0:T(8,128)(2,1)S(1)} custom-call(s32[16]{0:T(128)S(1)} %compare_select_fusion.14.adapter_ref, bf16[2048,1024]{1,0:T(8,128)(2,1)} %tokens_ref.17, bf16[64,1024,128]{2,1,0:T(8,128)(2,1)} %all-gather.3.cloned.1.call-done.pool_ref, bf16[1024,256]{1,0:T(8,128)(2,1)S(1)} %collective-permute-done.11.first_ref.refs_0_, ...), custom_call_target="tpu_custom_call" | custom-call | flops 536870912 | bytes 8388608 | tf_op jit(solution)/shard_map/partial_shrink/pallas_call | solution.py:118
  95.9 3.0 %collective-permute-done.10.refs_0_ = bf16[1024,256]{1,0:T(8,128)(2,1)S(1)} collective-permute-done((bf16[1024,256]{1,0:T(8,128)(2,1)}, bf16[1024,256]{1,0:T(8,128)(2,1)S(1)}, u32[]{:S(2)}, u32[]{:S(2)}) %collective-permute-start.10) | collective-permute-done | bytes 524320 | tf_op jit(solution)/shard_map/ppermute | solution.py:248
  98.8 22.1 %all_to_all.17 = bf16[8,256,128]{2,1,0:T(8,128)(2,1)S(1)} all-to-all(bf16[8,256,128]{2,1,0:T(8,128)(2,1)S(1)} %bitcast.5), channel_id=1, replica_groups=mesh['group'=32,'tensor'=8] {'tensor'}, dimensions={0} | all-to-all | bytes 1048576 | tf_op jit(solution)/shard_map/all_to_all | solution.py:295
  121.9 3.7 %all-to-all-start.1 = ((bf16[8,256,128]{2,1,0:T(8,128)(2,1)}), bf16[8,256,128]{2,1,0:T(8,128)(2,1)S(1)}, u32[]{:S(2)}, u32[]{:S(2)}) async-start(bf16[8,256,128]{2,1,0:T(8,128)(2,1)} %broadcast_in_dim.39), calls=%async_computation.1 | async-start | bytes 1048576 | tf_op jit(solution)/shard_map/all_to_all | solution.py:301
  125.6 4.9 %product.15 = (bf16[1024,256]{1,0:T(8,128)(2,1)S(1)}, bf16[1024,256]{1,0:T(8,128)(2,1)S(1)}) custom-call(s32[2]{0:T(128)S(1)} %broadcast.99.owner_ref, bf16[2048,1024]{1,0:T(8,128)(2,1)} %tokens_ref.17, bf16[1024,2048]{1,0:T(8,128)(2,1)} %weight_ref.15, bf16[1024,256]{1,0:T(8,128)(2,1)S(1)} %collective-permute-done.11.first_ref.refs_0_, ...), custom_call_target="tpu_custom_call" | custom-call | flops 1073741824 | bytes 6291456 | tf_op jit(solution)/shard_map/product/pallas_call | solution.py:61
  132.0 8.6 %all-gather.5.cloned.1.call-done.pool_ref = bf16[64,64,256]{2,1,0:T(8,128)(2,1)} async-done(((bf16[2,64,256]{2,1,0:T(8,128)(2,1)}), bf16[64,64,256]{2,1,0:T(8,128)(2,1)}) %all-gather.5.cloned.1.call-update) | async-done | bytes 2097168 | tf_op jit(solution)/shard_map/all_gather | solution.py:287
  140.6 2.7 %take.1.lift_ref = bf16[16,64,256]{2,1,0:T(8,128)(2,1)} custom-call(s32[16]{0:T(128)} %copy-done.3, bf16[64,64,256]{2,1,0:T(8,128)(2,1)} %all-gather.5.cloned.1.call-done.pool_ref, bf16[256,2048]{1,0:T(8,128)(2,1)} %copy-done), custom_call_target="tpu_custom_call" | custom-call | tf_op jit(solution)/shard_map/take/pallas_call | solution.py:153
  (65 shorter events, 23.9 us)
Async XLA Ops:
  6.5 83.8 %all-gather.3.cloned.1.call-start = ((), (), s32[]{:S(2)}) async-start(), calls=%async_computation.2 | async-start | bytes 17301504 | tf_op jit(solution)/shard_map/all_gather | solution.py:286
  7.3 133.4 %all-gather.5.cloned.1.call-start = ((), (), s32[]{:S(2)}) async-start(), calls=%async_computation.3 | async-start | bytes 2162688 | tf_op jit(solution)/shard_map/all_gather | solution.py:287
  13.6 18.7 %collective-permute-start = (bf16[1024,256]{1,0:T(8,128)(2,1)S(1)}, bf16[1024,256]{1,0:T(8,128)(2,1)S(1)}, u32[]{:S(2)}, u32[]{:S(2)}) collective-permute-start(bf16[1024,256]{1,0:T(8,128)(2,1)S(1)} %get-tuple-element.22.refs_0_), channel_id=1, source_target_pairs={{0,1},{1,2},{2,3},{3,4},{4,5},{5,6},{6,7},{7,0},{8,9},{9,10},{10,1... | collective-permute-start | bytes 1572872 | tf_op jit(solution)/shard_map/ppermute | solution.py:248
  15.6 16.7 %collective-permute-start.1 = (bf16[1024,256]{1,0:T(8,128)(2,1)}, bf16[1024,256]{1,0:T(8,128)(2,1)S(1)}, u32[]{:S(2)}, u32[]{:S(2)}) collective-permute-start(bf16[1024,256]{1,0:T(8,128)(2,1)} %get-tuple-element.23), channel_id=1, source_target_pairs={{0,7},{1,0},{2,1},{3,2},{4,3},{5,4},{6,5},{7,6},{8,15},{9,8},{10,9... | collective-permute-start | bytes 1572872 | tf_op jit(solution)/shard_map/ppermute | solution.py:248
  19.6 8.0 %copy-start.11 = (s32[2]{0:T(128)S(1)}, s32[2]{0:T(128)}, u32[]{:S(2)}) copy-start(s32[2]{0:T(128)} %constant.90.clone) | copy-start | bytes 28
  25.2 18.2 %collective-permute-start.4 = (bf16[1024,256]{1,0:T(8,128)(2,1)S(1)}, bf16[1024,256]{1,0:T(8,128)(2,1)S(1)}, u32[]{:S(2)}, u32[]{:S(2)}) collective-permute-start(bf16[1024,256]{1,0:T(8,128)(2,1)S(1)} %get-tuple-element.24.refs_2_), channel_id=1, source_target_pairs={{0,7},{1,0},{2,1},{3,2},{4,3},{5,4},{6,5},{7,6},{8,15},{9,8},{10,9... | collective-permute-start | bytes 1572872 | tf_op jit(solution)/shard_map/ppermute | solution.py:248
  27.2 16.3 %collective-permute-start.5 = (bf16[1024,256]{1,0:T(8,128)(2,1)}, bf16[1024,256]{1,0:T(8,128)(2,1)S(1)}, u32[]{:S(2)}, u32[]{:S(2)}) collective-permute-start(bf16[1024,256]{1,0:T(8,128)(2,1)} %get-tuple-element.27), channel_id=1, source_target_pairs={{0,1},{1,2},{2,3},{3,4},{4,5},{5,6},{6,7},{7,0},{8,9},{9,10},{10,1... | collective-permute-start | bytes 1572872 | tf_op jit(solution)/shard_map/ppermute | solution.py:248
  27.6 13.2 %copy-start.10 = (s32[2]{0:T(128)S(1)}, s32[2]{0:T(128)}, u32[]{:S(2)}) copy-start(s32[2]{0:T(128)} %constant.92.clone) | copy-start | bytes 28
  27.6 13.2 %copy-start.9 = (s32[2]{0:T(128)S(1)}, s32[2]{0:T(128)}, u32[]{:S(2)}) copy-start(s32[2]{0:T(128)} %constant.91.clone) | copy-start | bytes 28
  37.1 17.4 %collective-permute-start.2 = (bf16[1024,256]{1,0:T(8,128)(2,1)S(1)}, bf16[1024,256]{1,0:T(8,128)(2,1)S(1)}, u32[]{:S(2)}, u32[]{:S(2)}) collective-permute-start(bf16[1024,256]{1,0:T(8,128)(2,1)S(1)} %get-tuple-element.25.refs_2_), channel_id=1, source_target_pairs={{0,1},{1,2},{2,3},{3,4},{4,5},{5,6},{6,7},{7,0},{8,9},{9,10},{10,1... | collective-permute-start | bytes 1572872 | tf_op jit(solution)/shard_map/ppermute | solution.py:248
  37.4 17.2 %collective-permute-start.3 = (bf16[1024,256]{1,0:T(8,128)(2,1)S(1)}, bf16[1024,256]{1,0:T(8,128)(2,1)S(1)}, u32[]{:S(2)}, u32[]{:S(2)}) collective-permute-start(bf16[1024,256]{1,0:T(8,128)(2,1)S(1)} %get-tuple-element.26), channel_id=1, source_target_pairs={{0,7},{1,0},{2,1},{3,2},{4,3},{5,4},{6,5},{7,6},{8,15},{9,8},{10,9... | collective-permute-start | bytes 1572872 | tf_op jit(solution)/shard_map/ppermute | solution.py:248
  48.3 17.6 %collective-permute-start.8 = (bf16[1024,256]{1,0:T(8,128)(2,1)S(1)}, bf16[1024,256]{1,0:T(8,128)(2,1)S(1)}, u32[]{:S(2)}, u32[]{:S(2)}) collective-permute-start(bf16[1024,256]{1,0:T(8,128)(2,1)S(1)} %get-tuple-element.28.refs_2_), channel_id=1, source_target_pairs={{0,7},{1,0},{2,1},{3,2},{4,3},{5,4},{6,5},{7,6},{8,15},{9,8},{10,9... | collective-permute-start | bytes 1572872 | tf_op jit(solution)/shard_map/ppermute | solution.py:248
  51.9 11.4 %copy-start.8 = (s32[2]{0:T(128)S(1)}, s32[2]{0:T(128)}, u32[]{:S(2)}) copy-start(s32[2]{0:T(128)} %constant.93.clone) | copy-start | bytes 28
  51.9 11.5 %copy-start.6 = (s32[13]{0:T(128)S(1)}, s32[13]{0:T(128)}, u32[]{:S(2)}) copy-start(s32[13]{0:T(128)} %param.23) | copy-start | bytes 160
  51.9 11.5 %copy-start.7 = (s32[13,1]{0,1:T(1,128)S(1)}, s32[13,1]{0,1:T(1,128)}, u32[]{:S(2)}) copy-start(s32[13,1]{0,1:T(1,128)} %param.22) | copy-start | bytes 160
  51.9 16.1 %collective-permute-start.9 = (bf16[1024,256]{1,0:T(8,128)(2,1)S(1)}, bf16[1024,256]{1,0:T(8,128)(2,1)S(1)}, u32[]{:S(2)}, u32[]{:S(2)}) collective-permute-start(bf16[1024,256]{1,0:T(8,128)(2,1)S(1)} %get-tuple-element.31), channel_id=1, source_target_pairs={{0,1},{1,2},{2,3},{3,4},{4,5},{5,6},{6,7},{7,0},{8,9},{9,10},{10,1... | collective-permute-start | bytes 1572872 | tf_op jit(solution)/shard_map/ppermute | solution.py:248
  59.4 17.4 %collective-permute-start.6 = (bf16[1024,256]{1,0:T(8,128)(2,1)S(1)}, bf16[1024,256]{1,0:T(8,128)(2,1)S(1)}, u32[]{:S(2)}, u32[]{:S(2)}) collective-permute-start(bf16[1024,256]{1,0:T(8,128)(2,1)S(1)} %get-tuple-element.29.refs_2_), channel_id=1, source_target_pairs={{0,1},{1,2},{2,3},{3,4},{4,5},{5,6},{6,7},{7,0},{8,9},{9,10},{10,1... | collective-permute-start | bytes 1572872 | tf_op jit(solution)/shard_map/ppermute | solution.py:248
  61.5 15.5 %collective-permute-start.7 = (bf16[1024,256]{1,0:T(8,128)(2,1)S(1)}, bf16[1024,256]{1,0:T(8,128)(2,1)S(1)}, u32[]{:S(2)}, u32[]{:S(2)}) collective-permute-start(bf16[1024,256]{1,0:T(8,128)(2,1)S(1)} %get-tuple-element.30), channel_id=1, source_target_pairs={{0,7},{1,0},{2,1},{3,2},{4,3},{5,4},{6,5},{7,6},{8,15},{9,8},{10,9... | collective-permute-start | bytes 1572872 | tf_op jit(solution)/shard_map/ppermute | solution.py:248
  72.9 15.4 %collective-permute-start.11 = (bf16[1024,256]{1,0:T(8,128)(2,1)S(1)}, bf16[1024,256]{1,0:T(8,128)(2,1)S(1)}, u32[]{:S(2)}, u32[]{:S(2)}) collective-permute-start(bf16[1024,256]{1,0:T(8,128)(2,1)S(1)} %get-tuple-element.32.refs_2_), channel_id=1, source_target_pairs={{0,7},{1,0},{2,1},{3,2},{4,3},{5,4},{6,5},{7,6},{8,15},{9,8},{10,9... | collective-permute-start | bytes 1572872 | tf_op jit(solution)/shard_map/ppermute | solution.py:248
  74.5 15.8 %collective-permute-start.12 = (bf16[1024,256]{1,0:T(8,128)(2,1)S(1)}, bf16[1024,256]{1,0:T(8,128)(2,1)S(1)}, u32[]{:S(2)}, u32[]{:S(2)}) collective-permute-start(bf16[1024,256]{1,0:T(8,128)(2,1)S(1)} %get-tuple-element.34), channel_id=1, source_target_pairs={{0,1},{1,2},{2,3},{3,4},{4,5},{5,6},{6,7},{7,0},{8,9},{9,10},{10,1... | collective-permute-start | bytes 1572872 | tf_op jit(solution)/shard_map/ppermute | solution.py:248
  82.0 16.8 %collective-permute-start.10 = (bf16[1024,256]{1,0:T(8,128)(2,1)}, bf16[1024,256]{1,0:T(8,128)(2,1)S(1)}, u32[]{:S(2)}, u32[]{:S(2)}) collective-permute-start(bf16[1024,256]{1,0:T(8,128)(2,1)} %get-tuple-element.33), channel_id=1, source_target_pairs={{0,1},{1,2},{2,3},{3,4},{4,5},{5,6},{6,7},{7,0},{8,9},{9,10},{10,1... | collective-permute-start | bytes 1572872 | tf_op jit(solution)/shard_map/ppermute | solution.py:248
  84.2 14.6 %collective-permute-start.13 = (bf16[1024,256]{1,0:T(8,128)(2,1)S(1)}, bf16[1024,256]{1,0:T(8,128)(2,1)S(1)}, u32[]{:S(2)}, u32[]{:S(2)}) collective-permute-start(bf16[1024,256]{1,0:T(8,128)(2,1)S(1)} %get-tuple-element.35), channel_id=1, source_target_pairs={{0,7},{1,0},{2,1},{3,2},{4,3},{5,4},{6,5},{7,6},{8,15},{9,8},{10,9... | collective-permute-start | bytes 1572872 | tf_op jit(solution)/shard_map/ppermute | solution.py:248
  86.1 9.7 %copy-start.3 = (s32[16]{0:T(128)}, s32[16]{0:T(128)S(1)}, u32[]{:S(2)}) copy-start(s32[16]{0:T(128)S(1)} %compare_select_fusion.14.adapter_ref) | copy-start | bytes 196
  121.9 21.5 %all-to-all-start.1 = ((bf16[8,256,128]{2,1,0:T(8,128)(2,1)}), bf16[8,256,128]{2,1,0:T(8,128)(2,1)S(1)}, u32[]{:S(2)}, u32[]{:S(2)}) async-start(bf16[8,256,128]{2,1,0:T(8,128)(2,1)} %broadcast_in_dim.39), calls=%async_computation.1 | async-start | bytes 1048576 | tf_op jit(solution)/shard_map/all_to_all | solution.py:301
  (6 other events, 28.2 us)
Sparse Core Ops, SparseCore 0:
  9.9 79.7 all-gather.2
  92.3 48.3 all-gather.4

commit v4 on v3

--- a/solution.py
+++ b/solution.py
@@ -136,32 +136,6 @@
     )(adapters, tokens, pools, *after)
 
 
-def take_kernel(adapter_ref, pool_ref, after_ref, out_ref, sems):
-    del after_ref
-
-    def copy(b):
-        return pltpu.make_async_copy(pool_ref.at[adapter_ref[b]], out_ref.at[b], sems.at[b])
-
-    for b in range(out_ref.shape[0]):
-        copy(b).start()
-    for b in range(out_ref.shape[0]):
-        copy(b).wait()
-
-
-def take(adapters, pools, after):
-    blocks = adapters.shape[0]
-    return pl.pallas_call(
-        take_kernel,
-        in_specs=[pl.BlockSpec(memory_space=pltpu.SMEM)]
-        + [pl.BlockSpec(memory_space=pl.ANY)] * 2,
-        out_specs=pl.BlockSpec(memory_space=pltpu.VMEM),
-        out_shape=jax.ShapeDtypeStruct((blocks,) + pools.shape[1:], pools.dtype),
-        scratch_shapes=[pltpu.SemaphoreType.DMA((blocks,))],
-        compiler_params=pltpu.CompilerParams(vmem_limit_bytes=60 * 2**20),
-        name="take",
-    )(adapters, pools, after)
-
-
 def turn_kernel(*refs):
     sums, out_ref = refs[:4], refs[4]
     columns = out_ref.shape[0]
@@ -194,16 +168,19 @@
     )(*sums)
 
 
-def finish_kernel(base_ref, shrink_ref, lift_ref, out_ref):
-    blocks, rank, _ = lift_ref.shape
-    tile = base_ref.shape[1] // blocks
-    for b in range(blocks):
+def finish_kernel(adapter_ref, base_ref, shrink_ref, pool_ref, out_ref):
+    step = pl.program_id(0)
+    tile = shrink_ref.shape[0] * pl.num_programs(0) // adapter_ref.shape[0]
+    here = shrink_ref.shape[0] // tile
+    rank = pool_ref.shape[1]
+    for b in range(here):
+        adapter = adapter_ref[step * here + b]
         at = slice(b * tile, (b + 1) * tile)
         for kind in range(2):
             rows = slice(kind * HEAD, (kind + 1) * HEAD)
             ranks = slice(kind * rank, (kind + 1) * rank)
             delta = lax.dot_general(
-                lift_ref[b, :, rows],
+                pool_ref[adapter, :, rows],
                 shrink_ref[at, ranks],
                 (((0,), (1,)), ((), ())),
                 preferred_element_type=jnp.float32,
@@ -213,26 +190,29 @@
             )
 
 
-def finish(base, shrink, lift):
+def finish(adapters, base, shrink, pools):
     columns, rows = base.shape
     steps = 2
-    step, lifts = rows // steps, lift.shape[0] // steps
+    step = rows // steps
     return pl.pallas_call(
         finish_kernel,
-        grid=(steps,),
-        in_specs=[
-            pl.BlockSpec((columns, step), lambda i: (0, i)),
-            pl.BlockSpec((step, shrink.shape[1]), lambda i: (i, 0)),
-            pl.BlockSpec((lifts,) + lift.shape[1:], lambda i: (i, 0, 0)),
-        ],
-        out_specs=pl.BlockSpec((columns, step), lambda i: (0, i)),
+        grid_spec=pltpu.PrefetchScalarGridSpec(
+            num_scalar_prefetch=1,
+            grid=(steps,),
+            in_specs=[
+                pl.BlockSpec((columns, step), lambda i, adapter: (0, i)),
+                pl.BlockSpec((step, shrink.shape[1]), lambda i, adapter: (i, 0)),
+                pl.BlockSpec(memory_space=pltpu.VMEM),
+            ],
+            out_specs=pl.BlockSpec((columns, step), lambda i, adapter: (0, i)),
+        ),
         out_shape=jax.ShapeDtypeStruct((columns, rows), jnp.bfloat16),
         cost_estimate=pl.CostEstimate(
             flops=2 * rows * columns * HEAD, bytes_accessed=6 * rows * columns, transcendentals=0
         ),
-        compiler_params=pltpu.CompilerParams(vmem_limit_bytes=VMEM),
+        compiler_params=pltpu.CompilerParams(vmem_limit_bytes=24 * 2**20),
         name="finish",
-    )(base, shrink, lift)
+    )(adapters, base, shrink, pools)
 
 
 def add(*terms):
@@ -299,8 +279,7 @@
     shrink, sums = ring_sum(tokens, kv_weight, adapted)
     shrink = jnp.broadcast_to(shrink[None], (tensor,) + shrink.shape).reshape(rows, -1)
     shrink = lax.all_to_all(shrink, "tensor", split_axis=0, concat_axis=0, tiled=True)
-    base = turn(sums)
-    return finish(base, shrink, take(adapters, pools_b, base))
+    return finish(adapters, turn(sums), shrink, pools_b)
 
 
 def solution(mesh):

time: 156 us -> 154 us (0.987)
  Pallas kernels: 51 us -> 49 us
    pallas_call x2 -> x1, Pallas kernels: 4.71 us -> 2.52 us  [finish(): pl.pallas_call(finish_kernel, grid_spec=pltpu.PrefetchScalarGridSpec(num_...]
  transfers between devices with their start and end apart: 17 -> 17, of which waited for: 13 -> 13; matrix products, arithmetic and copies ran while one was open for 1% -> 1% of each run, Pallas kernels for 32% -> 31%
where the time goes in v4:
time: 154 us; the launch traced here: 152 us
  Pallas kernels  49 us (32%)
  waiting for transfers between devices  33.9 us (22%)
  starting transfers between devices  29.2 us (19%)
  blocking collectives  22.1 us (14%)
  between operations  13.6 us (9%)
  local copies, waits for them, and re-layouts  2.5 us (2%)
    pallas_call x8, Pallas kernels, product(): pl.pallas_call(functools.partial(product_kernel, len(arrived)), in_specs=...  40.3 us
    ppermute x14, starting transfers between devices, hop(): lax.ppermute(value, 'tensor', [(i, (i + way) % count) for i in range(coun...  25.5 us
    ppermute x14, waiting for transfers between devices, hop(): lax.ppermute(value, 'tensor', [(i, (i + way) % count) for i in range(coun...  23.6 us
    all_to_all x1, blocking collectives, adapted(): lax.all_to_all(shrink, 'tensor', split_axis=0, concat_axis=0, tiled=True)  22.1 us
    all_gather x1, waiting for transfers between devices, per_device(): pools_b = lax.all_gather(b_pool, 'group', tiled=True)  9.59 us
    pallas_call x1, Pallas kernels, partial_shrink(): pl.pallas_call(shrink_kernel, in_specs=[pl.BlockSpec(memory_space=pltpu.S...  5.74 us
    all_to_all x1, starting transfers between devices, per_device(): lax.all_to_all(shrink, 'tensor', split_axis=0, concat_axis=0, tiled=True)  3.71 us
  transfers between devices with their start and end apart: 17, of which 13 were waited for; matrix products, arithmetic and copies ran while one was open for 1% of the time, Pallas kernels for 31%

profile of v4, /device:TPU:24, one launch (start us, length us, event | category | flops | bytes accessed | tf_op | source)
XLA Modules:
  0.0 151.6 jit_solution(13269644855744806410)
XLA Ops:
  8.0 5.6 %product.8 = (bf16[1024,256]{1,0:T(8,128)(2,1)S(1)}, bf16[1024,256]{1,0:T(8,128)(2,1)}) custom-call(s32[2]{0:T(128)S(1)} %get-tuple-element.40.owner_ref, bf16[2048,1024]{1,0:T(8,128)(2,1)} %tokens_ref.17, bf16[1024,2048]{1,0:T(8,128)(2,1)} %weight_ref.15), custom_call_target="tpu_custom_call" | custom-call | flops 1073741824 | bytes 6291456 | tf_op jit(solution)/shard_map/product/pallas_call | solution.py:61
  15.6 4.0 %collective-permute-start.1 = (bf16[1024,256]{1,0:T(8,128)(2,1)}, bf16[1024,256]{1,0:T(8,128)(2,1)S(1)}, u32[]{:S(2)}, u32[]{:S(2)}) collective-permute-start(bf16[1024,256]{1,0:T(8,128)(2,1)} %get-tuple-element.23), channel_id=1, source_target_pairs={{0,7},{1,0},{2,1},{3,2},{4,3},{5,4},{6,5},{7,6},{8,15},{9,8},{10,9... | collective-permute-start | bytes 1572872 | tf_op jit(solution)/shard_map/ppermute | solution.py:228
  19.6 5.6 %product.9 = (bf16[1024,256]{1,0:T(8,128)(2,1)S(1)}, bf16[1024,256]{1,0:T(8,128)(2,1)}) custom-call(s32[2]{0:T(128)S(1)} %get-tuple-element.39.owner_ref, bf16[2048,1024]{1,0:T(8,128)(2,1)} %tokens_ref.17, bf16[1024,2048]{1,0:T(8,128)(2,1)} %weight_ref.15, bf16[1024,256]{1,0:T(8,128)(2,1)S(1)} %get-tuple-element.22.refs_0_), custom_call_target="tpu_custom_call" | custom-call | flops 1073741824 | bytes 6291456 | tf_op jit(solution)/shard_map/product/pallas_call | solution.py:61
  27.6 4.7 %collective-permute-done.refs_0_ = bf16[1024,256]{1,0:T(8,128)(2,1)S(1)} collective-permute-done((bf16[1024,256]{1,0:T(8,128)(2,1)S(1)}, bf16[1024,256]{1,0:T(8,128)(2,1)S(1)}, u32[]{:S(2)}, u32[]{:S(2)}) %collective-permute-start) | collective-permute-done | bytes 524320 | tf_op jit(solution)/shard_map/ppermute | solution.py:228
  32.2 4.8 %product.10 = (bf16[1024,256]{1,0:T(8,128)(2,1)S(1)}, bf16[1024,256]{1,0:T(8,128)(2,1)S(1)}) custom-call(s32[2]{0:T(128)S(1)} %and_select_fusion.4.owner_ref, bf16[2048,1024]{1,0:T(8,128)(2,1)} %tokens_ref.17, bf16[1024,2048]{1,0:T(8,128)(2,1)} %weight_ref.15, bf16[1024,256]{1,0:T(8,128)(2,1)S(1)} %collective-permute-done.refs_0_, ...), custom_call_target="tpu_custom_call" | custom-call | flops 1073741824 | bytes 6291456 | tf_op jit(solution)/shard_map/product/pallas_call | solution.py:61
  37.4 3.4 %collective-permute-start.3 = (bf16[1024,256]{1,0:T(8,128)(2,1)S(1)}, bf16[1024,256]{1,0:T(8,128)(2,1)S(1)}, u32[]{:S(2)}, u32[]{:S(2)}) collective-permute-start(bf16[1024,256]{1,0:T(8,128)(2,1)S(1)} %get-tuple-element.26), channel_id=1, source_target_pairs={{0,7},{1,0},{2,1},{3,2},{4,3},{5,4},{6,5},{7,6},{8,15},{9,8},{10,9... | collective-permute-start | bytes 1572872 | tf_op jit(solution)/shard_map/ppermute | solution.py:228
  40.8 2.5 %collective-permute-done.4.refs_0_ = bf16[1024,256]{1,0:T(8,128)(2,1)S(1)} collective-permute-done((bf16[1024,256]{1,0:T(8,128)(2,1)S(1)}, bf16[1024,256]{1,0:T(8,128)(2,1)S(1)}, u32[]{:S(2)}, u32[]{:S(2)}) %collective-permute-start.4) | collective-permute-done | bytes 524320 | tf_op jit(solution)/shard_map/ppermute | solution.py:228
  43.5 4.8 %product.11 = (bf16[1024,256]{1,0:T(8,128)(2,1)S(1)}, bf16[1024,256]{1,0:T(8,128)(2,1)S(1)}) custom-call(s32[2]{0:T(128)S(1)} %and_select_fusion.1.owner_ref, bf16[2048,1024]{1,0:T(8,128)(2,1)} %tokens_ref.17, bf16[1024,2048]{1,0:T(8,128)(2,1)} %weight_ref.15, bf16[1024,256]{1,0:T(8,128)(2,1)S(1)} %collective-permute-done.4.refs_0_, ...), custom_call_target="tpu_custom_call" | custom-call | flops 1073741824 | bytes 6291456 | tf_op jit(solution)/shard_map/product/pallas_call | solution.py:61
  48.3 3.6 %collective-permute-start.8 = (bf16[1024,256]{1,0:T(8,128)(2,1)S(1)}, bf16[1024,256]{1,0:T(8,128)(2,1)S(1)}, u32[]{:S(2)}, u32[]{:S(2)}) collective-permute-start(bf16[1024,256]{1,0:T(8,128)(2,1)S(1)} %get-tuple-element.28.refs_2_), channel_id=1, source_target_pairs={{0,7},{1,0},{2,1},{3,2},{4,3},{5,4},{6,5},{7,6},{8,15},{9,8},{10,9... | collective-permute-start | bytes 1572872 | tf_op jit(solution)/shard_map/ppermute | solution.py:228
  51.9 2.5 %collective-permute-done.2.refs_0_ = bf16[1024,256]{1,0:T(8,128)(2,1)S(1)} collective-permute-done((bf16[1024,256]{1,0:T(8,128)(2,1)S(1)}, bf16[1024,256]{1,0:T(8,128)(2,1)S(1)}, u32[]{:S(2)}, u32[]{:S(2)}) %collective-permute-start.2) | collective-permute-done | bytes 524320 | tf_op jit(solution)/shard_map/ppermute | solution.py:228
  54.6 4.8 %product.12 = (bf16[1024,256]{1,0:T(8,128)(2,1)S(1)}, bf16[1024,256]{1,0:T(8,128)(2,1)S(1)}) custom-call(s32[2]{0:T(128)S(1)} %and_select_fusion.5.owner_ref, bf16[2048,1024]{1,0:T(8,128)(2,1)} %tokens_ref.17, bf16[1024,2048]{1,0:T(8,128)(2,1)} %weight_ref.15, bf16[1024,256]{1,0:T(8,128)(2,1)S(1)} %collective-permute-done.2.refs_0_, ...), custom_call_target="tpu_custom_call" | custom-call | flops 1073741824 | bytes 6291456 | tf_op jit(solution)/shard_map/product/pallas_call | solution.py:61
  63.4 2.4 %collective-permute-done.8.refs_0_ = bf16[1024,256]{1,0:T(8,128)(2,1)S(1)} collective-permute-done((bf16[1024,256]{1,0:T(8,128)(2,1)S(1)}, bf16[1024,256]{1,0:T(8,128)(2,1)S(1)}, u32[]{:S(2)}, u32[]{:S(2)}) %collective-permute-start.8) | collective-permute-done | bytes 524320 | tf_op jit(solution)/shard_map/ppermute | solution.py:228
  65.8 2.2 %collective-permute-done.9.refs_1_ = bf16[1024,256]{1,0:T(8,128)(2,1)S(1)} collective-permute-done((bf16[1024,256]{1,0:T(8,128)(2,1)S(1)}, bf16[1024,256]{1,0:T(8,128)(2,1)S(1)}, u32[]{:S(2)}, u32[]{:S(2)}) %collective-permute-start.9) | collective-permute-done | bytes 524320 | tf_op jit(solution)/shard_map/ppermute | solution.py:228
  68.0 4.9 %product.13 = (bf16[1024,256]{1,0:T(8,128)(2,1)S(1)}, bf16[1024,256]{1,0:T(8,128)(2,1)S(1)}) custom-call(s32[2]{0:T(128)S(1)} %and_select_fusion.owner_ref, bf16[2048,1024]{1,0:T(8,128)(2,1)} %tokens_ref.17, bf16[1024,2048]{1,0:T(8,128)(2,1)} %weight_ref.15, bf16[1024,256]{1,0:T(8,128)(2,1)S(1)} %collective-permute-done.8.refs_0_, ...), custom_call_target="tpu_custom_call" | custom-call | flops 1073741824 | bytes 6291456 | tf_op jit(solution)/shard_map/product/pallas_call | solution.py:61
  77.1 4.9 %product.14 = (bf16[1024,256]{1,0:T(8,128)(2,1)}, bf16[1024,256]{1,0:T(8,128)(2,1)S(1)}) custom-call(s32[2]{0:T(128)S(1)} %and_select_fusion.6.owner_ref, bf16[2048,1024]{1,0:T(8,128)(2,1)} %tokens_ref.17, bf16[1024,2048]{1,0:T(8,128)(2,1)} %weight_ref.15, bf16[1024,256]{1,0:T(8,128)(2,1)S(1)} %collective-permute-done.6.refs_0_, ...), custom_call_target="tpu_custom_call" | custom-call | flops 1073741824 | bytes 6291456 | tf_op jit(solution)/shard_map/product/pallas_call | solution.py:61
  82.0 2.2 %collective-permute-start.10 = (bf16[1024,256]{1,0:T(8,128)(2,1)}, bf16[1024,256]{1,0:T(8,128)(2,1)S(1)}, u32[]{:S(2)}, u32[]{:S(2)}) collective-permute-start(bf16[1024,256]{1,0:T(8,128)(2,1)} %get-tuple-element.33), channel_id=1, source_target_pairs={{0,1},{1,2},{2,3},{3,4},{4,5},{5,6},{6,7},{7,0},{8,9},{9,10},{10,1... | collective-permute-start | bytes 1572872 | tf_op jit(solution)/shard_map/ppermute | solution.py:228
  86.1 2.2 %collective-permute-done.11.first_ref.refs_0_ = bf16[1024,256]{1,0:T(8,128)(2,1)S(1)} collective-permute-done((bf16[1024,256]{1,0:T(8,128)(2,1)S(1)}, bf16[1024,256]{1,0:T(8,128)(2,1)S(1)}, u32[]{:S(2)}, u32[]{:S(2)}) %collective-permute-start.11) | collective-permute-done | bytes 524320 | tf_op jit(solution)/shard_map/ppermute | solution.py:228
  90.4 5.7 %partial_shrink.1 = bf16[2048,128]{1,0:T(8,128)(2,1)S(1)} custom-call(s32[16]{0:T(128)S(1)} %compare_select_fusion.14.adapter_ref, bf16[2048,1024]{1,0:T(8,128)(2,1)} %tokens_ref.17, bf16[64,1024,128]{2,1,0:T(8,128)(2,1)} %all-gather.3.cloned.1.call-done.pool_ref, bf16[1024,256]{1,0:T(8,128)(2,1)S(1)} %collective-permute-done.11.first_ref.refs_0_, ...), custom_call_target="tpu_custom_call" | custom-call | flops 536870912 | bytes 8388608 | tf_op jit(solution)/shard_map/partial_shrink/pallas_call | solution.py:118
  96.1 2.7 %collective-permute-done.10.refs_0_ = bf16[1024,256]{1,0:T(8,128)(2,1)S(1)} collective-permute-done((bf16[1024,256]{1,0:T(8,128)(2,1)}, bf16[1024,256]{1,0:T(8,128)(2,1)S(1)}, u32[]{:S(2)}, u32[]{:S(2)}) %collective-permute-start.10) | collective-permute-done | bytes 524320 | tf_op jit(solution)/shard_map/ppermute | solution.py:228
  98.8 22.1 %all_to_all.17 = bf16[8,256,128]{2,1,0:T(8,128)(2,1)S(1)} all-to-all(bf16[8,256,128]{2,1,0:T(8,128)(2,1)S(1)} %bitcast.6), channel_id=1, replica_groups=mesh['group'=32,'tensor'=8] {'tensor'}, dimensions={0} | all-to-all | bytes 1048576 | tf_op jit(solution)/shard_map/all_to_all | solution.py:275
  121.9 3.7 %all-to-all-start.1 = ((bf16[8,256,128]{2,1,0:T(8,128)(2,1)}), bf16[8,256,128]{2,1,0:T(8,128)(2,1)S(1)}, u32[]{:S(2)}, u32[]{:S(2)}) async-start(bf16[8,256,128]{2,1,0:T(8,128)(2,1)} %broadcast_in_dim.39), calls=%async_computation.1 | async-start | bytes 1048576 | tf_op jit(solution)/shard_map/all_to_all | solution.py:281
  125.7 4.9 %product.15 = (bf16[1024,256]{1,0:T(8,128)(2,1)S(1)}, bf16[1024,256]{1,0:T(8,128)(2,1)S(1)}) custom-call(s32[2]{0:T(128)S(1)} %broadcast.99.owner_ref, bf16[2048,1024]{1,0:T(8,128)(2,1)} %tokens_ref.17, bf16[1024,2048]{1,0:T(8,128)(2,1)} %weight_ref.15, bf16[1024,256]{1,0:T(8,128)(2,1)S(1)} %collective-permute-done.11.first_ref.refs_0_, ...), custom_call_target="tpu_custom_call" | custom-call | flops 1073741824 | bytes 6291456 | tf_op jit(solution)/shard_map/product/pallas_call | solution.py:61
  131.0 9.6 %all-gather.5.cloned.1.call-done.pool_ref = bf16[64,64,256]{2,1,0:T(8,128)(2,1)} async-done(((bf16[2,64,256]{2,1,0:T(8,128)(2,1)}), bf16[64,64,256]{2,1,0:T(8,128)(2,1)}) %all-gather.5.cloned.1.call-update) | async-done | bytes 2097168 | tf_op jit(solution)/shard_map/all_gather | solution.py:267
  142.2 2.5 %finish.1 = bf16[256,2048]{1,0:T(8,128)(2,1)} custom-call(s32[16]{0:T(128)S(1)} %compare_select_fusion.14.adapter_ref, bf16[256,2048]{1,0:T(8,128)(2,1)S(1)} %turn.1.base_ref, bf16[2048,128]{1,0:T(8,128)(2,1)S(1)} %bitcast.5, bf16[64,64,256]{2,1,0:T(8,128)(2,1)S(1)} %copy-done), custom_call_target="tpu_custom_call" | custom-call | flops 134217728 | bytes 3145728 | tf_op jit(solution)/shard_map/finish/pallas_call | solution.py:197
  (58 shorter events, 21.5 us)
Async XLA Ops:
  6.5 83.8 %all-gather.3.cloned.1.call-start = ((), (), s32[]{:S(2)}) async-start(), calls=%async_computation.2 | async-start | bytes 17301504 | tf_op jit(solution)/shard_map/all_gather | solution.py:266
  7.3 133.4 %all-gather.5.cloned.1.call-start = ((), (), s32[]{:S(2)}) async-start(), calls=%async_computation.3 | async-start | bytes 2162688 | tf_op jit(solution)/shard_map/all_gather | solution.py:267
  13.6 18.7 %collective-permute-start = (bf16[1024,256]{1,0:T(8,128)(2,1)S(1)}, bf16[1024,256]{1,0:T(8,128)(2,1)S(1)}, u32[]{:S(2)}, u32[]{:S(2)}) collective-permute-start(bf16[1024,256]{1,0:T(8,128)(2,1)S(1)} %get-tuple-element.22.refs_0_), channel_id=1, source_target_pairs={{0,1},{1,2},{2,3},{3,4},{4,5},{5,6},{6,7},{7,0},{8,9},{9,10},{10,1... | collective-permute-start | bytes 1572872 | tf_op jit(solution)/shard_map/ppermute | solution.py:228
  15.6 16.7 %collective-permute-start.1 = (bf16[1024,256]{1,0:T(8,128)(2,1)}, bf16[1024,256]{1,0:T(8,128)(2,1)S(1)}, u32[]{:S(2)}, u32[]{:S(2)}) collective-permute-start(bf16[1024,256]{1,0:T(8,128)(2,1)} %get-tuple-element.23), channel_id=1, source_target_pairs={{0,7},{1,0},{2,1},{3,2},{4,3},{5,4},{6,5},{7,6},{8,15},{9,8},{10,9... | collective-permute-start | bytes 1572872 | tf_op jit(solution)/shard_map/ppermute | solution.py:228
  19.6 7.9 %copy-start.9 = (s32[2]{0:T(128)S(1)}, s32[2]{0:T(128)}, u32[]{:S(2)}) copy-start(s32[2]{0:T(128)} %constant.94.clone) | copy-start | bytes 28
  19.6 7.9 %copy-start.8 = (s32[2]{0:T(128)S(1)}, s32[2]{0:T(128)}, u32[]{:S(2)}) copy-start(s32[2]{0:T(128)} %constant.90.clone) | copy-start | bytes 28
  25.2 18.2 %collective-permute-start.4 = (bf16[1024,256]{1,0:T(8,128)(2,1)S(1)}, bf16[1024,256]{1,0:T(8,128)(2,1)S(1)}, u32[]{:S(2)}, u32[]{:S(2)}) collective-permute-start(bf16[1024,256]{1,0:T(8,128)(2,1)S(1)} %get-tuple-element.24.refs_2_), channel_id=1, source_target_pairs={{0,7},{1,0},{2,1},{3,2},{4,3},{5,4},{6,5},{7,6},{8,15},{9,8},{10,9... | collective-permute-start | bytes 1572872 | tf_op jit(solution)/shard_map/ppermute | solution.py:228
  27.2 16.3 %collective-permute-start.5 = (bf16[1024,256]{1,0:T(8,128)(2,1)}, bf16[1024,256]{1,0:T(8,128)(2,1)S(1)}, u32[]{:S(2)}, u32[]{:S(2)}) collective-permute-start(bf16[1024,256]{1,0:T(8,128)(2,1)} %get-tuple-element.27), channel_id=1, source_target_pairs={{0,1},{1,2},{2,3},{3,4},{4,5},{5,6},{6,7},{7,0},{8,9},{9,10},{10,1... | collective-permute-start | bytes 1572872 | tf_op jit(solution)/shard_map/ppermute | solution.py:228
  27.6 13.2 %copy-start.7 = (s32[2]{0:T(128)S(1)}, s32[2]{0:T(128)}, u32[]{:S(2)}) copy-start(s32[2]{0:T(128)} %constant.92.clone) | copy-start | bytes 28
  27.6 13.2 %copy-start.6 = (s32[2]{0:T(128)S(1)}, s32[2]{0:T(128)}, u32[]{:S(2)}) copy-start(s32[2]{0:T(128)} %constant.91.clone) | copy-start | bytes 28
  37.1 17.4 %collective-permute-start.2 = (bf16[1024,256]{1,0:T(8,128)(2,1)S(1)}, bf16[1024,256]{1,0:T(8,128)(2,1)S(1)}, u32[]{:S(2)}, u32[]{:S(2)}) collective-permute-start(bf16[1024,256]{1,0:T(8,128)(2,1)S(1)} %get-tuple-element.25.refs_2_), channel_id=1, source_target_pairs={{0,1},{1,2},{2,3},{3,4},{4,5},{5,6},{6,7},{7,0},{8,9},{9,10},{10,1... | collective-permute-start | bytes 1572872 | tf_op jit(solution)/shard_map/ppermute | solution.py:228
  37.4 17.2 %collective-permute-start.3 = (bf16[1024,256]{1,0:T(8,128)(2,1)S(1)}, bf16[1024,256]{1,0:T(8,128)(2,1)S(1)}, u32[]{:S(2)}, u32[]{:S(2)}) collective-permute-start(bf16[1024,256]{1,0:T(8,128)(2,1)S(1)} %get-tuple-element.26), channel_id=1, source_target_pairs={{0,7},{1,0},{2,1},{3,2},{4,3},{5,4},{6,5},{7,6},{8,15},{9,8},{10,9... | collective-permute-start | bytes 1572872 | tf_op jit(solution)/shard_map/ppermute | solution.py:228
  48.3 17.6 %collective-permute-start.8 = (bf16[1024,256]{1,0:T(8,128)(2,1)S(1)}, bf16[1024,256]{1,0:T(8,128)(2,1)S(1)}, u32[]{:S(2)}, u32[]{:S(2)}) collective-permute-start(bf16[1024,256]{1,0:T(8,128)(2,1)S(1)} %get-tuple-element.28.refs_2_), channel_id=1, source_target_pairs={{0,7},{1,0},{2,1},{3,2},{4,3},{5,4},{6,5},{7,6},{8,15},{9,8},{10,9... | collective-permute-start | bytes 1572872 | tf_op jit(solution)/shard_map/ppermute | solution.py:228
  51.9 11.4 %copy-start.5 = (s32[2]{0:T(128)S(1)}, s32[2]{0:T(128)}, u32[]{:S(2)}) copy-start(s32[2]{0:T(128)} %constant.93.clone) | copy-start | bytes 28
  51.9 11.5 %copy-start.3 = (s32[13]{0:T(128)S(1)}, s32[13]{0:T(128)}, u32[]{:S(2)}) copy-start(s32[13]{0:T(128)} %param.23) | copy-start | bytes 160
  51.9 11.5 %copy-start.4 = (s32[13,1]{0,1:T(1,128)S(1)}, s32[13,1]{0,1:T(1,128)}, u32[]{:S(2)}) copy-start(s32[13,1]{0,1:T(1,128)} %param.22) | copy-start | bytes 160
  51.9 16.1 %collective-permute-start.9 = (bf16[1024,256]{1,0:T(8,128)(2,1)S(1)}, bf16[1024,256]{1,0:T(8,128)(2,1)S(1)}, u32[]{:S(2)}, u32[]{:S(2)}) collective-permute-start(bf16[1024,256]{1,0:T(8,128)(2,1)S(1)} %get-tuple-element.31), channel_id=1, source_target_pairs={{0,1},{1,2},{2,3},{3,4},{4,5},{5,6},{6,7},{7,0},{8,9},{9,10},{10,1... | collective-permute-start | bytes 1572872 | tf_op jit(solution)/shard_map/ppermute | solution.py:228
  59.4 17.4 %collective-permute-start.6 = (bf16[1024,256]{1,0:T(8,128)(2,1)S(1)}, bf16[1024,256]{1,0:T(8,128)(2,1)S(1)}, u32[]{:S(2)}, u32[]{:S(2)}) collective-permute-start(bf16[1024,256]{1,0:T(8,128)(2,1)S(1)} %get-tuple-element.29.refs_2_), channel_id=1, source_target_pairs={{0,1},{1,2},{2,3},{3,4},{4,5},{5,6},{6,7},{7,0},{8,9},{9,10},{10,1... | collective-permute-start | bytes 1572872 | tf_op jit(solution)/shard_map/ppermute | solution.py:228
  61.5 15.5 %collective-permute-start.7 = (bf16[1024,256]{1,0:T(8,128)(2,1)S(1)}, bf16[1024,256]{1,0:T(8,128)(2,1)S(1)}, u32[]{:S(2)}, u32[]{:S(2)}) collective-permute-start(bf16[1024,256]{1,0:T(8,128)(2,1)S(1)} %get-tuple-element.30), channel_id=1, source_target_pairs={{0,7},{1,0},{2,1},{3,2},{4,3},{5,4},{6,5},{7,6},{8,15},{9,8},{10,9... | collective-permute-start | bytes 1572872 | tf_op jit(solution)/shard_map/ppermute | solution.py:228
  72.9 15.4 %collective-permute-start.11 = (bf16[1024,256]{1,0:T(8,128)(2,1)S(1)}, bf16[1024,256]{1,0:T(8,128)(2,1)S(1)}, u32[]{:S(2)}, u32[]{:S(2)}) collective-permute-start(bf16[1024,256]{1,0:T(8,128)(2,1)S(1)} %get-tuple-element.32.refs_2_), channel_id=1, source_target_pairs={{0,7},{1,0},{2,1},{3,2},{4,3},{5,4},{6,5},{7,6},{8,15},{9,8},{10,9... | collective-permute-start | bytes 1572872 | tf_op jit(solution)/shard_map/ppermute | solution.py:228
  74.5 15.8 %collective-permute-start.12 = (bf16[1024,256]{1,0:T(8,128)(2,1)S(1)}, bf16[1024,256]{1,0:T(8,128)(2,1)S(1)}, u32[]{:S(2)}, u32[]{:S(2)}) collective-permute-start(bf16[1024,256]{1,0:T(8,128)(2,1)S(1)} %get-tuple-element.34), channel_id=1, source_target_pairs={{0,1},{1,2},{2,3},{3,4},{4,5},{5,6},{6,7},{7,0},{8,9},{9,10},{10,1... | collective-permute-start | bytes 1572872 | tf_op jit(solution)/shard_map/ppermute | solution.py:228
  82.0 16.8 %collective-permute-start.10 = (bf16[1024,256]{1,0:T(8,128)(2,1)}, bf16[1024,256]{1,0:T(8,128)(2,1)S(1)}, u32[]{:S(2)}, u32[]{:S(2)}) collective-permute-start(bf16[1024,256]{1,0:T(8,128)(2,1)} %get-tuple-element.33), channel_id=1, source_target_pairs={{0,1},{1,2},{2,3},{3,4},{4,5},{5,6},{6,7},{7,0},{8,9},{9,10},{10,1... | collective-permute-start | bytes 1572872 | tf_op jit(solution)/shard_map/ppermute | solution.py:228
  84.2 14.6 %collective-permute-start.13 = (bf16[1024,256]{1,0:T(8,128)(2,1)S(1)}, bf16[1024,256]{1,0:T(8,128)(2,1)S(1)}, u32[]{:S(2)}, u32[]{:S(2)}) collective-permute-start(bf16[1024,256]{1,0:T(8,128)(2,1)S(1)} %get-tuple-element.35), channel_id=1, source_target_pairs={{0,7},{1,0},{2,1},{3,2},{4,3},{5,4},{6,5},{7,6},{8,15},{9,8},{10,9... | collective-permute-start | bytes 1572872 | tf_op jit(solution)/shard_map/ppermute | solution.py:228
  121.9 18.7 %all-to-all-start.1 = ((bf16[8,256,128]{2,1,0:T(8,128)(2,1)}), bf16[8,256,128]{2,1,0:T(8,128)(2,1)S(1)}, u32[]{:S(2)}, u32[]{:S(2)}) async-start(bf16[8,256,128]{2,1,0:T(8,128)(2,1)} %broadcast_in_dim.39), calls=%async_computation.1 | async-start | bytes 1048576 | tf_op jit(solution)/shard_map/all_to_all | solution.py:281
  (3 other events, 17.1 us)
Sparse Core Ops, SparseCore 0:
  9.9 79.7 all-gather.2
  92.3 48.3 all-gather.4

commit v5 on v4

--- a/solution.py
+++ b/solution.py
@@ -8,6 +8,7 @@
 from jax.sharding import PartitionSpec as P
 
 HEAD = 128
+CORES = 2
 TILE = 512
 VMEM = 50 * 2**20
 NT = (((1,), (1,)), ((), ()))
@@ -168,19 +169,19 @@
     )(*sums)
 
 
-def finish_kernel(adapter_ref, base_ref, shrink_ref, pool_ref, out_ref):
+def finish_kernel(place_ref, base_ref, shrink_ref, own_ref, other_ref, out_ref):
     step = pl.program_id(0)
-    tile = shrink_ref.shape[0] * pl.num_programs(0) // adapter_ref.shape[0]
+    tile = shrink_ref.shape[0] * pl.num_programs(0) // place_ref.shape[0]
     here = shrink_ref.shape[0] // tile
-    rank = pool_ref.shape[1]
-    for b in range(here):
-        adapter = adapter_ref[step * here + b]
+    count, rank, _ = own_ref.shape
+
+    def write(b, table_ref, place):
         at = slice(b * tile, (b + 1) * tile)
         for kind in range(2):
             rows = slice(kind * HEAD, (kind + 1) * HEAD)
             ranks = slice(kind * rank, (kind + 1) * rank)
             delta = lax.dot_general(
-                pool_ref[adapter, :, rows],
+                table_ref[place, :, rows],
                 shrink_ref[at, ranks],
                 (((0,), (1,)), ((), ())),
                 preferred_element_type=jnp.float32,
@@ -189,8 +190,13 @@
                 out_ref.dtype
             )
 
-
-def finish(adapters, base, shrink, pools):
+    for b in range(here):
+        place = place_ref[step * here + b]
+        pl.when(place < count)(functools.partial(write, b, own_ref, place))
+        pl.when(place >= count)(functools.partial(write, b, other_ref, place - count))
+
+
+def finish(places, base, shrink, own, other):
     columns, rows = base.shape
     steps = 2
     step = rows // steps
@@ -203,6 +209,7 @@
                 pl.BlockSpec((columns, step), lambda i, adapter: (0, i)),
                 pl.BlockSpec((step, shrink.shape[1]), lambda i, adapter: (i, 0)),
                 pl.BlockSpec(memory_space=pltpu.VMEM),
+                pl.BlockSpec(memory_space=pltpu.VMEM),
             ],
             out_specs=pl.BlockSpec((columns, step), lambda i, adapter: (0, i)),
         ),
@@ -212,7 +219,7 @@
         ),
         compiler_params=pltpu.CompilerParams(vmem_limit_bytes=24 * 2**20),
         name="finish",
-    )(adapters, base, shrink, pools)
+    )(places, base, shrink, own, other)
 
 
 def add(*terms):
@@ -264,7 +271,10 @@
     tensor = lax.axis_size("tensor")
     rows = tokens.shape[0]
     pools_a = lax.all_gather(a_pool, "group", tiled=True)
-    pools_b = lax.all_gather(b_pool, "group", tiled=True)
+    groups = lax.axis_size("group")
+    same = [list(range(core, groups, CORES)) for core in range(CORES)]
+    own_b = lax.all_gather(b_pool, "group", axis_index_groups=same, tiled=True)
+    other_b = lax.ppermute(own_b, "group", [(i, i ^ 1) for i in range(groups)])
     adapters = block_adapters(
         a_pool.shape[0], request_entry, block_request[0], fetch_source[:, 0], fetch_slot
     )
@@ -279,7 +289,12 @@
     shrink, sums = ring_sum(tokens, kv_weight, adapted)
     shrink = jnp.broadcast_to(shrink[None], (tensor,) + shrink.shape).reshape(rows, -1)
     shrink = lax.all_to_all(shrink, "tensor", split_axis=0, concat_axis=0, tiled=True)
-    return finish(adapters, turn(sums), shrink, pools_b)
+    pool = b_pool.shape[0]
+    group = adapters // pool
+    places = group // CORES * pool + adapters % pool
+    far = group % CORES != lax.axis_index("group") % CORES
+    places = jnp.where(far, places + own_b.shape[0], places)
+    return finish(places, turn(sums), shrink, own_b, other_b)
 
 
 def solution(mesh):

time: 154 us -> 181 us (1.18)
  waiting for transfers between devices: 33.9 us -> 69.9 us
  blocking collectives: 22.1 us -> 0 us
  starting transfers between devices: 29.2 us -> 37.6 us
  Pallas kernels: 49 us -> 55.6 us
    all_gather x1, waiting for transfers between devices: 9.59 us -> 34.5 us  [per_device(): own_b = lax.all_gather(b_pool, 'group', axis_index_groups=same, tiled=True)]
    all_to_all x1 -> x0, blocking collectives: 22.1 us -> none  [adapted(): lax.all_to_all(shrink, 'tensor', split_axis=0, concat_axis=0, tiled=True)]
    all_to_all x1, waiting for transfers between devices: 0.01 us -> 12.9 us  [per_device(): lax.all_to_all(shrink, 'tensor', split_axis=0, concat_axis=0, tiled=True)]
    all_to_all x0 -> x1, starting transfers between devices: none -> 5.41 us  [adapted(): lax.all_to_all(shrink, 'tensor', split_axis=0, concat_axis=0, tiled=True)]
    pallas_call x1, Pallas kernels: 2.52 us -> 6.44 us  [finish(): pl.pallas_call(finish_kernel, grid_spec=pltpu.PrefetchScalarGridSpec(num_...]
    all_to_all x1, starting transfers between devices: 3.71 us -> 7.01 us  [per_device(): lax.all_to_all(shrink, 'tensor', split_axis=0, concat_axis=0, tiled=True)]
    pallas_call x8, Pallas kernels: 40.3 us -> 42.4 us  [product(): pl.pallas_call(functools.partial(product_kernel, len(arrived)), in_specs=...]
  transfers between devices with their start and end apart: 17 -> 19, of which waited for: 13 -> 13; matrix products, arithmetic and copies ran while one was open for 1% -> 1% of each run, Pallas kernels for 31% -> 27%
where the time goes in v5:
time: 181 us; the launch traced here: 179 us
  waiting for transfers between devices  69.9 us (39%)
  Pallas kernels  55.6 us (31%)
  starting transfers between devices  37.6 us (21%)
  between operations  13.7 us (8%)
    pallas_call x8, Pallas kernels, product(): pl.pallas_call(functools.partial(product_kernel, len(arrived)), in_specs=...  42.4 us
    all_gather x1, waiting for transfers between devices, per_device(): own_b = lax.all_gather(b_pool, 'group', axis_index_groups=same, tiled=True)  34.5 us
    ppermute x14, starting transfers between devices, hop(): lax.ppermute(value, 'tensor', [(i, (i + way) % count) for i in range(coun...  25.1 us
    ppermute x14, waiting for transfers between devices, hop(): lax.ppermute(value, 'tensor', [(i, (i + way) % count) for i in range(coun...  21.8 us
    all_to_all x1, waiting for transfers between devices, per_device(): lax.all_to_all(shrink, 'tensor', split_axis=0, concat_axis=0, tiled=True)  12.9 us
    all_to_all x1, starting transfers between devices, per_device(): lax.all_to_all(shrink, 'tensor', split_axis=0, concat_axis=0, tiled=True)  7.01 us
    pallas_call x1, Pallas kernels, finish(): pl.pallas_call(finish_kernel, grid_spec=pltpu.PrefetchScalarGridSpec(num_...  6.44 us
    pallas_call x1, Pallas kernels, partial_shrink(): pl.pallas_call(shrink_kernel, in_specs=[pl.BlockSpec(memory_space=pltpu.S...  6.27 us
  transfers between devices with their start and end apart: 19, of which 13 were waited for; matrix products, arithmetic and copies ran while one was open for 1% of the time, Pallas kernels for 27%

profile of v5, /device:TPU:24, one launch (start us, length us, event | category | flops | bytes accessed | tf_op | source)
XLA Modules:
  0.0 178.9 jit_solution(17625622043735943125)
XLA Ops:
  8.0 5.6 %product.8 = (bf16[1024,256]{1,0:T(8,128)(2,1)S(1)}, bf16[1024,256]{1,0:T(8,128)(2,1)}) custom-call(s32[2]{0:T(128)S(1)} %get-tuple-element.42.owner_ref, bf16[2048,1024]{1,0:T(8,128)(2,1)} %tokens_ref.17, bf16[1024,2048]{1,0:T(8,128)(2,1)} %weight_ref.15), custom_call_target="tpu_custom_call" | custom-call | flops 1073741824 | bytes 6291456 | tf_op jit(solution)/shard_map/product/pallas_call | solution.py:62
  15.6 4.0 %collective-permute-start.1 = (bf16[1024,256]{1,0:T(8,128)(2,1)}, bf16[1024,256]{1,0:T(8,128)(2,1)S(1)}, u32[]{:S(2)}, u32[]{:S(2)}) collective-permute-start(bf16[1024,256]{1,0:T(8,128)(2,1)} %get-tuple-element.23), channel_id=1, source_target_pairs={{0,7},{1,0},{2,1},{3,2},{4,3},{5,4},{6,5},{7,6},{8,15},{9,8},{10,9... | collective-permute-start | bytes 1572872 | tf_op jit(solution)/shard_map/ppermute | solution.py:235
  19.6 5.6 %product.9 = (bf16[1024,256]{1,0:T(8,128)(2,1)S(1)}, bf16[1024,256]{1,0:T(8,128)(2,1)}) custom-call(s32[2]{0:T(128)S(1)} %get-tuple-element.41.owner_ref, bf16[2048,1024]{1,0:T(8,128)(2,1)} %tokens_ref.17, bf16[1024,2048]{1,0:T(8,128)(2,1)} %weight_ref.15, bf16[1024,256]{1,0:T(8,128)(2,1)S(1)} %get-tuple-element.22.refs_0_), custom_call_target="tpu_custom_call" | custom-call | flops 1073741824 | bytes 6291456 | tf_op jit(solution)/shard_map/product/pallas_call | solution.py:62
  27.4 4.9 %collective-permute-done.refs_0_ = bf16[1024,256]{1,0:T(8,128)(2,1)S(1)} collective-permute-done((bf16[1024,256]{1,0:T(8,128)(2,1)S(1)}, bf16[1024,256]{1,0:T(8,128)(2,1)S(1)}, u32[]{:S(2)}, u32[]{:S(2)}) %collective-permute-start) | collective-permute-done | bytes 524320 | tf_op jit(solution)/shard_map/ppermute | solution.py:235
  32.2 4.8 %product.10 = (bf16[1024,256]{1,0:T(8,128)(2,1)S(1)}, bf16[1024,256]{1,0:T(8,128)(2,1)S(1)}) custom-call(s32[2]{0:T(128)S(1)} %and_select_fusion.4.owner_ref, bf16[2048,1024]{1,0:T(8,128)(2,1)} %tokens_ref.17, bf16[1024,2048]{1,0:T(8,128)(2,1)} %weight_ref.15, bf16[1024,256]{1,0:T(8,128)(2,1)S(1)} %collective-permute-done.refs_0_, ...), custom_call_target="tpu_custom_call" | custom-call | flops 1073741824 | bytes 6291456 | tf_op jit(solution)/shard_map/product/pallas_call | solution.py:62
  37.4 3.4 %collective-permute-start.3 = (bf16[1024,256]{1,0:T(8,128)(2,1)S(1)}, bf16[1024,256]{1,0:T(8,128)(2,1)S(1)}, u32[]{:S(2)}, u32[]{:S(2)}) collective-permute-start(bf16[1024,256]{1,0:T(8,128)(2,1)S(1)} %get-tuple-element.26), channel_id=1, source_target_pairs={{0,7},{1,0},{2,1},{3,2},{4,3},{5,4},{6,5},{7,6},{8,15},{9,8},{10,9... | collective-permute-start | bytes 1572872 | tf_op jit(solution)/shard_map/ppermute | solution.py:235
  40.8 2.5 %collective-permute-done.4.refs_0_ = bf16[1024,256]{1,0:T(8,128)(2,1)S(1)} collective-permute-done((bf16[1024,256]{1,0:T(8,128)(2,1)S(1)}, bf16[1024,256]{1,0:T(8,128)(2,1)S(1)}, u32[]{:S(2)}, u32[]{:S(2)}) %collective-permute-start.4) | collective-permute-done | bytes 524320 | tf_op jit(solution)/shard_map/ppermute | solution.py:235
  43.5 5.6 %product.11 = (bf16[1024,256]{1,0:T(8,128)(2,1)S(1)}, bf16[1024,256]{1,0:T(8,128)(2,1)}) custom-call(s32[2]{0:T(128)S(1)} %and_select_fusion.1.owner_ref, bf16[2048,1024]{1,0:T(8,128)(2,1)} %tokens_ref.17, bf16[1024,2048]{1,0:T(8,128)(2,1)} %weight_ref.15, bf16[1024,256]{1,0:T(8,128)(2,1)S(1)} %collective-permute-done.4.refs_0_, ...), custom_call_target="tpu_custom_call" | custom-call | flops 1073741824 | bytes 6291456 | tf_op jit(solution)/shard_map/product/pallas_call | solution.py:62
  49.1 3.6 %collective-permute-start.8 = (bf16[1024,256]{1,0:T(8,128)(2,1)S(1)}, bf16[1024,256]{1,0:T(8,128)(2,1)S(1)}, u32[]{:S(2)}, u32[]{:S(2)}) collective-permute-start(bf16[1024,256]{1,0:T(8,128)(2,1)S(1)} %get-tuple-element.28.refs_2_), channel_id=1, source_target_pairs={{0,7},{1,0},{2,1},{3,2},{4,3},{5,4},{6,5},{7,6},{8,15},{9,8},{10,9... | collective-permute-start | bytes 1572872 | tf_op jit(solution)/shard_map/ppermute | solution.py:235
  54.6 5.6 %product.12 = (bf16[1024,256]{1,0:T(8,128)(2,1)S(1)}, bf16[1024,256]{1,0:T(8,128)(2,1)}) custom-call(s32[2]{0:T(128)S(1)} %and_select_fusion.5.owner_ref, bf16[2048,1024]{1,0:T(8,128)(2,1)} %tokens_ref.17, bf16[1024,2048]{1,0:T(8,128)(2,1)} %weight_ref.15, bf16[1024,256]{1,0:T(8,128)(2,1)S(1)} %collective-permute-done.2.refs_0_, ...), custom_call_target="tpu_custom_call" | custom-call | flops 1073741824 | bytes 6291456 | tf_op jit(solution)/shard_map/product/pallas_call | solution.py:62
  62.0 2.2 %collective-permute-start.7 = (bf16[1024,256]{1,0:T(8,128)(2,1)}, bf16[1024,256]{1,0:T(8,128)(2,1)S(1)}, u32[]{:S(2)}, u32[]{:S(2)}) collective-permute-start(bf16[1024,256]{1,0:T(8,128)(2,1)} %get-tuple-element.30), channel_id=1, source_target_pairs={{0,7},{1,0},{2,1},{3,2},{4,3},{5,4},{6,5},{7,6},{8,15},{9,8},{10,9... | collective-permute-start | bytes 1572872 | tf_op jit(solution)/shard_map/ppermute | solution.py:235
  65.8 2.8 %collective-permute-done.9.refs_1_ = bf16[1024,256]{1,0:T(8,128)(2,1)S(1)} collective-permute-done((bf16[1024,256]{1,0:T(8,128)(2,1)}, bf16[1024,256]{1,0:T(8,128)(2,1)S(1)}, u32[]{:S(2)}, u32[]{:S(2)}) %collective-permute-start.9) | collective-permute-done | bytes 524320 | tf_op jit(solution)/shard_map/ppermute | solution.py:235
  68.6 4.8 %product.13 = (bf16[1024,256]{1,0:T(8,128)(2,1)S(1)}, bf16[1024,256]{1,0:T(8,128)(2,1)S(1)}) custom-call(s32[2]{0:T(128)S(1)} %and_select_fusion.owner_ref, bf16[2048,1024]{1,0:T(8,128)(2,1)} %tokens_ref.17, bf16[1024,2048]{1,0:T(8,128)(2,1)} %weight_ref.15, bf16[1024,256]{1,0:T(8,128)(2,1)S(1)} %collective-permute-done.8.refs_0_, ...), custom_call_target="tpu_custom_call" | custom-call | flops 1073741824 | bytes 6291456 | tf_op jit(solution)/shard_map/product/pallas_call | solution.py:62
  75.6 2.5 %collective-permute-done.6.refs_0_ = bf16[1024,256]{1,0:T(8,128)(2,1)S(1)} collective-permute-done((bf16[1024,256]{1,0:T(8,128)(2,1)S(1)}, bf16[1024,256]{1,0:T(8,128)(2,1)S(1)}, u32[]{:S(2)}, u32[]{:S(2)}) %collective-permute-start.6) | collective-permute-done | bytes 524320 | tf_op jit(solution)/shard_map/ppermute | solution.py:235
  78.0 5.7 %product.14 = (bf16[1024,256]{1,0:T(8,128)(2,1)}, bf16[1024,256]{1,0:T(8,128)(2,1)}) custom-call(s32[2]{0:T(128)S(1)} %and_select_fusion.6.owner_ref, bf16[2048,1024]{1,0:T(8,128)(2,1)} %tokens_ref.17, bf16[1024,2048]{1,0:T(8,128)(2,1)} %weight_ref.15, bf16[1024,256]{1,0:T(8,128)(2,1)S(1)} %collective-permute-done.6.refs_0_, ...), custom_call_target="tpu_custom_call" | custom-call | flops 1073741824 | bytes 6291456 | tf_op jit(solution)/shard_map/product/pallas_call | solution.py:62
  88.3 2.3 %collective-permute-done.12.second_ref.refs_1_ = bf16[1024,256]{1,0:T(8,128)(2,1)S(1)} collective-permute-done((bf16[1024,256]{1,0:T(8,128)(2,1)S(1)}, bf16[1024,256]{1,0:T(8,128)(2,1)S(1)}, u32[]{:S(2)}, u32[]{:S(2)}) %collective-permute-start.12) | collective-permute-done | bytes 524320 | tf_op jit(solution)/shard_map/ppermute | solution.py:235
  90.6 6.3 %partial_shrink.1 = bf16[2048,128]{1,0:T(8,128)(2,1)} custom-call(s32[16]{0:T(128)S(1)} %get-tuple-element.40.adapter_ref, bf16[2048,1024]{1,0:T(8,128)(2,1)} %tokens_ref.17, bf16[64,1024,128]{2,1,0:T(8,128)(2,1)} %all-gather.3.cloned.1.call-done.pool_ref, bf16[1024,256]{1,0:T(8,128)(2,1)S(1)} %collective-permute-done.11.first_ref.refs_0_, ...), custom_call_target="tpu_custom_call" | custom-call | flops 536870912 | bytes 8388608 | tf_op jit(solution)/shard_map/partial_shrink/pallas_call | solution.py:119
  96.9 2.6 %collective-permute-done.10.refs_0_ = bf16[1024,256]{1,0:T(8,128)(2,1)S(1)} collective-permute-done((bf16[1024,256]{1,0:T(8,128)(2,1)}, bf16[1024,256]{1,0:T(8,128)(2,1)S(1)}, u32[]{:S(2)}, u32[]{:S(2)}) %collective-permute-start.10) | collective-permute-done | bytes 524320 | tf_op jit(solution)/shard_map/ppermute | solution.py:235
  99.5 5.4 %all-to-all-start = ((bf16[8,256,128]{2,1,0:T(8,128)(2,1)}), bf16[8,256,128]{2,1,0:T(8,128)(2,1)S(1)}, u32[]{:S(2)}, u32[]{:S(2)}) async-start(bf16[8,256,128]{2,1,0:T(8,128)(2,1)} %bitcast.2), calls=%async_computation | async-start | bytes 1048576 | tf_op jit(solution)/shard_map/all_to_all | solution.py:285
  104.9 34.5 %all-gather.5.cloned.1.call-done.own_ref = bf16[32,64,256]{2,1,0:T(8,128)(2,1)} async-done(((bf16[2,64,256]{2,1,0:T(8,128)(2,1)}), bf16[32,64,256]{2,1,0:T(8,128)(2,1)}) %all-gather.5.cloned.1.call-update) | async-done | bytes 1048592 | tf_op jit(solution)/shard_map/all_gather | solution.py:276
  140.3 7.0 %all-to-all-start.1 = ((bf16[8,256,128]{2,1,0:T(8,128)(2,1)}), bf16[8,256,128]{2,1,0:T(8,128)(2,1)S(1)}, u32[]{:S(2)}, u32[]{:S(2)}) async-start(bf16[8,256,128]{2,1,0:T(8,128)(2,1)} %broadcast_in_dim.39), calls=%async_computation.1 | async-start | bytes 1048576 | tf_op jit(solution)/shard_map/all_to_all | solution.py:291
  147.4 4.8 %product.15 = (bf16[1024,256]{1,0:T(8,128)(2,1)S(1)}, bf16[1024,256]{1,0:T(8,128)(2,1)S(1)}) custom-call(s32[2]{0:T(128)S(1)} %broadcast.127.owner_ref, bf16[2048,1024]{1,0:T(8,128)(2,1)} %tokens_ref.17, bf16[1024,2048]{1,0:T(8,128)(2,1)} %weight_ref.15, bf16[1024,256]{1,0:T(8,128)(2,1)S(1)} %collective-permute-done.11.first_ref.refs_0_, ...), custom_call_target="tpu_custom_call" | custom-call | flops 1073741824 | bytes 6291456 | tf_op jit(solution)/shard_map/product/pallas_call | solution.py:62
  152.7 12.9 %all-to-all-done.1 = bf16[8,256,128]{2,1,0:T(8,128)(2,1)S(1)} async-done(((bf16[8,256,128]{2,1,0:T(8,128)(2,1)}), bf16[8,256,128]{2,1,0:T(8,128)(2,1)S(1)}, u32[]{:S(2)}, u32[]{:S(2)}) %all-to-all-start.1) | async-done | bytes 524320 | tf_op jit(solution)/shard_map/all_to_all | solution.py:291
  165.6 6.4 %finish.1 = bf16[256,2048]{1,0:T(8,128)(2,1)} custom-call(s32[16]{0:T(128)S(1)} %get-tuple-element.39.place_ref, bf16[256,2048]{1,0:T(8,128)(2,1)S(1)} %turn.1.base_ref, bf16[2048,128]{1,0:T(8,128)(2,1)S(1)} %bitcast.5, bf16[32,64,256]{2,1,0:T(8,128)(2,1)S(1)} %copy-done, bf16[32,64,256]{2,1,0:T(8,128)(2,1)} %collective-permute-done.14.other_ref), custom_call_target="tpu_custom_call" | custom-call | flops 134217728 | bytes 3145728 | tf_op jit(solution)/shard_map/finish/pallas_call | solution.py:203
  (65 shorter events, 19.5 us)
Async XLA Ops:
  6.5 84.1 %all-gather.3.cloned.1.call-start = ((), (), s32[]{:S(2)}) async-start(), calls=%async_computation.2 | async-start | bytes 17301504 | tf_op jit(solution)/shard_map/all_gather | solution.py:273
  7.3 132.1 %all-gather.5.cloned.1.call-start = ((), (), s32[]{:S(2)}) async-start(), calls=%async_computation.3 | async-start | bytes 1114112 | tf_op jit(solution)/shard_map/all_gather | solution.py:276
  13.6 18.7 %collective-permute-start = (bf16[1024,256]{1,0:T(8,128)(2,1)S(1)}, bf16[1024,256]{1,0:T(8,128)(2,1)S(1)}, u32[]{:S(2)}, u32[]{:S(2)}) collective-permute-start(bf16[1024,256]{1,0:T(8,128)(2,1)S(1)} %get-tuple-element.22.refs_0_), channel_id=1, source_target_pairs={{0,1},{1,2},{2,3},{3,4},{4,5},{5,6},{6,7},{7,0},{8,9},{9,10},{10,1... | collective-permute-start | bytes 1572872 | tf_op jit(solution)/shard_map/ppermute | solution.py:235
  15.6 16.7 %collective-permute-start.1 = (bf16[1024,256]{1,0:T(8,128)(2,1)}, bf16[1024,256]{1,0:T(8,128)(2,1)S(1)}, u32[]{:S(2)}, u32[]{:S(2)}) collective-permute-start(bf16[1024,256]{1,0:T(8,128)(2,1)} %get-tuple-element.23), channel_id=1, source_target_pairs={{0,7},{1,0},{2,1},{3,2},{4,3},{5,4},{6,5},{7,6},{8,15},{9,8},{10,9... | collective-permute-start | bytes 1572872 | tf_op jit(solution)/shard_map/ppermute | solution.py:235
  25.2 18.2 %collective-permute-start.4 = (bf16[1024,256]{1,0:T(8,128)(2,1)S(1)}, bf16[1024,256]{1,0:T(8,128)(2,1)S(1)}, u32[]{:S(2)}, u32[]{:S(2)}) collective-permute-start(bf16[1024,256]{1,0:T(8,128)(2,1)S(1)} %get-tuple-element.24.refs_2_), channel_id=1, source_target_pairs={{0,7},{1,0},{2,1},{3,2},{4,3},{5,4},{6,5},{7,6},{8,15},{9,8},{10,9... | collective-permute-start | bytes 1572872 | tf_op jit(solution)/shard_map/ppermute | solution.py:235
  27.2 16.3 %collective-permute-start.5 = (bf16[1024,256]{1,0:T(8,128)(2,1)}, bf16[1024,256]{1,0:T(8,128)(2,1)S(1)}, u32[]{:S(2)}, u32[]{:S(2)}) collective-permute-start(bf16[1024,256]{1,0:T(8,128)(2,1)} %get-tuple-element.27), channel_id=1, source_target_pairs={{0,1},{1,2},{2,3},{3,4},{4,5},{5,6},{6,7},{7,0},{8,9},{9,10},{10,1... | collective-permute-start | bytes 1572872 | tf_op jit(solution)/shard_map/ppermute | solution.py:235
  27.3 13.4 %copy-start.9 = (s32[2]{0:T(128)S(1)}, s32[2]{0:T(128)}, u32[]{:S(2)}) copy-start(s32[2]{0:T(128)} %constant.135.clone) | copy-start | bytes 28
  27.4 13.4 %copy-start.8 = (s32[2]{0:T(128)S(1)}, s32[2]{0:T(128)}, u32[]{:S(2)}) copy-start(s32[2]{0:T(128)} %constant.134.clone) | copy-start | bytes 28
  37.1 16.8 %collective-permute-start.2 = (bf16[1024,256]{1,0:T(8,128)(2,1)S(1)}, bf16[1024,256]{1,0:T(8,128)(2,1)S(1)}, u32[]{:S(2)}, u32[]{:S(2)}) collective-permute-start(bf16[1024,256]{1,0:T(8,128)(2,1)S(1)} %get-tuple-element.25.refs_2_), channel_id=1, source_target_pairs={{0,1},{1,2},{2,3},{3,4},{4,5},{5,6},{6,7},{7,0},{8,9},{9,10},{10,1... | collective-permute-start | bytes 1572872 | tf_op jit(solution)/shard_map/ppermute | solution.py:235
  37.4 17.2 %collective-permute-start.3 = (bf16[1024,256]{1,0:T(8,128)(2,1)S(1)}, bf16[1024,256]{1,0:T(8,128)(2,1)S(1)}, u32[]{:S(2)}, u32[]{:S(2)}) collective-permute-start(bf16[1024,256]{1,0:T(8,128)(2,1)S(1)} %get-tuple-element.26), channel_id=1, source_target_pairs={{0,7},{1,0},{2,1},{3,2},{4,3},{5,4},{6,5},{7,6},{8,15},{9,8},{10,9... | collective-permute-start | bytes 1572872 | tf_op jit(solution)/shard_map/ppermute | solution.py:235
  49.1 16.8 %collective-permute-start.8 = (bf16[1024,256]{1,0:T(8,128)(2,1)S(1)}, bf16[1024,256]{1,0:T(8,128)(2,1)S(1)}, u32[]{:S(2)}, u32[]{:S(2)}) collective-permute-start(bf16[1024,256]{1,0:T(8,128)(2,1)S(1)} %get-tuple-element.28.refs_2_), channel_id=1, source_target_pairs={{0,7},{1,0},{2,1},{3,2},{4,3},{5,4},{6,5},{7,6},{8,15},{9,8},{10,9... | collective-permute-start | bytes 1572872 | tf_op jit(solution)/shard_map/ppermute | solution.py:235
  52.7 11.7 %copy-start.5 = (s32[13]{0:T(128)S(1)}, s32[13]{0:T(128)}, u32[]{:S(2)}) copy-start(s32[13]{0:T(128)} %param.23) | copy-start | bytes 160
  52.7 15.9 %collective-permute-start.9 = (bf16[1024,256]{1,0:T(8,128)(2,1)}, bf16[1024,256]{1,0:T(8,128)(2,1)S(1)}, u32[]{:S(2)}, u32[]{:S(2)}) collective-permute-start(bf16[1024,256]{1,0:T(8,128)(2,1)} %get-tuple-element.31), channel_id=1, source_target_pairs={{0,1},{1,2},{2,3},{3,4},{4,5},{5,6},{6,7},{7,0},{8,9},{9,10},{10,1... | collective-permute-start | bytes 1572872 | tf_op jit(solution)/shard_map/ppermute | solution.py:235
  60.2 17.8 %collective-permute-start.6 = (bf16[1024,256]{1,0:T(8,128)(2,1)S(1)}, bf16[1024,256]{1,0:T(8,128)(2,1)S(1)}, u32[]{:S(2)}, u32[]{:S(2)}) collective-permute-start(bf16[1024,256]{1,0:T(8,128)(2,1)S(1)} %get-tuple-element.29.refs_2_), channel_id=1, source_target_pairs={{0,1},{1,2},{2,3},{3,4},{4,5},{5,6},{6,7},{7,0},{8,9},{9,10},{10,1... | collective-permute-start | bytes 1572872 | tf_op jit(solution)/shard_map/ppermute | solution.py:235
  62.0 16.0 %collective-permute-start.7 = (bf16[1024,256]{1,0:T(8,128)(2,1)}, bf16[1024,256]{1,0:T(8,128)(2,1)S(1)}, u32[]{:S(2)}, u32[]{:S(2)}) collective-permute-start(bf16[1024,256]{1,0:T(8,128)(2,1)} %get-tuple-element.30), channel_id=1, source_target_pairs={{0,7},{1,0},{2,1},{3,2},{4,3},{5,4},{6,5},{7,6},{8,15},{9,8},{10,9... | collective-permute-start | bytes 1572872 | tf_op jit(solution)/shard_map/ppermute | solution.py:235
  73.5 14.8 %collective-permute-start.11 = (bf16[1024,256]{1,0:T(8,128)(2,1)S(1)}, bf16[1024,256]{1,0:T(8,128)(2,1)S(1)}, u32[]{:S(2)}, u32[]{:S(2)}) collective-permute-start(bf16[1024,256]{1,0:T(8,128)(2,1)S(1)} %get-tuple-element.32.refs_2_), channel_id=1, source_target_pairs={{0,7},{1,0},{2,1},{3,2},{4,3},{5,4},{6,5},{7,6},{8,15},{9,8},{10,9... | collective-permute-start | bytes 1572872 | tf_op jit(solution)/shard_map/ppermute | solution.py:235
  74.5 16.1 %collective-permute-start.12 = (bf16[1024,256]{1,0:T(8,128)(2,1)S(1)}, bf16[1024,256]{1,0:T(8,128)(2,1)S(1)}, u32[]{:S(2)}, u32[]{:S(2)}) collective-permute-start(bf16[1024,256]{1,0:T(8,128)(2,1)S(1)} %get-tuple-element.34), channel_id=1, source_target_pairs={{0,1},{1,2},{2,3},{3,4},{4,5},{5,6},{6,7},{7,0},{8,9},{9,10},{10,1... | collective-permute-start | bytes 1572872 | tf_op jit(solution)/shard_map/ppermute | solution.py:235
  83.7 15.8 %collective-permute-start.10 = (bf16[1024,256]{1,0:T(8,128)(2,1)}, bf16[1024,256]{1,0:T(8,128)(2,1)S(1)}, u32[]{:S(2)}, u32[]{:S(2)}) collective-permute-start(bf16[1024,256]{1,0:T(8,128)(2,1)} %get-tuple-element.33), channel_id=1, source_target_pairs={{0,1},{1,2},{2,3},{3,4},{4,5},{5,6},{6,7},{7,0},{8,9},{9,10},{10,1... | collective-permute-start | bytes 1572872 | tf_op jit(solution)/shard_map/ppermute | solution.py:235
  85.7 13.8 %collective-permute-start.13 = (bf16[1024,256]{1,0:T(8,128)(2,1)}, bf16[1024,256]{1,0:T(8,128)(2,1)S(1)}, u32[]{:S(2)}, u32[]{:S(2)}) collective-permute-start(bf16[1024,256]{1,0:T(8,128)(2,1)} %get-tuple-element.35), channel_id=1, source_target_pairs={{0,7},{1,0},{2,1},{3,2},{4,3},{5,4},{6,5},{7,6},{8,15},{9,8},{10,9... | collective-permute-start | bytes 1572872 | tf_op jit(solution)/shard_map/ppermute | solution.py:235
  99.5 40.9 %copy-start.1 = (bf16[1024,256]{1,0:T(8,128)(2,1)}, bf16[1024,256]{1,0:T(8,128)(2,1)S(1)}, u32[]{:S(2)}) copy-start(bf16[1024,256]{1,0:T(8,128)(2,1)S(1)} %collective-permute-done.13.refs_2_) | copy-start | bytes 1572868
  99.5 39.9 %all-to-all-start = ((bf16[8,256,128]{2,1,0:T(8,128)(2,1)}), bf16[8,256,128]{2,1,0:T(8,128)(2,1)S(1)}, u32[]{:S(2)}, u32[]{:S(2)}) async-start(bf16[8,256,128]{2,1,0:T(8,128)(2,1)} %bitcast.2), calls=%async_computation | async-start | bytes 1048576 | tf_op jit(solution)/shard_map/all_to_all | solution.py:285
  139.4 13.3 %collective-permute-start.14 = (bf16[32,64,256]{2,1,0:T(8,128)(2,1)}, bf16[32,64,256]{2,1,0:T(8,128)(2,1)}, u32[]{:S(2)}, u32[]{:S(2)}) collective-permute-start(bf16[32,64,256]{2,1,0:T(8,128)(2,1)} %all-gather.5.cloned.1.call-done.own_ref), channel_id=1, source_target_pairs={{0,8},{8,0},{16,24},{24,16},{32,40},{40,32},{48,56},{56,48},{64,72... | collective-permute-start | bytes 3145736 | tf_op jit(solution)/shard_map/ppermute | solution.py:277
  140.3 25.2 %all-to-all-start.1 = ((bf16[8,256,128]{2,1,0:T(8,128)(2,1)}), bf16[8,256,128]{2,1,0:T(8,128)(2,1)S(1)}, u32[]{:S(2)}, u32[]{:S(2)}) async-start(bf16[8,256,128]{2,1,0:T(8,128)(2,1)} %broadcast_in_dim.39), calls=%async_computation.1 | async-start | bytes 1048576 | tf_op jit(solution)/shard_map/all_to_all | solution.py:291
  147.4 18.2 %copy-start = (bf16[32,64,256]{2,1,0:T(8,128)(2,1)S(1)}, bf16[32,64,256]{2,1,0:T(8,128)(2,1)}, u32[]{:S(2)}) copy-start(bf16[32,64,256]{2,1,0:T(8,128)(2,1)} %all-gather.5.cloned.1.call-done.own_ref) | copy-start | bytes 3145732
  (7 other events, 66.3 us)
Sparse Core Ops, SparseCore 0:
  9.9 79.7 all-gather.2
  92.2 47.1 all-gather.4
